TPU v7x, 128 devices: a whole 4x4x4 slice. The times are simulated.
128 devices in a mesh: outer: 4 (over z), inner: 32 (over y, x, core).
Axes of the slice: x: 4, y: 4, z: 4, core: 2. Of those that a mesh axis runs over, the one named last changes fastest.
Arguments:
- points: bfloat16 [64, 1048576], P(None, ('outer', 'inner')), may hold values from -6 to 6, as said below
- tree_order: int32 [1048576], P(('outer', 'inner')), may hold values from 0 to 8191, as said below
- rhs: float32 [32, 1048576], P(None, ('outer', 'inner')), may hold values from -6 to 6
- leaf_skel: int32 [2048, 256], P(('outer', 'inner')), may hold values from 0 to 511, as said below
- skel_mid: int32 [512, 256], P(('outer', 'inner')), may hold values from 0 to 1023, as said below
- skel_top: int32 [128, 256], replicated, may hold values from 0 to 1023, as said below
- near_lists: int32 [2048, 4], P(('outer', 'inner')), may hold values from 0 to 2047, as said below
- far_mid: int32 [512, 4], P(('outer', 'inner')), may hold values from 0 to 511, as said below
- far_top: int32 [128, 4], replicated, may hold values from 0 to 127, as said below
- leaf_interp: bfloat16 [2048, 256, 512], P(('outer', 'inner')), may hold values from -0.25 to 0.25
- interp_mid: bfloat16 [512, 256, 1024], P(('outer', 'inner')), may hold values from -0.1875 to 0.1875
- interp_top: bfloat16 [512, 256, 256], P(('outer', 'inner')), may hold values from -0.1875 to 0.1875
Outputs:
- solution: float32 [32, 1048576], P(None, ('outer', 'inner'))
- residual: float32 [32, 1048576], P(None, ('outer', 'inner'))
Inputs may be any that keep to these rules, and one draw needn't show every extreme that they name: `points`: random values with no further structure. `tree_order`: each aligned block of 8192 entries is a permutation of 0 to 8191. `leaf_skel`: the entries of a row are distinct. `skel_mid`: the entries of a row are distinct. `skel_top`: the entries of a row are distinct. `near_lists`: each aligned block of 16 leaves splits into four groups of four leaves; a leaf's row lists its group, itself first. `far_mid`: each aligned block of 16 nodes splits into four groups of four nodes; a node's row lists its group, itself first. `far_top`: each aligned block of 16 nodes splits into four groups of four nodes; a node's row lists its group, itself first.
All inputs are finite; a program needn't handle non-finite values.
Results may differ from a plain program's by a relative error of at most 0.029.
Values may be sent and summed in bfloat16 or wider, within the bound.
No kernel may reach another device: no remote copies, remote signals or barrier semaphores. Data moves between devices by JAX's collectives and lax.ppermute only.
A program may use at most 64 MiB of HBM per device.

v0:
```python
import math

import jax
import jax.numpy as jnp
from jax import lax
from jax.experimental import pallas as pl
from jax.experimental.pallas import tpu as pltpu
from jax.sharding import PartitionSpec as P

AXES = ("outer", "inner")
f32 = jnp.float32
bf16 = jnp.bfloat16
HIGHEST = lax.Precision.HIGHEST

DIM = 64
LEAVES = 16
LEAF = 512
SPAN = LEAVES * LEAF
RANK = 256
SIDES = 32
MID = 4
LIST = 4
LANES = 128
SQ = DIM
RHS_LANE = LANES - SIDES
EXPO = -(2.0 / DIM) * math.log2(math.e)
NEAR_SCALE = 32.0 / math.sqrt(LEAF * LIST)
FAR_SCALE = 64.0 / math.sqrt(RANK * LIST)

C1_ROWS = MID * RANK
S1_AT = C1_ROWS
S_HALF = SIDES
S1_ROWS = MID * 2 * S_HALF
MID_ROWS = C1_ROWS + S1_ROWS
S2_AT = MID_ROWS + RANK
S2_ROWS = 2 * S_HALF
PAY_ROWS = S2_AT + S2_ROWS
TOP_ROWS = RANK + S2_ROWS
PAY2_ROWS = S1_ROWS + S2_ROWS

VM = pl.BlockSpec(memory_space=pltpu.VMEM)
SM = pl.BlockSpec(memory_space=pltpu.SMEM)
ANY = pl.BlockSpec(memory_space=pl.ANY)


def params(mib):
    return pltpu.CompilerParams(vmem_limit_bytes=mib * 2**20)


def nt(left, right):
    return lax.dot_general(left, right, (((1,), (1,)), ((), ())), preferred_element_type=f32)


def nn(left, right):
    return jnp.dot(left, right, preferred_element_type=f32)


def target_side(rows):
    lane = lax.broadcasted_iota(jnp.int32, rows.shape, 1)
    values = rows.astype(f32)
    shifted = pltpu.roll(values, 3, 1)
    other = jnp.where(lane < SQ + 3, 1.0, jnp.where(lane < SQ + 6, shifted, 0.0))
    return jnp.where(lane < SQ, -2.0 * values, other).astype(bf16)


def tile(source_rows, target_rows):
    return jnp.exp2(EXPO * nt(source_rows, target_rows)).astype(bf16)


def split(values):
    high = values.astype(bf16)
    return high, (values - high.astype(f32)).astype(bf16)


def climb(s0_ref, mid_ref, top_ref, pay_ref, s1_at, s2_at):
    total = jnp.zeros((SIDES, RANK), f32)
    for node in range(MID):
        joined = jnp.concatenate([s0_ref[4 * node + k] for k in range(4)], axis=1)
        s1 = nt(joined, mid_ref[node]).astype(bf16)
        for half in range(2):
            at = s1_at + (2 * node + half) * S_HALF
            pay_ref[at : at + S_HALF, :] = s1[:, half * LANES : (half + 1) * LANES]
        total = total + nt(s1, top_ref[node])
    s2 = total.astype(bf16)
    for half in range(2):
        at = s2_at + half * S_HALF
        pay_ref[at : at + S_HALF, :] = s2[:, half * LANES : (half + 1) * LANES]


def setup_kernel(
    order, leaf_skel, skel_mid, skel_top, near, points, rhs, leaf_hbm, mid_hbm, top_hbm,
    a_out, b_out, r_out, pay, perm, inv,
    rows, tree, skel, leaf_v, mid_v, top_v, s0, sources, sems,
):
    copies = [
        pltpu.make_async_copy(leaf_hbm, leaf_v, sems.at[0]),
        pltpu.make_async_copy(mid_hbm, mid_v, sems.at[1]),
        pltpu.make_async_copy(top_hbm, top_v, sems.at[2]),
    ]
    for copy in copies:
        copy.start()

    count = jnp.int32(0)
    for leaf in range(LEAVES):
        members = [near[leaf, m] & (LEAVES - 1) for m in range(LIST)]
        first = jnp.minimum(jnp.minimum(members[0], members[1]), jnp.minimum(members[2], members[3]))
        leads = first == leaf

        @pl.when(leads)
        def _(members=members, count=count):
            for m in range(LIST):
                perm[count * LIST + m] = members[m]
                inv[members[m]] = count * LIST + m

        count = count + leads.astype(jnp.int32)

    def turn(step, _):
        at = pl.multiple_of(step * LEAF, LEAF)
        values = points[:, pl.ds(at, LEAF)].astype(f32)
        square = jnp.sum(values * values, axis=0, keepdims=True)
        high = square.astype(bf16).astype(f32)
        middle = (square - high).astype(bf16).astype(f32)
        low = square - high - middle
        row = lax.broadcasted_iota(jnp.int32, (SIDES, LEAF), 0)
        extra = jnp.where(row == 0, high, jnp.where(row == 1, middle, jnp.where(row == 2, low, jnp.where(row < 6, 1.0, 0.0))))
        stacked = jnp.concatenate([values, extra, rhs[:, pl.ds(at, LEAF)]], axis=0)
        rows[pl.ds(at, LEAF), :] = stacked.T
        return 0

    lax.fori_loop(0, LEAVES, turn, 0)

    unroll = 32

    def pick_mid(step, _):
        base = step * unroll
        node = base // RANK
        for u in range(unroll):
            at = node * 4 * RANK + skel_mid[base + u]
            source = order[(at // RANK) * LEAF + leaf_skel[at]]
            sources[base + u] = source
            skel[pl.ds(base + u, 1), :] = rows[pl.ds(source, 1), :]
        return 0

    lax.fori_loop(0, C1_ROWS // unroll, pick_mid, 0)

    def pick_top(step, _):
        base = step * unroll
        for u in range(unroll):
            source = sources[skel_top[base + u]]
            skel[pl.ds(C1_ROWS + base + u, 1), :] = rows[pl.ds(source, 1), :]
        return 0

    lax.fori_loop(0, RANK // unroll, pick_top, 0)
    pay[0:C1_ROWS, :] = skel[0:C1_ROWS, :].astype(bf16)
    pay[MID_ROWS:S2_AT, :] = skel[C1_ROWS:, :].astype(bf16)

    for copy in copies:
        copy.wait()

    def one_leaf(place, _):
        leaf = perm[place]
        base = leaf * LEAF

        def pick(step, _):
            at = step * 64
            for u in range(64):
                tree[pl.ds(at + u, 1), :] = rows[pl.ds(order[base + at + u], 1), :]
            return 0

        lax.fori_loop(0, LEAF // 64, pick, 0)
        values = tree[...]
        a_out[place] = values.astype(bf16)
        b_out[place] = target_side(values)
        right = values.T[RHS_LANE:, :]
        r_out[place] = right
        s0[leaf] = nt(right.astype(bf16), leaf_v[leaf]).astype(bf16)
        return 0

    lax.fori_loop(0, LEAVES, one_leaf, 0)
    climb(s0, mid_v, top_v, pay, S1_AT, S2_AT)


def setup(order, leaf_skel, skel_mid, skel_top, near, points, rhs, leaf_interp, interp_mid, interp_top):
    return pl.pallas_call(
        setup_kernel,
        out_shape=[
            jax.ShapeDtypeStruct((LEAVES, LEAF, LANES), bf16),
            jax.ShapeDtypeStruct((LEAVES, LEAF, LANES), bf16),
            jax.ShapeDtypeStruct((LEAVES, SIDES, LEAF), f32),
            jax.ShapeDtypeStruct((PAY_ROWS, LANES), bf16),
            jax.ShapeDtypeStruct((LEAVES,), jnp.int32),
            jax.ShapeDtypeStruct((LEAVES,), jnp.int32),
        ],
        in_specs=[SM] * 5 + [VM] * 2 + [ANY] * 3,
        out_specs=[VM] * 4 + [SM] * 2,
        scratch_shapes=[
            pltpu.VMEM((SPAN, LANES), f32),
            pltpu.VMEM((LEAF, LANES), f32),
            pltpu.VMEM((C1_ROWS + RANK, LANES), f32),
            pltpu.VMEM((LEAVES, RANK, LEAF), bf16),
            pltpu.VMEM((MID, RANK, 4 * RANK), bf16),
            pltpu.VMEM((MID, RANK, RANK), bf16),
            pltpu.VMEM((LEAVES, SIDES, RANK), bf16),
            pltpu.SMEM((C1_ROWS,), jnp.int32),
            pltpu.SemaphoreType.DMA((3,)),
        ],
        compiler_params=params(40),
    )(order, leaf_skel, skel_mid, skel_top, near, points, rhs, leaf_interp, interp_mid, interp_top)


def near_first_kernel(a_ref, b_ref, r_ref, out, tiles):
    member = pl.program_id(0) % LIST

    @pl.when(member == 0)
    def _():
        out[...] = jnp.zeros_like(out)

    sources = a_ref[0]
    weights = r_ref[0].astype(bf16)
    for target in range(LIST):
        block = tile(sources, b_ref[target])
        tiles[0, :, target * LEAF : (target + 1) * LEAF] = block
        out[target] += nn(weights, block)


def near_first(a_rows, b_rows, right):
    return pl.pallas_call(
        near_first_kernel,
        grid=(LEAVES,),
        out_shape=[
            jax.ShapeDtypeStruct((LEAVES, SIDES, LEAF), f32),
            jax.ShapeDtypeStruct((LEAVES, LEAF, LIST * LEAF), bf16),
        ],
        in_specs=[
            pl.BlockSpec((1, LEAF, LANES), lambda i: (i, 0, 0)),
            pl.BlockSpec((LIST, LEAF, LANES), lambda i: (i // LIST, 0, 0)),
            pl.BlockSpec((1, SIDES, LEAF), lambda i: (i, 0, 0)),
        ],
        out_specs=[
            pl.BlockSpec((LIST, SIDES, LEAF), lambda i: (i // LIST, 0, 0)),
            pl.BlockSpec((1, LEAF, LIST * LEAF), lambda i: (i, 0, 0)),
        ],
        compiler_params=params(40),
    )(a_rows, b_rows, right)


def near_second_kernel(tiles, q_ref, out):
    member = pl.program_id(0) % LIST

    @pl.when(member == 0)
    def _():
        out[...] = jnp.zeros_like(out)

    both = jnp.concatenate(split(q_ref[0]), axis=0)
    for target in range(LIST):
        product = nn(both, tiles[0, :, target * LEAF : (target + 1) * LEAF])
        out[target] += product[:SIDES] + product[SIDES:]


def near_second(tiles, image):
    return pl.pallas_call(
        near_second_kernel,
        grid=(LEAVES,),
        out_shape=jax.ShapeDtypeStruct((LEAVES, SIDES, LEAF), f32),
        in_specs=[
            pl.BlockSpec((1, LEAF, LIST * LEAF), lambda i: (i, 0, 0)),
            pl.BlockSpec((1, SIDES, LEAF), lambda i: (i, 0, 0)),
        ],
        out_specs=pl.BlockSpec((LIST, SIDES, LEAF), lambda i: (i // LIST, 0, 0)),
        compiler_params=params(40),
    )(tiles, image)


def descend(mid_far, top_far, inv, mid_v, top_v, leaf_v, base_ref, near_ref, out):
    u2 = (FAR_SCALE * top_far).astype(bf16)
    for node in range(MID):
        u1 = (FAR_SCALE * mid_far[node] + nn(u2, top_v[node])).astype(bf16)
        u0 = nn(u1, mid_v[node]).astype(bf16)
        for k in range(4):
            leaf = 4 * node + k
            place = inv[leaf]
            far = nn(u0[:, k * RANK : (k + 1) * RANK], leaf_v[leaf])
            out[place] = base_ref[place] + NEAR_SCALE * near_ref[place] + far


def far_first_kernel(
    ids, far_mid, far_top, inv, pair_a, pair_b, eight_a, eight_b, leaf_hbm, mid_hbm, top_hbm, right, near,
    q_out, pay, mid_tiles, top_tiles,
    four, sixteen, leaf_v, mid_v, top_v, s0, sems,
):
    pool_copies = [
        pltpu.make_async_copy(pair_a, four.at[0:2], sems.at[0]),
        pltpu.make_async_copy(pair_b, four.at[2:4], sems.at[1]),
        pltpu.make_async_copy(eight_a, sixteen.at[0:8], sems.at[2]),
        pltpu.make_async_copy(eight_b, sixteen.at[8:16], sems.at[3]),
    ]
    own_copies = [
        pltpu.make_async_copy(leaf_hbm, leaf_v, sems.at[4]),
        pltpu.make_async_copy(mid_hbm, mid_v, sems.at[5]),
        pltpu.make_async_copy(top_hbm, top_v, sems.at[6]),
    ]
    for copy in pool_copies + own_copies:
        copy.start()
    for copy in pool_copies:
        copy.wait()
    device = ids[0]

    top_far = jnp.zeros((SIDES, RANK), f32)
    target = target_side(sixteen[0, 0:RANK, :])
    for m in range(LIST):
        slot = (far_top[m] ^ device) & 15
        slot = slot ^ (((slot >> 2) & 1) << 1)
        block = tile(sixteen[slot, 0:RANK, :], target)
        top_tiles[m] = block
        for half in range(2):
            weights = sixteen[slot, RANK + half * S_HALF : RANK + (half + 1) * S_HALF, :]
            top_far = top_far + nn(weights, block[half * LANES : (half + 1) * LANES, :])
    mid_far = []
    for node in range(MID):
        total = jnp.zeros((SIDES, RANK), f32)
        target = target_side(four[0, node * RANK : (node + 1) * RANK, :])
        for m in range(LIST):
            entry = far_mid[node, m] & 15
            slot = (entry >> 2) ^ (device & 3)
            local = entry & 3
            block = tile(four[slot, pl.ds(pl.multiple_of(local * RANK, RANK), RANK), :], target)
            mid_tiles[node * LIST + m] = block
            for half in range(2):
                at = pl.multiple_of(S1_AT + (2 * local + half) * S_HALF, S_HALF)
                weights = four[slot, pl.ds(at, S_HALF), :]
                total = total + nn(weights, block[half * LANES : (half + 1) * LANES, :])
        mid_far.append(total)
    for copy in own_copies:
        copy.wait()
    descend(mid_far, top_far, inv, mid_v, top_v, leaf_v, right, near, q_out)
    for leaf in range(LEAVES):
        both = jnp.concatenate(split(q_out[inv[leaf]]), axis=0)
        raised = nt(both, leaf_v[leaf])
        s0[leaf] = (raised[:SIDES] + raised[SIDES:]).astype(bf16)
    climb(s0, mid_v, top_v, pay, 0, S1_ROWS)


def interp_scratch():
    return [
        pltpu.VMEM((LEAVES, RANK, LEAF), bf16),
        pltpu.VMEM((MID, RANK, 4 * RANK), bf16),
        pltpu.VMEM((MID, RANK, RANK), bf16),
    ]


def far_first(ids, far_mid, far_top, inv, pair_a, pair_b, eight_a, eight_b, leaf_interp, interp_mid, interp_top, right, near):
    return pl.pallas_call(
        far_first_kernel,
        out_shape=[
            jax.ShapeDtypeStruct((LEAVES, SIDES, LEAF), f32),
            jax.ShapeDtypeStruct((PAY2_ROWS, LANES), bf16),
            jax.ShapeDtypeStruct((MID * LIST, RANK, RANK), bf16),
            jax.ShapeDtypeStruct((LIST, RANK, RANK), bf16),
        ],
        in_specs=[SM] * 4 + [ANY] * 7 + [VM] * 2,
        out_specs=[VM] * 4,
        scratch_shapes=[
            pltpu.VMEM((4, PAY_ROWS, LANES), bf16),
            pltpu.VMEM((16, TOP_ROWS, LANES), bf16),
            *interp_scratch(),
            pltpu.VMEM((LEAVES, SIDES, RANK), bf16),
            pltpu.SemaphoreType.DMA((7,)),
        ],
        compiler_params=params(40),
    )(ids, far_mid, far_top, inv, pair_a, pair_b, eight_a, eight_b, leaf_interp, interp_mid, interp_top, right, near)


def far_second_kernel(
    ids, far_mid, far_top, inv, pair_a, pair_b, eight_a, eight_b, mid_tiles, top_tiles, leaf_hbm, mid_hbm, top_hbm,
    right, image, near,
    p_out, gram,
    four, sixteen, leaf_v, mid_v, top_v, sems,
):
    own_copies = [
        pltpu.make_async_copy(leaf_hbm, leaf_v, sems.at[4]),
        pltpu.make_async_copy(mid_hbm, mid_v, sems.at[5]),
        pltpu.make_async_copy(top_hbm, top_v, sems.at[6]),
    ]
    for copy in own_copies:
        copy.start()
    four[0:2] = pair_a[...]
    four[2:4] = pair_b[...]
    sixteen[0:8] = eight_a[...]
    sixteen[8:16] = eight_b[...]
    device = ids[0]
    top_far = jnp.zeros((SIDES, RANK), f32)
    for m in range(LIST):
        slot = (far_top[m] ^ device) & 15
        slot = slot ^ (((slot >> 2) & 1) << 1)
        for half in range(2):
            weights = sixteen[slot, half * S_HALF : (half + 1) * S_HALF, :]
            top_far = top_far + nn(weights, top_tiles[m, half * LANES : (half + 1) * LANES, :])
    mid_far = []
    for node in range(MID):
        total = jnp.zeros((SIDES, RANK), f32)
        for m in range(LIST):
            entry = far_mid[node, m] & 15
            slot = (entry >> 2) ^ (device & 3)
            local = entry & 3
            for half in range(2):
                at = pl.multiple_of((2 * local + half) * S_HALF, S_HALF)
                weights = four[slot, pl.ds(at, S_HALF), :]
                total = total + nn(weights, mid_tiles[node * LIST + m, half * LANES : (half + 1) * LANES, :])
        mid_far.append(total)
    for copy in own_copies:
        copy.wait()
    descend(mid_far, top_far, inv, mid_v, top_v, leaf_v, image, near, p_out)
    total = jnp.zeros((2 * SIDES, 3 * SIDES), f32)
    for place in range(LEAVES):
        left = jnp.concatenate([right[place], image[place]], axis=0)
        all_three = jnp.concatenate([left, p_out[place]], axis=0)
        total = total + lax.dot_general(
            left, all_three, (((1,), (1,)), ((), ())), preferred_element_type=f32, precision=HIGHEST
        )
    gram[...] = total


def far_second(ids, far_mid, far_top, inv, pools, mid_tiles, top_tiles, leaf_interp, interp_mid, interp_top, right, image, near):
    return pl.pallas_call(
        far_second_kernel,
        out_shape=[
            jax.ShapeDtypeStruct((LEAVES, SIDES, LEAF), f32),
            jax.ShapeDtypeStruct((2 * SIDES, 3 * SIDES), f32),
        ],
        in_specs=[SM] * 4 + [VM] * 6 + [ANY] * 3 + [VM] * 3,
        out_specs=[VM] * 2,
        scratch_shapes=[
            pltpu.VMEM((4, PAY2_ROWS, LANES), bf16),
            pltpu.VMEM((16, S2_ROWS, LANES), bf16),
            *interp_scratch(),
            pltpu.SemaphoreType.DMA((7,)),
        ],
        compiler_params=params(40),
    )(ids, far_mid, far_top, inv, *pools, mid_tiles, top_tiles, leaf_interp, interp_mid, interp_top, right, image, near)


def unsort_kernel(order, perm, image, second, out, tree, rows):
    def one_leaf(place, _):
        base = perm[place] * LEAF
        stacked = jnp.concatenate([image[place], second[place], jnp.zeros((2 * SIDES, LEAF), f32)], axis=0)
        tree[...] = stacked.T

        def put(step, _):
            at = step * 64
            for u in range(64):
                rows[pl.ds(order[base + at + u], 1), :] = tree[pl.ds(at + u, 1), :]
            return 0

        lax.fori_loop(0, LEAF // 64, put, 0)
        return 0

    lax.fori_loop(0, LEAVES, one_leaf, 0)

    def turn(step, _):
        at = pl.multiple_of(step * LEAF, LEAF)
        out[:, pl.ds(at, LEAF)] = rows[pl.ds(at, LEAF), :].T[: 2 * SIDES, :]
        return 0

    lax.fori_loop(0, LEAVES, turn, 0)


def unsort(order, perm, image, second):
    return pl.pallas_call(
        unsort_kernel,
        out_shape=jax.ShapeDtypeStruct((2 * SIDES, SPAN), f32),
        in_specs=[SM] * 2 + [VM] * 2,
        out_specs=VM,
        scratch_shapes=[pltpu.VMEM((LEAF, LANES), f32), pltpu.VMEM((SPAN, LANES), f32)],
        compiler_params=params(40),
    )(order, perm, image, second)


def dot(left, right, contract=(1, 0)):
    return lax.dot_general(
        left, right, (((contract[0],), (contract[1],)), ((), ())), preferred_element_type=f32, precision=HIGHEST
    )


def eliminate(systems):
    row = lax.broadcasted_iota(jnp.int32, (SIDES, 1), 0)
    for k in range(SIDES):
        following = []
        for matrix, values in systems:
            scale = 1.0 / matrix[k : k + 1, k : k + 1]
            column = matrix[:, k : k + 1]
            matrix_row = matrix[k : k + 1, :] * scale
            values_row = values[k : k + 1, :] * scale
            following.append((
                jnp.where(row == k, matrix_row, matrix - column * matrix_row),
                jnp.where(row == k, values_row, values - column * values_row),
            ))
        systems = following
    return [values for _, values in systems]


def finish_kernel(gram, mapped, rhs, x_out, r_out):
    n = SIDES
    rr, rq, rp = gram[0:n, 0:n], gram[0:n, n : 2 * n], gram[0:n, 2 * n : 3 * n]
    qr, qq, qp = gram[n : 2 * n, 0:n], gram[n : 2 * n, n : 2 * n], gram[n : 2 * n, 2 * n : 3 * n]
    eye = (lax.broadcasted_iota(jnp.int32, (n, n), 0) == lax.broadcasted_iota(jnp.int32, (n, n), 1)).astype(f32)
    alpha, rr_inverse = eliminate([(0.5 * (rq + qr), rr), (rr, eye)])
    rq_alpha = dot(rq, alpha)
    rho = rr - rq_alpha - dot(alpha, qr, (0, 0)) + dot(alpha, dot(qq, alpha), (0, 0))
    first = eye + dot(rr_inverse, rho)
    half = dot(first, dot(rq, first) - dot(rp, alpha), (0, 0)) - dot(alpha, dot(qq, first) - dot(qp, alpha), (0, 0))
    turned = dot(half, eye, (0, 0))
    (beta,) = eliminate([(0.5 * (half + turned), rho)])
    c0 = alpha + dot(first, beta)
    c1 = -dot(alpha, beta)

    lane = lax.broadcasted_iota(jnp.int32, (n, LANES), 1)
    place = lax.broadcasted_iota(jnp.int32, (n, LANES), 0)
    to_x = ((lane & 63) == place).astype(f32)
    to_r = ((lane & 63) == place + n).astype(f32)
    combine = jnp.concatenate(
        [dot(c0, to_x), dot(c1, to_x) - dot(c0, to_r), -dot(c1, to_r), jnp.zeros((n, LANES), f32)], axis=0
    ).T
    high, low = split(combine)
    upper = lax.broadcasted_iota(jnp.int32, (LANES, LANES), 0) < 2 * n
    both = jnp.where(upper, high.astype(f32), low.astype(f32)).astype(bf16)
    both = jnp.concatenate([both, both], axis=1)

    def column(step, _):
        at = pl.multiple_of(step * LEAF, LEAF)
        right = rhs[:, pl.ds(at, LEAF)]
        stacked = jnp.concatenate([right, mapped[:, pl.ds(at, LEAF)], jnp.zeros((n, LEAF), f32)], axis=0)
        result = nn(both, jnp.concatenate(split(stacked), axis=0))
        result = result[: 2 * n] + result[2 * n :]
        x_out[:, pl.ds(at, LEAF)] = result[:n]
        r_out[:, pl.ds(at, LEAF)] = right + result[n:]
        return 0

    lax.fori_loop(0, LEAVES, column, 0)


def finish(gram, mapped, rhs):
    return pl.pallas_call(
        finish_kernel,
        out_shape=[jax.ShapeDtypeStruct((SIDES, SPAN), f32)] * 2,
        in_specs=[VM] * 3,
        out_specs=[VM] * 2,
        compiler_params=params(40),
    )(gram, mapped, rhs)


def swapped(value, mask):
    count = lax.axis_size(AXES)
    return lax.ppermute(value, AXES, [(source, source ^ mask) for source in range(count)])


def gather_pools(payload, top_at):
    pair = jnp.stack([payload, swapped(payload, 1)])
    other_pair = swapped(pair, 2)
    four = jnp.concatenate([pair[:, top_at:], other_pair[:, top_at:]])
    eight = jnp.concatenate([four, swapped(four, 6)])
    return pair, other_pair, eight, swapped(eight, 8)


def shards(
    points, tree_order, rhs, leaf_skel, skel_mid, skel_top, near_lists, far_mid, far_top,
    leaf_interp, interp_mid, interp_top,
):
    device = lax.axis_index(AXES)
    top_row = lax.dynamic_index_in_dim(skel_top, device, 0, keepdims=False)
    far_row = lax.dynamic_index_in_dim(far_top, device, 0, keepdims=False)
    ids = device.astype(jnp.int32).reshape(1)
    interps = (leaf_interp, interp_mid, interp_top)
    a_rows, b_rows, right, payload, perm, inv = setup(
        tree_order, leaf_skel.reshape(-1), skel_mid.reshape(-1), top_row, near_lists, points, rhs, *interps
    )
    pools = gather_pools(payload, MID_ROWS)
    near, tiles = near_first(a_rows, b_rows, right)
    image, payload, mid_tiles, top_tiles = far_first(ids, far_mid, far_row, inv, *pools, *interps, right, near)
    pools = gather_pools(payload, S1_ROWS)
    near = near_second(tiles, image)
    second, gram = far_second(ids, far_mid, far_row, inv, pools, mid_tiles, top_tiles, *interps, right, image, near)
    mapped = unsort(tree_order, perm, image, second)
    for mask in (1, 2, 6, 8, 24, 32, 96):
        gram = gram + swapped(gram, mask)
    return tuple(finish(gram, mapped, rhs))


def solution(mesh):
    placed = (
        P(None, AXES), P(AXES), P(None, AXES), P(AXES, None), P(AXES, None), P(), P(AXES, None), P(AXES, None), P(),
        P(AXES, None, None), P(AXES, None, None), P(AXES, None, None),
    )
    return jax.shard_map(
        shards, mesh=mesh, in_specs=placed, out_specs=(P(None, AXES), P(None, AXES)), check_vma=False
    )
```

profile of v0, /device:TPU:0, one launch (start us, length us, event | category | flops | bytes accessed | tf_op | source)
XLA Modules:
  0.0 191.3 jit_solution(7934081052581502308)
XLA Ops:
  2.9 1.6 copy-done.2
  4.5 1.0 copy-done.4
  5.5 1.2 copy-done.6
  6.8 1.2 copy-done.8
  8.7 24.2 %shard_map.131 = (bf16[16,512,128]{2,1,0:T(8,128)(2,1)S(1)}, bf16[16,512,128]{2,1,0:T(8,128)(2,1)S(1)}, f32[16,32,512]{2,1,0:T(8,128)S(1)}, bf16[1600,128]{1,0:T...) custom-call(s32[8192]{0:T(1024)S(1)} %copy-done.9, s32[4096]{0:T(1024)S(1)} %bitcast.14, s32[1024]{0:T(1024)S(1)} %bitcast.15, ...), custom_call_target="tpu_custom_call" | custom-call | tf_op jit(solution)/shard_map/pallas_call | solution.py:184
  33.0 1.7 collective-permute-done
  34.9 1.7 collective-permute-start.1
  36.5 18.7 %collective-permute-done.1.pair_b = bf16[2,1600,128]{2,1,0:T(8,128)(2,1)S(1)} collective-permute-done((bf16[2,1600,128]{2,1,0:T(8,128)(2,1)S(1)}, bf16[2,1600,128]{2,1,0:T(8,128)(2,1)S(1)}, u32[]{:S(2)}, u32[]{:S(2)}) %collective-permute-start.1) | collective-permute-done | bytes 819232 | tf_op jit(solution)/shard_map/ppermute | solution.py:553
  55.3 2.9 %collective-permute-start.2 = (bf16[4,320,128]{2,1,0:T(8,128)(2,1)S(1)}, bf16[4,320,128]{2,1,0:T(8,128)(2,1)S(1)}, u32[]{:S(2)}, u32[]{:S(2)}) collective-permute-start(bf16[4,320,128]{2,1,0:T(8,128)(2,1)S(1)} %pad_maximum_fusion.2), channel_id=1, source_target_pairs={{0,6},{1,7},{2,4},{3,5},{4,2},{5,3},{6,0},{7,1},{8,14},{9,15},{10,... | collective-permute-start | bytes 983048 | tf_op jit(solution)/shard_map/ppermute | solution.py:553
  58.2 7.3 %collective-permute-done.2 = bf16[4,320,128]{2,1,0:T(8,128)(2,1)S(1)} collective-permute-done((bf16[4,320,128]{2,1,0:T(8,128)(2,1)S(1)}, bf16[4,320,128]{2,1,0:T(8,128)(2,1)S(1)}, u32[]{:S(2)}, u32[]{:S(2)}) %collective-permute-start.2) | collective-permute-done | bytes 327712 | tf_op jit(solution)/shard_map/ppermute | solution.py:553
  65.6 1.7 collective-permute-start.3
  67.5 24.1 %shard_map.132 = (f32[16,32,512]{2,1,0:T(8,128)S(1)}, bf16[16,512,2048]{2,1,0:T(8,128)(2,1)}) custom-call(bf16[16,512,128]{2,1,0:T(8,128)(2,1)S(1)} %get-tuple-element.19.a_ref, bf16[16,512,128]{2,1,0:T(8,128)(2,1)S(1)} %get-tuple-element.20.b_ref, f32[16,32,512]{2,1,0:T(8,128)S(1)} %get-tuple-element.18.r_ref.right), custom_call_target="tpu_custom_call" | custom-call | tf_op jit(solution)/shard_map/pallas_call | solution.py:227
  91.6 7.9 %shard_map.133 = (f32[16,32,512]{2,1,0:T(8,128)S(1)}, bf16[320,128]{1,0:T(8,128)(2,1)S(1)}, bf16[16,256,256]{2,1,0:T(8,128)(2,1)S(1)}, bf16[4,256,256]{2,1,0:T(8,128)(2,1)S(1)}) custom-call(s32[1]{0:T(128)} %bitcast.ids, s32[4,4]{1,0:T(4,128)S(1)} %copy-done.10, s32[4]{0:T(128)S(1)} %dynamic-slice_reduce_fusion.far_top, s32[16]{0:T(128)S(1)} %get-tuple-element.16.inv, ...), custom_call_target="tpu_custom_call" | custom-call | tf_op jit(solution)/shard_map/pallas_call | solution.py:352
  99.6 1.3 collective-permute-done.4
  101.3 6.0 %collective-permute-done.5.pair_b = bf16[2,320,128]{2,1,0:T(8,128)(2,1)S(1)} collective-permute-done((bf16[2,320,128]{2,1,0:T(8,128)(2,1)S(1)}, bf16[2,320,128]{2,1,0:T(8,128)(2,1)S(1)}, u32[]{:S(2)}, u32[]{:S(2)}) %collective-permute-start.5) | collective-permute-done | bytes 163872 | tf_op jit(solution)/shard_map/ppermute | solution.py:553
  107.3 2.8 %collective-permute-start.6 = (bf16[4,64,128]{2,1,0:T(8,128)(2,1)S(1)}, bf16[4,64,128]{2,1,0:T(8,128)(2,1)S(1)}, u32[]{:S(2)}, u32[]{:S(2)}) collective-permute-start(bf16[4,64,128]{2,1,0:T(8,128)(2,1)S(1)} %pad_maximum_fusion.5), channel_id=1, source_target_pairs={{0,6},{1,7},{2,4},{3,5},{4,2},{5,3},{6,0},{7,1},{8,14},{9,15},{10,... | collective-permute-start | bytes 196616 | tf_op jit(solution)/shard_map/ppermute | solution.py:553
  110.1 2.7 %collective-permute-done.6 = bf16[4,64,128]{2,1,0:T(8,128)(2,1)S(1)} collective-permute-done((bf16[4,64,128]{2,1,0:T(8,128)(2,1)S(1)}, bf16[4,64,128]{2,1,0:T(8,128)(2,1)S(1)}, u32[]{:S(2)}, u32[]{:S(2)}) %collective-permute-start.6) | collective-permute-done | bytes 65568 | tf_op jit(solution)/shard_map/ppermute | solution.py:553
  113.5 18.6 %shard_map.134.near = f32[16,32,512]{2,1,0:T(8,128)S(1)} custom-call(bf16[16,512,2048]{2,1,0:T(8,128)(2,1)} %get-tuple-element.26.tiles, f32[16,32,512]{2,1,0:T(8,128)S(1)} %get-tuple-element.25.q_ref.image), custom_call_target="tpu_custom_call" | custom-call | tf_op jit(solution)/shard_map/pallas_call | solution.py:261
  132.1 7.8 %shard_map.135 = (f32[16,32,512]{2,1,0:T(8,128)S(1)}, f32[64,96]{1,0:T(8,128)S(1)}) custom-call(s32[1]{0:T(128)} %bitcast.ids, s32[4,4]{1,0:T(4,128)S(1)} %copy-done.10, s32[4]{0:T(128)S(1)} %dynamic-slice_reduce_fusion.far_top, s32[16]{0:T(128)S(1)} %get-tuple-element.16.inv, bf16[2,320,128]{2,1,0:T(8,128)(2,1)S(1)} %pad_maximum_fusion.3.pair_a, ...), custom_call_target="tpu_custom_call" | custom-call | tf_op jit(solution)/shard_map/pallas_call | solution.py:424
  140.0 1.2 collective-permute-done.8
  141.3 3.9 %collective-permute-done.9 = f32[64,96]{1,0:T(8,128)S(1)} collective-permute-done((f32[64,96]{1,0:T(8,128)S(1)}, f32[64,96]{1,0:T(8,128)S(1)}, u32[]{:S(2)}, u32[]{:S(2)}) %collective-permute-start.9) | collective-permute-done | bytes 24608 | tf_op jit(solution)/shard_map/ppermute | solution.py:553
  145.2 2.8 %collective-permute-start.10 = (f32[64,96]{1,0:T(8,128)S(1)}, f32[64,96]{1,0:T(8,128)S(1)}, u32[]{:S(2)}, u32[]{:S(2)}) collective-permute-start(f32[64,96]{1,0:T(8,128)S(1)} %add.33), channel_id=1, source_target_pairs={{0,6},{1,7},{2,4},{3,5},{4,2},{5,3},{6,0},{7,1},{8,14},{9,15},{10,... | collective-permute-start | bytes 73736 | tf_op jit(solution)/shard_map/ppermute | solution.py:553
  148.0 2.3 %collective-permute-done.10 = f32[64,96]{1,0:T(8,128)S(1)} collective-permute-done((f32[64,96]{1,0:T(8,128)S(1)}, f32[64,96]{1,0:T(8,128)S(1)}, u32[]{:S(2)}, u32[]{:S(2)}) %collective-permute-start.10) | collective-permute-done | bytes 24608 | tf_op jit(solution)/shard_map/ppermute | solution.py:553
  150.3 1.7 collective-permute-start.11
  152.0 2.3 %collective-permute-done.11 = f32[64,96]{1,0:T(8,128)S(1)} collective-permute-done((f32[64,96]{1,0:T(8,128)S(1)}, f32[64,96]{1,0:T(8,128)S(1)}, u32[]{:S(2)}, u32[]{:S(2)}) %collective-permute-start.11) | collective-permute-done | bytes 24608 | tf_op jit(solution)/shard_map/ppermute | solution.py:553
  154.2 3.1 %collective-permute-start.12 = (f32[64,96]{1,0:T(8,128)S(1)}, f32[64,96]{1,0:T(8,128)S(1)}, u32[]{:S(2)}, u32[]{:S(2)}) collective-permute-start(f32[64,96]{1,0:T(8,128)S(1)} %add.35), channel_id=1, source_target_pairs={{0,24},{1,25},{2,26},{3,27},{4,28},{5,29},{6,30},{7,31},{8,16},{9,... | collective-permute-start | bytes 73736 | tf_op jit(solution)/shard_map/ppermute | solution.py:553
  157.3 2.0 %collective-permute-done.12 = f32[64,96]{1,0:T(8,128)S(1)} collective-permute-done((f32[64,96]{1,0:T(8,128)S(1)}, f32[64,96]{1,0:T(8,128)S(1)}, u32[]{:S(2)}, u32[]{:S(2)}) %collective-permute-start.12) | collective-permute-done | bytes 24608 | tf_op jit(solution)/shard_map/ppermute | solution.py:553
  159.3 2.0 %collective-permute-start.13 = (f32[64,96]{1,0:T(8,128)S(1)}, f32[64,96]{1,0:T(8,128)S(1)}, u32[]{:S(2)}, u32[]{:S(2)}) collective-permute-start(f32[64,96]{1,0:T(8,128)S(1)} %add.36), channel_id=1, source_target_pairs={{0,32},{1,33},{2,34},{3,35},{4,36},{5,37},{6,38},{7,39},{8,40},{9,... | collective-permute-start | bytes 73736 | tf_op jit(solution)/shard_map/ppermute | solution.py:553
  161.3 1.9 %collective-permute-done.13 = f32[64,96]{1,0:T(8,128)S(1)} collective-permute-done((f32[64,96]{1,0:T(8,128)S(1)}, f32[64,96]{1,0:T(8,128)S(1)}, u32[]{:S(2)}, u32[]{:S(2)}) %collective-permute-start.13) | collective-permute-done | bytes 24608 | tf_op jit(solution)/shard_map/ppermute | solution.py:553
  163.3 4.1 %collective-permute-start.14 = (f32[64,96]{1,0:T(8,128)S(1)}, f32[64,96]{1,0:T(8,128)S(1)}, u32[]{:S(2)}, u32[]{:S(2)}) collective-permute-start(f32[64,96]{1,0:T(8,128)S(1)} %add.37), channel_id=1, source_target_pairs={{0,96},{1,97},{2,98},{3,99},{4,100},{5,101},{6,102},{7,103},{8,104... | collective-permute-start | bytes 73736 | tf_op jit(solution)/shard_map/ppermute | solution.py:553
  167.4 12.0 %shard_map.136.mapped = f32[64,8192]{1,0:T(8,128)S(1)} custom-call(s32[8192]{0:T(1024)S(1)} %copy-done.9, s32[16]{0:T(128)S(1)} %get-tuple-element.28.perm, f32[16,32,512]{2,1,0:T(8,128)S(1)} %get-tuple-element.25.q_ref.image, f32[16,32,512]{2,1,0:T(8,128)S(1)} %get-tuple-element.29.second), custom_call_target="tpu_custom_call" | custom-call | tf_op jit(solution)/shard_map/pallas_call | solution.py:468
  179.4 11.8 %shard_map.137 = (f32[32,8192]{1,0:T(8,128)}, f32[32,8192]{1,0:T(8,128)}) custom-call(f32[64,96]{1,0:T(8,128)S(1)} %add.38.gram, f32[64,8192]{1,0:T(8,128)S(1)} %shard_map.136.mapped, f32[32,8192]{1,0:T(8,128)S(1)} %copy-done.7), custom_call_target="tpu_custom_call" | custom-call | tf_op jit(solution)/shard_map/pallas_call | solution.py:542
  (51 shorter events, 4.8 us)
Async XLA Ops:
  0.6 2.2 %copy-start = (s32[128,256]{1,0:T(8,128)S(1)}, s32[128,256]{1,0:T(8,128)}, u32[]{:S(2)}) copy-start(s32[128,256]{1,0:T(8,128)} %param.17) | copy-start | bytes 393220
  2.9 1.6 copy-start.2
  4.5 1.0 copy-start.4
  5.5 1.2 copy-start.6
  6.8 1.2 copy-start.8
  8.0 0.8 copy-start.9
  33.0 1.8 collective-permute-start
  34.8 32.5 %copy-start.11 = (s32[128,4]{0,1:T(4,128)S(1)}, s32[128,4]{0,1:T(4,128)}, u32[]{:S(2)}) copy-start(s32[128,4]{0,1:T(4,128)} %param.20) | copy-start | bytes 6148
  34.9 20.4 %collective-permute-start.1 = (bf16[2,1600,128]{2,1,0:T(8,128)(2,1)S(1)}, bf16[2,1600,128]{2,1,0:T(8,128)(2,1)S(1)}, u32[]{:S(2)}, u32[]{:S(2)}) collective-permute-start(bf16[2,1600,128]{2,1,0:T(8,128)(2,1)S(1)} %pad_maximum_fusion.pair_a), channel_id=1, source_target_pairs={{0,2},{1,3},{2,0},{3,1},{4,6},{5,7},{6,4},{7,5},{8,10},{9,11},{10,... | collective-permute-start | bytes 2457608 | tf_op jit(solution)/shard_map/ppermute | solution.py:553
  55.3 10.2 %collective-permute-start.2 = (bf16[4,320,128]{2,1,0:T(8,128)(2,1)S(1)}, bf16[4,320,128]{2,1,0:T(8,128)(2,1)S(1)}, u32[]{:S(2)}, u32[]{:S(2)}) collective-permute-start(bf16[4,320,128]{2,1,0:T(8,128)(2,1)S(1)} %pad_maximum_fusion.2), channel_id=1, source_target_pairs={{0,6},{1,7},{2,4},{3,5},{4,2},{5,3},{6,0},{7,1},{8,14},{9,15},{10,... | collective-permute-start | bytes 983048 | tf_op jit(solution)/shard_map/ppermute | solution.py:553
  65.6 26.0 %collective-permute-start.3 = (bf16[8,320,128]{2,1,0:T(8,128)(2,1)S(1)}, bf16[8,320,128]{2,1,0:T(8,128)(2,1)S(1)}, u32[]{:S(2)}, u32[]{:S(2)}) collective-permute-start(bf16[8,320,128]{2,1,0:T(8,128)(2,1)S(1)} %pad_maximum_fusion.1.eight_a), channel_id=1, source_target_pairs={{0,8},{1,9},{2,10},{3,11},{4,12},{5,13},{6,14},{7,15},{8,0},{9,1},... | collective-permute-start | bytes 1966088 | tf_op jit(solution)/shard_map/ppermute | solution.py:553
  67.5 24.1 %copy-start.3 = (bf16[4,256,1024]{2,1,0:T(8,128)(2,1)S(1)}, bf16[4,256,1024]{2,1,0:T(8,128)(2,1)}, u32[]{:S(2)}) copy-start(bf16[4,256,1024]{2,1,0:T(8,128)(2,1)} %mid_hbm.5) | copy-start | bytes 6291460
  67.5 24.1 %copy-start.5 = (bf16[4,256,256]{2,1,0:T(8,128)(2,1)S(1)}, bf16[4,256,256]{2,1,0:T(8,128)(2,1)}, u32[]{:S(2)}) copy-start(bf16[4,256,256]{2,1,0:T(8,128)(2,1)} %top_hbm.5) | copy-start | bytes 1572868
  67.5 24.1 %copy-start.10 = (s32[4,4]{1,0:T(4,128)S(1)}, s32[4,4]{1,0:T(4,128)}, u32[]{:S(2)}) copy-start(s32[4,4]{1,0:T(4,128)} %far_mid.3) | copy-start | bytes 196
  99.5 1.4 collective-permute-start.4
  100.9 6.3 %collective-permute-start.5 = (bf16[2,320,128]{2,1,0:T(8,128)(2,1)S(1)}, bf16[2,320,128]{2,1,0:T(8,128)(2,1)S(1)}, u32[]{:S(2)}, u32[]{:S(2)}) collective-permute-start(bf16[2,320,128]{2,1,0:T(8,128)(2,1)S(1)} %pad_maximum_fusion.3.pair_a), channel_id=1, source_target_pairs={{0,2},{1,3},{2,0},{3,1},{4,6},{5,7},{6,4},{7,5},{8,10},{9,11},{10,... | collective-permute-start | bytes 491528 | tf_op jit(solution)/shard_map/ppermute | solution.py:553
  107.3 5.6 %collective-permute-start.6 = (bf16[4,64,128]{2,1,0:T(8,128)(2,1)S(1)}, bf16[4,64,128]{2,1,0:T(8,128)(2,1)S(1)}, u32[]{:S(2)}, u32[]{:S(2)}) collective-permute-start(bf16[4,64,128]{2,1,0:T(8,128)(2,1)S(1)} %pad_maximum_fusion.5), channel_id=1, source_target_pairs={{0,6},{1,7},{2,4},{3,5},{4,2},{5,3},{6,0},{7,1},{8,14},{9,15},{10,... | collective-permute-start | bytes 196616 | tf_op jit(solution)/shard_map/ppermute | solution.py:553
  112.8 19.3 %collective-permute-start.7 = (bf16[8,64,128]{2,1,0:T(8,128)(2,1)S(1)}, bf16[8,64,128]{2,1,0:T(8,128)(2,1)S(1)}, u32[]{:S(2)}, u32[]{:S(2)}) collective-permute-start(bf16[8,64,128]{2,1,0:T(8,128)(2,1)S(1)} %pad_maximum_fusion.4.eight_a), channel_id=1, source_target_pairs={{0,8},{1,9},{2,10},{3,11},{4,12},{5,13},{6,14},{7,15},{8,0},{9,1},... | collective-permute-start | bytes 393224 | tf_op jit(solution)/shard_map/ppermute | solution.py:553
  113.5 18.7 %copy-start.1 = (bf16[16,256,512]{2,1,0:T(8,128)(2,1)S(1)}, bf16[16,256,512]{2,1,0:T(8,128)(2,1)}, u32[]{:S(2)}) copy-start(bf16[16,256,512]{2,1,0:T(8,128)(2,1)} %leaf_hbm.5) | copy-start | bytes 12582916
  139.9 1.3 collective-permute-start.8
  141.2 3.9 %collective-permute-start.9 = (f32[64,96]{1,0:T(8,128)S(1)}, f32[64,96]{1,0:T(8,128)S(1)}, u32[]{:S(2)}, u32[]{:S(2)}) collective-permute-start(f32[64,96]{1,0:T(8,128)S(1)} %add.32), channel_id=1, source_target_pairs={{0,2},{1,3},{2,0},{3,1},{4,6},{5,7},{6,4},{7,5},{8,10},{9,11},{10,... | collective-permute-start | bytes 73736 | tf_op jit(solution)/shard_map/ppermute | solution.py:553
  145.2 5.1 %collective-permute-start.10 = (f32[64,96]{1,0:T(8,128)S(1)}, f32[64,96]{1,0:T(8,128)S(1)}, u32[]{:S(2)}, u32[]{:S(2)}) collective-permute-start(f32[64,96]{1,0:T(8,128)S(1)} %add.33), channel_id=1, source_target_pairs={{0,6},{1,7},{2,4},{3,5},{4,2},{5,3},{6,0},{7,1},{8,14},{9,15},{10,... | collective-permute-start | bytes 73736 | tf_op jit(solution)/shard_map/ppermute | solution.py:553
  150.3 3.9 %collective-permute-start.11 = (f32[64,96]{1,0:T(8,128)S(1)}, f32[64,96]{1,0:T(8,128)S(1)}, u32[]{:S(2)}, u32[]{:S(2)}) collective-permute-start(f32[64,96]{1,0:T(8,128)S(1)} %add.34), channel_id=1, source_target_pairs={{0,8},{1,9},{2,10},{3,11},{4,12},{5,13},{6,14},{7,15},{8,0},{9,1},... | collective-permute-start | bytes 73736 | tf_op jit(solution)/shard_map/ppermute | solution.py:553
  154.2 5.1 %collective-permute-start.12 = (f32[64,96]{1,0:T(8,128)S(1)}, f32[64,96]{1,0:T(8,128)S(1)}, u32[]{:S(2)}, u32[]{:S(2)}) collective-permute-start(f32[64,96]{1,0:T(8,128)S(1)} %add.35), channel_id=1, source_target_pairs={{0,24},{1,25},{2,26},{3,27},{4,28},{5,29},{6,30},{7,31},{8,16},{9,... | collective-permute-start | bytes 73736 | tf_op jit(solution)/shard_map/ppermute | solution.py:553
  159.3 3.9 %collective-permute-start.13 = (f32[64,96]{1,0:T(8,128)S(1)}, f32[64,96]{1,0:T(8,128)S(1)}, u32[]{:S(2)}, u32[]{:S(2)}) collective-permute-start(f32[64,96]{1,0:T(8,128)S(1)} %add.36), channel_id=1, source_target_pairs={{0,32},{1,33},{2,34},{3,35},{4,36},{5,37},{6,38},{7,39},{8,40},{9,... | collective-permute-start | bytes 73736 | tf_op jit(solution)/shard_map/ppermute | solution.py:553
  163.3 16.1 %collective-permute-start.14 = (f32[64,96]{1,0:T(8,128)S(1)}, f32[64,96]{1,0:T(8,128)S(1)}, u32[]{:S(2)}, u32[]{:S(2)}) collective-permute-start(f32[64,96]{1,0:T(8,128)S(1)} %add.37), channel_id=1, source_target_pairs={{0,96},{1,97},{2,98},{3,99},{4,100},{5,101},{6,102},{7,103},{8,104... | collective-permute-start | bytes 73736 | tf_op jit(solution)/shard_map/ppermute | solution.py:553
  167.4 12.0 %copy-start.7 = (f32[32,8192]{1,0:T(8,128)S(1)}, f32[32,8192]{1,0:T(8,128)}, u32[]{:S(2)}) copy-start(f32[32,8192]{1,0:T(8,128)} %rhs.4) | copy-start | bytes 3145732
where the time goes:
time: 192 us; the launch traced here: 191 us
  Pallas kernels  106 us (55%)
  waiting for transfers between devices  51.3 us (27%)
  starting transfers between devices  24.1 us (13%)
  local copies, waits for them, and re-layouts  8.29 us (4%)
    ppermute x15, waiting for transfers between devices, swapped(): lax.ppermute(value, AXES, [(source, source ^ mask) for source in range(co...  51.3 us
    pallas_call x1, Pallas kernels, setup(): pl.pallas_call(setup_kernel, out_shape=[jax.ShapeDtypeStruct((LEAVES, LEA...  24.2 us
    ppermute x15, starting transfers between devices, swapped(): lax.ppermute(value, AXES, [(source, source ^ mask) for source in range(co...  24.1 us
    pallas_call x1, Pallas kernels, near_first(): pl.pallas_call(near_first_kernel, grid=(LEAVES,), out_shape=[jax.ShapeDty...  24.1 us
    pallas_call x1, Pallas kernels, near_second(): pl.pallas_call(near_second_kernel, grid=(LEAVES,), out_shape=jax.ShapeDty...  18.6 us
    pallas_call x1, Pallas kernels, unsort(): pl.pallas_call(unsort_kernel, out_shape=jax.ShapeDtypeStruct((2 * SIDES,...  12 us
    pallas_call x1, Pallas kernels, finish(): pl.pallas_call(finish_kernel, out_shape=[jax.ShapeDtypeStruct((SIDES, SPA...  11.8 us
    unnamed x27, local copies, waits for them, and re-layouts  8.08 us
  transfers between devices with their start and end apart: 15, of which 12 were waited for; matrix products, arithmetic and copies ran while one was open for 0% of the time, Pallas kernels for 29%

commit v1 on v0

v1 whole, which is shorter than its diff:
```python
import math

import jax
import jax.numpy as jnp
from jax import lax
from jax.experimental import pallas as pl
from jax.experimental.pallas import tpu as pltpu
from jax.sharding import PartitionSpec as P

AXES = ("outer", "inner")
f32 = jnp.float32
bf16 = jnp.bfloat16
HIGHEST = lax.Precision.HIGHEST

DIM = 64
LEAVES = 16
LEAF = 512
SPAN = LEAVES * LEAF
RANK = 256
SIDES = 32
MID = 4
LIST = 4
LANES = 128
SQ = DIM
RHS_LANE = LANES - SIDES
EXPO = -(2.0 / DIM) * math.log2(math.e)
NEAR_SCALE = 32.0 / math.sqrt(LEAF * LIST)
FAR_SCALE = 64.0 / math.sqrt(RANK * LIST)

C_ROWS = RANK // 2 + 2 * 16
S_ROWS = 2 * SIDES
S1_AT = MID * C_ROWS
MID_ROWS = MID * (C_ROWS + S_ROWS)
S2_AT = MID_ROWS + C_ROWS
PAY_ROWS = S2_AT + S_ROWS
TOP_ROWS = C_ROWS + S_ROWS
S1_ROWS = MID * S_ROWS
PAY2_ROWS = S1_ROWS + S_ROWS
GROUPS = LEAVES // LIST
PAIRS = [(p, q) for p in range(LIST) for q in range(p, LIST)]

VM = pl.BlockSpec(memory_space=pltpu.VMEM)
SM = pl.BlockSpec(memory_space=pltpu.SMEM)
HBM = pl.BlockSpec(memory_space=pltpu.HBM)


def params(mib):
    return pltpu.CompilerParams(vmem_limit_bytes=mib * 2**20)


def in_hbm(*arrays):
    return [pltpu.with_memory_space_constraint(array, pltpu.HBM) for array in arrays]


def lasting(microseconds):
    return pl.CostEstimate(flops=int(1.15e9 * microseconds), bytes_accessed=0, transcendentals=0)


def nt(left, right):
    return lax.dot_general(left, right, (((1,), (1,)), ((), ())), preferred_element_type=f32)


def nn(left, right):
    return jnp.dot(left, right, preferred_element_type=f32)


def target_side(rows):
    lane = lax.broadcasted_iota(jnp.int32, rows.shape, 1)
    values = rows.astype(f32)
    shifted = pltpu.roll(values, 3, 1)
    other = jnp.where(lane < SQ + 3, 1.0, jnp.where(lane < SQ + 6, shifted, 0.0))
    return jnp.where(lane < SQ, -2.0 * values, other).astype(bf16)


def tile(source_rows, target_rows):
    return jnp.exp2(EXPO * nt(source_rows, target_rows)).astype(bf16)


def split(values):
    high = values.astype(bf16)
    return high, (values - high.astype(f32)).astype(bf16)


def halves(pay_ref, at, values):
    for half in range(2):
        pay_ref[at + half * SIDES : at + (half + 1) * SIDES, :] = values[:, half * LANES : (half + 1) * LANES]


def joined(ref, slot, at):
    return jnp.concatenate([ref[slot, pl.ds(at + half * SIDES, SIDES), :] for half in range(2)], axis=1)


def climb(s0_ref, mid_ref, top_ref, pay_ref, s1_at, s2_at):
    total = jnp.zeros((SIDES, RANK), f32)
    for node in range(MID):
        children = jnp.concatenate([s0_ref[4 * node + k] for k in range(4)], axis=1)
        s1 = nt(children, mid_ref[node]).astype(bf16)
        halves(pay_ref, s1_at + node * S_ROWS, s1)
        total = total + nt(s1, top_ref[node])
    halves(pay_ref, s2_at, total.astype(bf16))


def pack_points(pay_ref, at, rows):
    lane = lax.broadcasted_iota(jnp.int32, (LANES, LANES), 1)
    second = pltpu.roll(rows[LANES:, :], DIM, 1)
    pay_ref[at : at + LANES, :] = jnp.where(lane < DIM, rows[:LANES, :], second).astype(bf16)
    squares = rows.T[SQ : SQ + 16, :].astype(bf16)
    for half in range(2):
        start = at + LANES + 16 * half
        pay_ref[start : start + 16, :] = squares[:, half * LANES : (half + 1) * LANES]


def unpack_points(ref, slot, at):
    lane = lax.broadcasted_iota(jnp.int32, (LANES, LANES), 1)
    packed = ref[slot, pl.ds(at, LANES), :].astype(f32)
    points = jnp.concatenate([packed, pltpu.roll(packed, DIM, 1)], axis=0)
    lane = lax.broadcasted_iota(jnp.int32, (RANK, LANES), 1)
    points = jnp.where(lane < DIM, points, jnp.where(lane < DIM + 3, 1.0, 0.0)).astype(bf16)
    squares = jnp.concatenate([ref[slot, pl.ds(at + LANES + 16 * half, 16), :] for half in range(2)], axis=1).astype(f32)
    return points, squares[0:1] + squares[1:2] + squares[2:3]


def far_tile(target, source):
    points, squares = source
    return jnp.exp2(EXPO * (nt(target, points) + squares)).astype(bf16)


def far_target(points, squares):
    lane = lax.broadcasted_iota(jnp.int32, (RANK, LANES), 1)
    values = points.astype(f32)
    columns = jnp.concatenate([squares, jnp.zeros((7, RANK), f32)], axis=0).T
    column = columns[:, 0:1]
    high = column.astype(bf16).astype(f32)
    middle = (column - high).astype(bf16).astype(f32)
    low = column - high - middle
    parts = jnp.where(lane == SQ, high, jnp.where(lane == SQ + 1, middle, jnp.where(lane == SQ + 2, low, 0.0)))
    return jnp.where(lane < SQ, -2.0 * values, parts).astype(bf16)


def setup_kernel(
    leaf_skel, skel_mid, near, order_hbm, skel_top_hbm, points_hbm, rhs_hbm, leaf_hbm, mid_hbm, top_hbm,
    a_out, b_out, r_out, pay, perm,
    order, skel_top, points, rhs, rows, tree, skel, leaf_v, mid_v, top_v, s0, sources, sems,
):
    device = this_device()
    eight = pl.multiple_of(device // 8 * 8, 8)
    quarter = SPAN // 4
    small = [
        pltpu.make_async_copy(order_hbm, order, sems.at[0]),
        pltpu.make_async_copy(skel_top_hbm.at[pl.ds(eight, 8), :], skel_top, sems.at[1]),
    ]
    chunks = []
    for i in range(4):
        part = pl.ds(i * quarter, quarter)
        chunks.append([
            pltpu.make_async_copy(points_hbm.at[:, part], points.at[:, part], sems.at[2 + i]),
            pltpu.make_async_copy(rhs_hbm.at[:, part], rhs.at[:, part], sems.at[6 + i]),
        ])
    large = [
        pltpu.make_async_copy(leaf_hbm, leaf_v, sems.at[10]),
        pltpu.make_async_copy(mid_hbm, mid_v, sems.at[11]),
        pltpu.make_async_copy(top_hbm, top_v, sems.at[12]),
    ]
    for copy in small + sum(chunks, []) + large:
        copy.start()

    count = jnp.int32(0)
    for leaf in range(LEAVES):
        members = [near[m, leaf] & (LEAVES - 1) for m in range(LIST)]
        first = jnp.minimum(jnp.minimum(members[0], members[1]), jnp.minimum(members[2], members[3]))
        leads = first == leaf

        @pl.when(leads)
        def _(members=members, count=count):
            for m in range(LIST):
                perm[count * LIST + m] = members[m]

        count = count + leads.astype(jnp.int32)

    def turn(step, _):
        at = pl.multiple_of(step * LEAF, LEAF)
        values = points[:, pl.ds(at, LEAF)].astype(f32)
        square = jnp.sum(values * values, axis=0, keepdims=True)
        high = square.astype(bf16).astype(f32)
        middle = (square - high).astype(bf16).astype(f32)
        low = square - high - middle
        row = lax.broadcasted_iota(jnp.int32, (SIDES, LEAF), 0)
        extra = jnp.where(row == 0, high, jnp.where(row == 1, middle, jnp.where(row == 2, low, jnp.where(row < 6, 1.0, 0.0))))
        stacked = jnp.concatenate([values, extra, rhs[:, pl.ds(at, LEAF)]], axis=0)
        rows[pl.ds(at, LEAF), :] = stacked.T
        return 0

    for i in range(4):
        for copy in chunks[i]:
            copy.wait()
        lax.fori_loop(4 * i, 4 * i + 4, turn, 0)
    for copy in small:
        copy.wait()

    unroll = 16

    for node in range(MID):
        def pick_mid(step, _, node=node):
            base = step * unroll
            spots = [skel_mid[node, base + u] for u in range(unroll)]
            leaves = [4 * node + (at >> 8) for at in spots]
            inner = [leaf_skel[leaf, at & (RANK - 1)] for leaf, at in zip(leaves, spots)]
            found = [order[leaf * LEAF + at] for leaf, at in zip(leaves, inner)]
            for u in range(unroll):
                skel[pl.ds(node * RANK + base + u, 1), :] = rows[pl.ds(found[u], 1), :]
            for u in range(unroll):
                sources[node * RANK + base + u] = found[u]
            return 0

        lax.fori_loop(0, RANK // unroll, pick_mid, 0)

    own = device & 7

    def pick_top(step, _):
        base = step * unroll
        spots = [skel_top[own, base + u] for u in range(unroll)]
        found = [sources[at] for at in spots]
        for u in range(unroll):
            skel[pl.ds(MID * RANK + base + u, 1), :] = rows[pl.ds(found[u], 1), :]
        return 0

    lax.fori_loop(0, RANK // unroll, pick_top, 0)
    for node in range(MID + 1):
        pack_points(pay, MID_ROWS if node == MID else node * C_ROWS, skel[node * RANK : (node + 1) * RANK, :])

    for copy in large:
        copy.wait()

    def one_leaf(place, _):
        leaf = perm[place]
        base = leaf * LEAF

        def pick(step, _):
            at = step * 64
            for u in range(64):
                source = order[base + at + u]
                tree[pl.ds(at + u, 1), :] = rows[pl.ds(source, 1), :]
            return 0

        lax.fori_loop(0, LEAF // 64, pick, 0)
        values = tree[...]
        a_out[place] = values.astype(bf16)
        b_out[place] = target_side(values)
        right = values.T[RHS_LANE:, :]
        r_out[place] = right
        s0[leaf] = nt(right.astype(bf16), leaf_v[leaf]).astype(bf16)
        return 0

    lax.fori_loop(0, LEAVES, one_leaf, 0)
    climb(s0, mid_v, top_v, pay, S1_AT, S2_AT)


def interp_scratch():
    return [
        pltpu.VMEM((LEAVES, RANK, LEAF), bf16),
        pltpu.VMEM((MID, RANK, 4 * RANK), bf16),
        pltpu.VMEM((MID, RANK, RANK), bf16),
    ]


def setup(leaf_skel, skel_mid, near, order, skel_top, points, rhs, interps):
    order, skel_top, points, rhs, *interps = in_hbm(order, skel_top, points, rhs, *interps)
    return pl.pallas_call(
        setup_kernel,
        out_shape=[
            jax.ShapeDtypeStruct((LEAVES, LEAF, LANES), bf16),
            jax.ShapeDtypeStruct((LEAVES, LEAF, LANES), bf16),
            jax.ShapeDtypeStruct((LEAVES, SIDES, LEAF), f32),
            jax.ShapeDtypeStruct((PAY_ROWS, LANES), bf16),
            jax.ShapeDtypeStruct((LEAVES,), jnp.int32),
        ],
        in_specs=[SM] * 3 + [HBM] * 7,
        out_specs=[VM] * 4 + [SM],
        scratch_shapes=[
            pltpu.SMEM((SPAN,), jnp.int32),
            pltpu.SMEM((8, RANK), jnp.int32),
            pltpu.VMEM((DIM, SPAN), bf16),
            pltpu.VMEM((SIDES, SPAN), f32),
            pltpu.VMEM((SPAN, LANES), f32),
            pltpu.VMEM((LEAF, LANES), f32),
            pltpu.VMEM(((MID + 1) * RANK, LANES), f32),
            *interp_scratch(),
            pltpu.VMEM((LEAVES, SIDES, RANK), bf16),
            pltpu.SMEM((MID * RANK,), jnp.int32),
            pltpu.SemaphoreType.DMA((13,)),
        ],
        compiler_params=params(32),
        cost_estimate=lasting(20),
    )(leaf_skel, skel_mid, near, order, skel_top, points, rhs, *interps)


def apply_near(weights, tiles, out):
    for target in range(LIST):
        total = jnp.zeros((weights[0].shape[0], LEAF), f32)
        for source in range(LIST):
            block = tiles[PAIRS.index((min(source, target), max(source, target)))]
            total = total + (nn if source <= target else nt)(weights[source], block)
        out[target] = total if total.shape[0] == SIDES else total[:SIDES] + total[SIDES:]


def near_first(group, a_rows, b_rows, right):
    def kernel(a_ref, b_ref, r_ref, out, tiles):
        for i, (p, q) in enumerate(PAIRS):
            tiles[i] = tile(a_ref[LIST * group + p], b_ref[LIST * group + q])
        apply_near([r_ref[LIST * group + s].astype(bf16) for s in range(LIST)], tiles, out)

    return pl.pallas_call(
        kernel,
        out_shape=[
            jax.ShapeDtypeStruct((LIST, SIDES, LEAF), f32),
            jax.ShapeDtypeStruct((len(PAIRS), LEAF, LEAF), bf16),
        ],
        in_specs=[VM] * 3,
        out_specs=[VM] * 2,
        compiler_params=params(16),
        cost_estimate=lasting(3.3),
    )(a_rows, b_rows, right)


def near_second(group, tiles, image):
    def kernel(tiles_ref, q_ref, out):
        weights = [jnp.concatenate(split(q_ref[LIST * group + s]), axis=0) for s in range(LIST)]
        apply_near(weights, tiles_ref, out)

    return pl.pallas_call(
        kernel,
        out_shape=jax.ShapeDtypeStruct((LIST, SIDES, LEAF), f32),
        in_specs=[VM] * 2,
        out_specs=VM,
        compiler_params=params(16),
        cost_estimate=lasting(2.6),
    )(tiles, image)


def descend(mid_far, top_far, perm, mid_v, top_v, leaf_v, u0, base_ref, near_refs, out):
    u2 = (FAR_SCALE * top_far).astype(bf16)
    for node in range(MID):
        u1 = (FAR_SCALE * mid_far[node] + nn(u2, top_v[node])).astype(bf16)
        down = nn(u1, mid_v[node]).astype(bf16)
        for k in range(4):
            u0[4 * node + k] = down[:, k * RANK : (k + 1) * RANK]
    for place in range(LEAVES):
        leaf = perm[place]
        far = nn(u0[leaf], leaf_v[leaf])
        out[place] = base_ref[place] + NEAR_SCALE * near_refs[place // LIST][place % LIST] + far


def top_slot(entry, device):
    mask = (entry ^ device) & 15
    ring = ((mask >> 1) & 1) ^ ((mask >> 2) & 1)
    return ring | (((mask >> 2) & 1) << 1) | (((mask >> 3) & 1) << 2) | ((mask & 1) << 3)


def mid_slot(entry, device):
    mask = ((entry >> 2) ^ device) & 3
    return (mask >> 1) | ((mask & 1) << 1)


def this_device():
    return lax.axis_index("outer") * lax.axis_size("inner") + lax.axis_index("inner")


def pool_copies(pair_a, pair_b, eight_a, eight_b, four, sixteen, sems):
    return [
        pltpu.make_async_copy(pair_a, four.at[0:2], sems.at[0]),
        pltpu.make_async_copy(pair_b, four.at[2:4], sems.at[1]),
        pltpu.make_async_copy(eight_a, sixteen.at[0:8], sems.at[2]),
        pltpu.make_async_copy(eight_b, sixteen.at[8:16], sems.at[3]),
    ]


def far_first_kernel(
    far_mid, far_top, perm, pair_a, pair_b, eight_a, eight_b, leaf_v, mid_v, top_v, right, near0, near1, near2, near3,
    q_out, pay, mid_tiles, top_tiles,
    four, sixteen, s0, sems,
):
    pools = pool_copies(pair_a, pair_b, eight_a, eight_b, four, sixteen, sems)
    for copy in pools:
        copy.start()
    for copy in pools:
        copy.wait()
    device = this_device()

    target = far_target(*unpack_points(sixteen, 0, 0))
    top_far = jnp.zeros((SIDES, RANK), f32)
    for m in range(LIST):
        slot = top_slot(far_top[m, device], device)
        block = far_tile(target, unpack_points(sixteen, slot, 0))
        top_tiles[m] = block
        top_far = top_far + nt(joined(sixteen, slot, C_ROWS), block)
    mid_far = []
    for node in range(MID):
        target = far_target(*unpack_points(four, 0, node * C_ROWS))
        total = jnp.zeros((SIDES, RANK), f32)
        for m in range(LIST):
            entry = far_mid[node, m]
            slot = mid_slot(entry, device)
            local = entry & 3
            block = far_tile(target, unpack_points(four, slot, pl.multiple_of(local * C_ROWS, C_ROWS)))
            mid_tiles[node * LIST + m] = block
            total = total + nt(joined(four, slot, pl.multiple_of(S1_AT + local * S_ROWS, S_ROWS)), block)
        mid_far.append(total)
    descend(mid_far, top_far, perm, mid_v, top_v, leaf_v, s0, right, (near0, near1, near2, near3), q_out)
    for place in range(LEAVES):
        leaf = perm[place]
        raised = nt(jnp.concatenate(split(q_out[place]), axis=0), leaf_v[leaf])
        s0[leaf] = (raised[:SIDES] + raised[SIDES:]).astype(bf16)
    climb(s0, mid_v, top_v, pay, 0, S1_ROWS)


def far_first(far_mid, far_top, perm, pools, interps, right, near):
    return pl.pallas_call(
        far_first_kernel,
        out_shape=[
            jax.ShapeDtypeStruct((LEAVES, SIDES, LEAF), f32),
            jax.ShapeDtypeStruct((PAY2_ROWS, LANES), bf16),
            jax.ShapeDtypeStruct((MID * LIST, RANK, RANK), bf16),
            jax.ShapeDtypeStruct((LIST, RANK, RANK), bf16),
        ],
        in_specs=[SM] * 3 + [pl.BlockSpec(memory_space=pl.ANY)] * 4 + [VM] * 8,
        out_specs=[VM] * 4,
        scratch_shapes=[
            pltpu.VMEM((4, PAY_ROWS, LANES), bf16),
            pltpu.VMEM((16, TOP_ROWS, LANES), bf16),
            pltpu.VMEM((LEAVES, SIDES, RANK), bf16),
            pltpu.SemaphoreType.DMA((4,)),
        ],
        compiler_params=params(14),
        cost_estimate=lasting(8),
    )(far_mid, far_top, perm, *pools, *interps, right, *near)


def far_second_kernel(
    far_mid, far_top, perm, pair_a, pair_b, eight_a, eight_b, leaf_v, mid_v, top_v, mid_tiles, top_tiles,
    right, image, near0, near1, near2, near3,
    p_out, gram,
    four, sixteen, u0, sems,
):
    pools = pool_copies(pair_a, pair_b, eight_a, eight_b, four, sixteen, sems)
    for copy in pools:
        copy.start()
    for copy in pools:
        copy.wait()
    device = this_device()
    top_far = jnp.zeros((SIDES, RANK), f32)
    for m in range(LIST):
        top_far = top_far + nt(joined(sixteen, top_slot(far_top[m, device], device), 0), top_tiles[m])
    mid_far = []
    for node in range(MID):
        total = jnp.zeros((SIDES, RANK), f32)
        for m in range(LIST):
            entry = far_mid[node, m]
            weights = joined(four, mid_slot(entry, device), pl.multiple_of((entry & 3) * S_ROWS, S_ROWS))
            total = total + nt(weights, mid_tiles[node * LIST + m])
        mid_far.append(total)
    descend(mid_far, top_far, perm, mid_v, top_v, leaf_v, u0, image, (near0, near1, near2, near3), p_out)
    total = jnp.zeros((4 * SIDES, 6 * SIDES), f32)
    for place in range(LEAVES):
        parts = [split(ref[place]) for ref in (right, image, p_out)]
        left = jnp.concatenate([part[i] for i in range(2) for part in parts[:2]], axis=0)
        total = total + nt(left, jnp.concatenate([part[i] for i in range(2) for part in parts], axis=0))
    total = total[: 2 * SIDES] + total[2 * SIDES :]
    turned = total.T
    total = (turned[: 3 * SIDES] + turned[3 * SIDES :]).T
    gram[...] = total


def far_second(far_mid, far_top, perm, pools, interps, mid_tiles, top_tiles, right, image, near):
    return pl.pallas_call(
        far_second_kernel,
        out_shape=[
            jax.ShapeDtypeStruct((LEAVES, SIDES, LEAF), f32),
            jax.ShapeDtypeStruct((2 * SIDES, 3 * SIDES), f32),
        ],
        in_specs=[SM] * 3 + [pl.BlockSpec(memory_space=pl.ANY)] * 4 + [VM] * 11,
        out_specs=[VM] * 2,
        scratch_shapes=[
            pltpu.VMEM((4, PAY2_ROWS, LANES), bf16),
            pltpu.VMEM((16, S_ROWS, LANES), bf16),
            pltpu.VMEM((LEAVES, SIDES, RANK), bf16),
            pltpu.SemaphoreType.DMA((4,)),
        ],
        compiler_params=params(14),
        cost_estimate=lasting(8),
    )(far_mid, far_top, perm, *pools, *interps, mid_tiles, top_tiles, right, image, *near)


PARTS = 2
PART = SPAN // PARTS


def put_back(group, order, perm, image, second, rows):
    def kernel(order_ref, perm_ref, q_ref, p_ref, *refs):
        out, tree = refs[-2:]
        for member in range(LIST):
            place = LIST * group + member
            stacked = jnp.concatenate([q_ref[place], p_ref[place], jnp.zeros((2 * SIDES, LEAF), f32)], axis=0)
            tree[member * LEAF : (member + 1) * LEAF, :] = stacked.T

        for member in range(LIST):
            base = perm_ref[LIST * group + member] * LEAF

            def put(step, _, member=member, base=base):
                at = step * 64
                for u in range(64):
                    out[pl.ds(order_ref[base + at + u], 1), :] = tree[pl.ds(member * LEAF + at + u, 1), :]
                return 0

            lax.fori_loop(0, LEAF // 64, put, 0)

    earlier = [] if rows is None else [rows]
    return pl.pallas_call(
        kernel, out_shape=jax.ShapeDtypeStruct((SPAN, LANES), f32),
        in_specs=[SM] * 2 + [VM] * (2 + len(earlier)), out_specs=VM,
        scratch_shapes=[pltpu.VMEM((LIST * LEAF, LANES), f32)],
        input_output_aliases={4: 0} if earlier else {},
        compiler_params=params(12), cost_estimate=lasting(2.5),
    )(order, perm, image, second, *earlier)


def to_columns(part, rows):
    def kernel(rows_ref, out):
        for i in range(PART // LEAF):
            at = part * PART + i * LEAF
            out[:, i * LEAF : (i + 1) * LEAF] = rows_ref[at : at + LEAF, :].T[: 2 * SIDES, :]

    return pl.pallas_call(
        kernel, out_shape=jax.ShapeDtypeStruct((2 * SIDES, PART), f32), in_specs=[VM], out_specs=VM,
        compiler_params=params(12), cost_estimate=lasting(2),
    )(rows)


def dot(left, right, contract=(1, 0)):
    return lax.dot_general(
        left, right, (((contract[0],), (contract[1],)), ((), ())), preferred_element_type=f32, precision=HIGHEST
    )


def eliminate(systems):
    row = lax.broadcasted_iota(jnp.int32, (SIDES, 1), 0)
    for k in range(SIDES):
        following = []
        for matrix, values in systems:
            scale = 1.0 / matrix[k : k + 1, k : k + 1]
            column = matrix[:, k : k + 1]
            matrix_row = matrix[k : k + 1, :] * scale
            values_row = values[k : k + 1, :] * scale
            following.append((
                jnp.where(row == k, matrix_row, matrix - column * matrix_row),
                jnp.where(row == k, values_row, values - column * values_row),
            ))
        systems = following
    return [values for _, values in systems]


def finish_kernel(gram, rhs, mapped0, mapped1, x_out, r_out):
    n = SIDES
    rr, rq, rp = gram[0:n, 0:n], gram[0:n, n : 2 * n], gram[0:n, 2 * n : 3 * n]
    qr, qq, qp = gram[n : 2 * n, 0:n], gram[n : 2 * n, n : 2 * n], gram[n : 2 * n, 2 * n : 3 * n]
    eye = (lax.broadcasted_iota(jnp.int32, (n, n), 0) == lax.broadcasted_iota(jnp.int32, (n, n), 1)).astype(f32)
    alpha, rr_inverse = eliminate([(0.5 * (rq + qr), rr), (rr, eye)])
    rq_alpha = dot(rq, alpha)
    rho = rr - rq_alpha - dot(alpha, qr, (0, 0)) + dot(alpha, dot(qq, alpha), (0, 0))
    first = eye + dot(rr_inverse, rho)
    half = dot(first, dot(rq, first) - dot(rp, alpha), (0, 0)) - dot(alpha, dot(qq, first) - dot(qp, alpha), (0, 0))
    turned = dot(half, eye, (0, 0))
    (beta,) = eliminate([(0.5 * (half + turned), rho)])
    c0 = alpha + dot(first, beta)
    c1 = -dot(alpha, beta)

    lane = lax.broadcasted_iota(jnp.int32, (n, LANES), 1)
    place = lax.broadcasted_iota(jnp.int32, (n, LANES), 0)
    to_x = ((lane & 63) == place).astype(f32)
    to_r = ((lane & 63) == place + n).astype(f32)
    combine = jnp.concatenate(
        [dot(c0, to_x), dot(c1, to_x) - dot(c0, to_r), -dot(c1, to_r), jnp.zeros((n, LANES), f32)], axis=0
    ).T
    high, low = split(combine)
    upper = lax.broadcasted_iota(jnp.int32, (LANES, LANES), 0) < 2 * n
    both = jnp.where(upper, high.astype(f32), low.astype(f32)).astype(bf16)
    both = jnp.concatenate([both, both], axis=1)

    for i in range(LEAVES):
        span = slice(i * LEAF, (i + 1) * LEAF)
        part = (mapped0, mapped1)[i * LEAF // PART]
        at = i * LEAF % PART
        right = rhs[:, span]
        stacked = jnp.concatenate([right, part[:, at : at + LEAF], jnp.zeros((n, LEAF), f32)], axis=0)
        result = nn(both, jnp.concatenate(split(stacked), axis=0))
        result = result[: 2 * n] + result[2 * n :]
        x_out[:, span] = result[:n]
        r_out[:, span] = right + result[n:]


def finish(gram, rhs, mapped):
    return pl.pallas_call(
        finish_kernel,
        out_shape=[jax.ShapeDtypeStruct((SIDES, SPAN), f32)] * 2,
        in_specs=[VM] * 4,
        out_specs=[VM] * 2,
        compiler_params=params(24),
    )(gram, rhs, *mapped)


def swapped(value, mask):
    count = lax.axis_size(AXES)
    return lax.ppermute(value, AXES, [(source, source ^ mask) for source in range(count)])


def gather_pools(payload, top_at, inputs, steps):
    done = []

    def beside(step, values):
        nonlocal inputs
        arrived, results, inputs = lax.optimization_barrier((values, steps[step](inputs), inputs))
        done.append(results)
        return arrived

    pair = jnp.stack([payload, beside(0, swapped(payload, 2))])
    two = pair[:, top_at:]
    four = jnp.concatenate([two, beside(1, swapped(two, 6))])
    eight = jnp.concatenate([four, beside(2, swapped(four, 8))])
    other_pair, other_eight = beside(3, (swapped(pair, 1), swapped(eight, 1)))
    return (pair, other_pair, eight, other_eight), [result for results in done for result in results]


def shards(
    points, tree_order, rhs, leaf_skel, skel_mid, skel_top, near_lists, far_mid, far_top,
    leaf_interp, interp_mid, interp_top,
):
    interps = (leaf_interp, interp_mid, interp_top)
    a_rows, b_rows, right, payload, perm = setup(
        leaf_skel, skel_mid, near_lists.T, tree_order, skel_top, points, rhs, interps
    )
    def first(*groups):
        return lambda inputs: [near_first(group, *inputs) for group in groups]

    pools, found = gather_pools(payload, MID_ROWS, (a_rows, b_rows, right), [first(0, 1), first(2), first(3), first()])
    near, tiles = zip(*found)
    lists = (far_mid, far_top.T)
    image, payload, mid_tiles, top_tiles = far_first(*lists, perm, pools, interps, right, near)
    def again(*groups):
        return lambda inputs: [near_second(group, tiles[group], *inputs) for group in groups]

    pools, near = gather_pools(payload, S1_ROWS, (image,), [again(0), again(1), again(2), again(3)])
    second, gram = far_second(*lists, perm, pools, interps, mid_tiles, top_tiles, right, image, near)
    rows = None
    for group in range(GROUPS):
        rows = put_back(group, tree_order, perm, image, second, rows)
    mapped = [to_columns(part, rows) for part in range(PARTS)]
    for mask in (1, 2, 6, 8, 24, 32, 96):
        gram = gram + swapped(gram, mask)
    return tuple(finish(gram, rhs, mapped))


def solution(mesh):
    placed = (
        P(None, AXES), P(AXES), P(None, AXES), P(AXES, None), P(AXES, None), P(), P(AXES, None), P(AXES, None), P(),
        P(AXES, None, None), P(AXES, None, None), P(AXES, None, None),
    )
    return jax.shard_map(
        shards, mesh=mesh, in_specs=placed, out_specs=(P(None, AXES), P(None, AXES)), check_vma=False
    )
```

time: 192 us -> 124 us (0.65)
  waiting for transfers between devices: 51.3 us -> 16.4 us
  Pallas kernels: 106 us -> 83.6 us
  local copies, waits for them, and re-layouts: 8.29 us -> 2.12 us
  starting transfers between devices: 24.1 us -> 21 us
    ppermute x15 -> x17, waiting for transfers between devices: 51.3 us -> 16.4 us  [swapped(): lax.ppermute(value, AXES, [(source, source ^ mask) for source in range(co...]
    pallas_call x3 -> x14, Pallas kernels: 54.7 us -> 34.5 us  [the longest x4 12.9 us: near_first(): pl.pallas_call(kernel, out_shape=[jax.ShapeDtypeStruct((LIST, SIDES, LEAF...]
    unnamed x27 -> x20, local copies, waits for them, and re-layouts: 8.08 us -> 2.12 us
    ppermute x15 -> x17, starting transfers between devices: 24.1 us -> 21 us  [swapped(): lax.ppermute(value, AXES, [(source, source ^ mask) for source in range(co...]
    pallas_call x1, Pallas kernels: 11.8 us -> 9.42 us  [finish(): pl.pallas_call(finish_kernel, out_shape=[jax.ShapeDtypeStruct((SIDES, SPA...]
  transfers between devices with their start and end apart: 15 -> 17, of which waited for: 12 -> 11; matrix products, arithmetic and copies ran while one was open for 0% -> 0% of each run, Pallas kernels for 29% -> 28%
where the time goes in v1:
time: 124 us
  Pallas kernels  83.6 us (67%)
  starting transfers between devices  21 us (17%)
  waiting for transfers between devices  16.4 us (13%)
  local copies, waits for them, and re-layouts  2.12 us (2%)
    pallas_call x1, Pallas kernels, setup(): pl.pallas_call(setup_kernel, out_shape=[jax.ShapeDtypeStruct((LEAVES, LEA...  25.6 us
    ppermute x17, starting transfers between devices, swapped(): lax.ppermute(value, AXES, [(source, source ^ mask) for source in range(co...  21 us
    ppermute x17, waiting for transfers between devices, swapped(): lax.ppermute(value, AXES, [(source, source ^ mask) for source in range(co...  16.4 us
    pallas_call x4, Pallas kernels, near_first(): pl.pallas_call(kernel, out_shape=[jax.ShapeDtypeStruct((LIST, SIDES, LEAF...  12.9 us
    pallas_call x4, Pallas kernels, put_back(): pl.pallas_call(kernel, out_shape=jax.ShapeDtypeStruct((SPAN, LANES), f32)...  12.6 us
    pallas_call x1, Pallas kernels, finish(): pl.pallas_call(finish_kernel, out_shape=[jax.ShapeDtypeStruct((SIDES, SPA...  9.42 us
    pallas_call x4, Pallas kernels, near_second(): pl.pallas_call(kernel, out_shape=jax.ShapeDtypeStruct((LIST, SIDES, LEAF)...  7.83 us
    pallas_call x1, Pallas kernels, far_first(): pl.pallas_call(far_first_kernel, out_shape=[jax.ShapeDtypeStruct((LEAVES,...  7.54 us
  transfers between devices with their start and end apart: 17, of which 11 were waited for; matrix products, arithmetic and copies ran while one was open for 0% of the time, Pallas kernels for 28%

profile of v1, /device:TPU:0, one launch (start us, length us, event | category | flops | bytes accessed | tf_op | source)
XLA Modules:
  0.0 124.3 jit_solution(12545613276597371377)
XLA Ops:
  2.7 25.6 %shard_map.131 = (bf16[16,512,128]{2,1,0:T(8,128)(2,1)S(1)}, bf16[16,512,128]{2,1,0:T(8,128)(2,1)S(1)}, f32[16,32,512]{2,1,0:T(8,128)S(1)}, bf16[1120,128]{1,0:T(8,128)(2,1)S(1)}, s32[16]{0:T(128)S(1)}) custom-call(s32[16,256]{1,0:T(8,128)S(1)} %copy-done.5, s32[4,256]{1,0:T(4,128)S(1)} %copy-done.6, s32[4,16]{1,0:T(4,128)S(1)} %bitcast.10, s32[8192]{0:T(1024)} %order_ref.7, ...), custom_call_target="tpu_custom_call" | custom-call | flops 23000000512 | tf_op jit(solution)/shard_map/pallas_call | solution.py:268
  28.3 1.7 %collective-permute-start = (bf16[1120,128]{1,0:T(8,128)(2,1)S(1)}, bf16[1120,128]{1,0:T(8,128)(2,1)S(1)}, u32[]{:S(2)}, u32[]{:S(2)}) collective-permute-start(bf16[1120,128]{1,0:T(8,128)(2,1)S(1)} %get-tuple-element.53), channel_id=1, source_target_pairs={{0,2},{1,3},{2,0},{3,1},{4,6},{5,7},{6,4},{7,5},{8,10},{9,11},{10,... | collective-permute-start | bytes 860168 | tf_op jit(solution)/shard_map/ppermute | solution.py:612
  30.0 3.2 %shard_map.133 = (f32[4,32,512]{2,1,0:T(8,128)S(1)}, bf16[10,512,512]{2,1,0:T(8,128)(2,1)S(1)}) custom-call(bf16[16,512,128]{2,1,0:T(8,128)(2,1)S(1)} %get-tuple-element.68.a_ref, bf16[16,512,128]{2,1,0:T(8,128)(2,1)S(1)} %get-tuple-element.69.b_ref, f32[16,32,512]{2,1,0:T(8,128)S(1)} %get-tuple-element.70.r_ref.right), custom_call_target="tpu_custom_call" | custom-call | flops 3795000064 | tf_op jit(solution)/shard_map/pallas_call | solution.py:312
  33.2 3.2 %shard_map.132 = (f32[4,32,512]{2,1,0:T(8,128)S(1)}, bf16[10,512,512]{2,1,0:T(8,128)(2,1)S(1)}) custom-call(bf16[16,512,128]{2,1,0:T(8,128)(2,1)S(1)} %get-tuple-element.68.a_ref, bf16[16,512,128]{2,1,0:T(8,128)(2,1)S(1)} %get-tuple-element.69.b_ref, f32[16,32,512]{2,1,0:T(8,128)S(1)} %get-tuple-element.70.r_ref.right), custom_call_target="tpu_custom_call" | custom-call | flops 3795000064 | tf_op jit(solution)/shard_map/pallas_call | solution.py:312
  36.9 3.1 %collective-permute-start.2 = (bf16[2,224,128]{2,1,0:T(8,128)(2,1)S(1)}, bf16[2,224,128]{2,1,0:T(8,128)(2,1)S(1)}, u32[]{:S(2)}, u32[]{:S(2)}) collective-permute-start(bf16[2,224,128]{2,1,0:T(8,128)(2,1)S(1)} %fusion), channel_id=1, source_target_pairs={{0,6},{1,7},{2,4},{3,5},{4,2},{5,3},{6,0},{7,1},{8,14},{9,15},{10,... | collective-permute-start | bytes 344072 | tf_op jit(solution)/shard_map/ppermute | solution.py:612
  40.0 3.2 %shard_map.134 = (f32[4,32,512]{2,1,0:T(8,128)S(1)}, bf16[10,512,512]{2,1,0:T(8,128)(2,1)S(1)}) custom-call(bf16[16,512,128]{2,1,0:T(8,128)(2,1)S(1)} %get-tuple-element.68.a_ref, bf16[16,512,128]{2,1,0:T(8,128)(2,1)S(1)} %get-tuple-element.69.b_ref, f32[16,32,512]{2,1,0:T(8,128)S(1)} %get-tuple-element.70.r_ref.right), custom_call_target="tpu_custom_call" | custom-call | flops 3795000064 | tf_op jit(solution)/shard_map/pallas_call | solution.py:312
  43.3 1.8 %collective-permute-start.3 = (bf16[4,224,128]{2,1,0:T(8,128)(2,1)S(1)}, bf16[4,224,128]{2,1,0:T(8,128)(2,1)S(1)}, u32[]{:S(2)}, u32[]{:S(2)}) collective-permute-start(bf16[4,224,128]{2,1,0:T(8,128)(2,1)S(1)} %pad_maximum_fusion.2), channel_id=1, source_target_pairs={{0,8},{1,9},{2,10},{3,11},{4,12},{5,13},{6,14},{7,15},{8,0},{9,1},... | collective-permute-start | bytes 688136 | tf_op jit(solution)/shard_map/ppermute | solution.py:612
  45.2 3.2 %shard_map.135 = (f32[4,32,512]{2,1,0:T(8,128)S(1)}, bf16[10,512,512]{2,1,0:T(8,128)(2,1)S(1)}) custom-call(bf16[16,512,128]{2,1,0:T(8,128)(2,1)S(1)} %get-tuple-element.68.a_ref, bf16[16,512,128]{2,1,0:T(8,128)(2,1)S(1)} %get-tuple-element.69.b_ref, f32[16,32,512]{2,1,0:T(8,128)S(1)} %get-tuple-element.70.r_ref.right), custom_call_target="tpu_custom_call" | custom-call | flops 3795000064 | tf_op jit(solution)/shard_map/pallas_call | solution.py:312
  48.4 3.2 %collective-permute-done.3 = bf16[4,224,128]{2,1,0:T(8,128)(2,1)S(1)} collective-permute-done((bf16[4,224,128]{2,1,0:T(8,128)(2,1)S(1)}, bf16[4,224,128]{2,1,0:T(8,128)(2,1)S(1)}, u32[]{:S(2)}, u32[]{:S(2)}) %collective-permute-start.3) | collective-permute-done | bytes 229408 | tf_op jit(solution)/shard_map/ppermute | solution.py:612
  51.8 1.8 %collective-permute-done.4.eight_b = bf16[8,224,128]{2,1,0:T(8,128)(2,1)S(1)} collective-permute-done((bf16[8,224,128]{2,1,0:T(8,128)(2,1)S(1)}, bf16[8,224,128]{2,1,0:T(8,128)(2,1)S(1)}, u32[]{:S(2)}, u32[]{:S(2)}) %collective-permute-start.4) | collective-permute-done | bytes 458784 | tf_op jit(solution)/shard_map/ppermute | solution.py:612
  53.6 7.5 %shard_map.136 = (f32[16,32,512]{2,1,0:T(8,128)S(1)}, bf16[320,128]{1,0:T(8,128)(2,1)S(1)}, bf16[16,256,256]{2,1,0:T(8,128)(2,1)S(1)}, bf16[4,256,256]{2,1,0:T(8,128)(2,1)S(1)}) custom-call(s32[4,4]{1,0:T(4,128)S(1)} %copy-done.8, s32[4,128]{1,0:T(4,128)S(1)} %bitcast.11, s32[16]{0:T(128)S(1)} %get-tuple-element.52.perm.perm_ref, ...), custom_call_target="tpu_custom_call" | custom-call | flops 9200000000 | tf_op jit(solution)/shard_map/pallas_call | solution.py:417
  61.4 2.0 %shard_map.137.near0 = f32[4,32,512]{2,1,0:T(8,128)S(1)} custom-call(bf16[10,512,512]{2,1,0:T(8,128)(2,1)S(1)} %get-tuple-element.81.tiles_ref, f32[16,32,512]{2,1,0:T(8,128)S(1)} %get-tuple-element.91.q_ref.image), custom_call_target="tpu_custom_call" | custom-call | flops 2990000128 | tf_op jit(solution)/shard_map/pallas_call | solution.py:330
  63.4 2.3 %collective-permute-done.5 = bf16[320,128]{1,0:T(8,128)(2,1)S(1)} collective-permute-done((bf16[320,128]{1,0:T(8,128)(2,1)S(1)}, bf16[320,128]{1,0:T(8,128)(2,1)S(1)}, u32[]{:S(2)}, u32[]{:S(2)}) %collective-permute-start.5) | collective-permute-done | bytes 81952 | tf_op jit(solution)/shard_map/ppermute | solution.py:612
  66.6 2.0 %shard_map.138.near1 = f32[4,32,512]{2,1,0:T(8,128)S(1)} custom-call(bf16[10,512,512]{2,1,0:T(8,128)(2,1)S(1)} %get-tuple-element.84.tiles_ref, f32[16,32,512]{2,1,0:T(8,128)S(1)} %get-tuple-element.91.q_ref.image), custom_call_target="tpu_custom_call" | custom-call | flops 2990000128 | tf_op jit(solution)/shard_map/pallas_call | solution.py:330
  68.5 2.4 %collective-permute-done.7 = bf16[2,64,128]{2,1,0:T(8,128)(2,1)S(1)} collective-permute-done((bf16[2,64,128]{2,1,0:T(8,128)(2,1)S(1)}, bf16[2,64,128]{2,1,0:T(8,128)(2,1)S(1)}, u32[]{:S(2)}, u32[]{:S(2)}) %collective-permute-start.7) | collective-permute-done | bytes 32800 | tf_op jit(solution)/shard_map/ppermute | solution.py:612
  70.9 1.7 %collective-permute-start.8 = (bf16[4,64,128]{2,1,0:T(8,128)(2,1)S(1)}, bf16[4,64,128]{2,1,0:T(8,128)(2,1)S(1)}, u32[]{:S(2)}, u32[]{:S(2)}) collective-permute-start(bf16[4,64,128]{2,1,0:T(8,128)(2,1)S(1)} %pad_maximum_fusion.5), channel_id=1, source_target_pairs={{0,8},{1,9},{2,10},{3,11},{4,12},{5,13},{6,14},{7,15},{8,0},{9,1},... | collective-permute-start | bytes 196616 | tf_op jit(solution)/shard_map/ppermute | solution.py:612
  72.6 2.0 %shard_map.139.near2 = f32[4,32,512]{2,1,0:T(8,128)S(1)} custom-call(bf16[10,512,512]{2,1,0:T(8,128)(2,1)S(1)} %get-tuple-element.87.tiles_ref, f32[16,32,512]{2,1,0:T(8,128)S(1)} %get-tuple-element.91.q_ref.image), custom_call_target="tpu_custom_call" | custom-call | flops 2990000128 | tf_op jit(solution)/shard_map/pallas_call | solution.py:330
  75.6 2.0 %shard_map.140.near3 = f32[4,32,512]{2,1,0:T(8,128)S(1)} custom-call(bf16[10,512,512]{2,1,0:T(8,128)(2,1)S(1)} %get-tuple-element.90.tiles_ref, f32[16,32,512]{2,1,0:T(8,128)S(1)} %get-tuple-element.91.q_ref.image), custom_call_target="tpu_custom_call" | custom-call | flops 2990000128 | tf_op jit(solution)/shard_map/pallas_call | solution.py:330
  77.6 6.5 %shard_map.141 = (f32[16,32,512]{2,1,0:T(8,128)S(1)}, f32[64,96]{1,0:T(8,128)S(1)}) custom-call(s32[4,4]{1,0:T(4,128)S(1)} %copy-done.8, s32[4,128]{1,0:T(4,128)S(1)} %bitcast.12, s32[16]{0:T(128)S(1)} %get-tuple-element.52.perm.perm_ref, bf16[2,320,128]{2,1,0:T(8,128)(2,1)S(1)} %pad_maximum_fusion.3.pair_a, ...), custom_call_target="tpu_custom_call" | custom-call | flops 9200000000 | tf_op jit(solution)/shard_map/pallas_call | solution.py:474
  84.7 0.9 collective-permute-done.10
  85.6 3.1 %shard_map.142.refs_0_ = f32[8192,128]{1,0:T(8,128)S(1)} custom-call(s32[8192]{0:T(1024)S(1)} %copy-done.4, s32[16]{0:T(128)S(1)} %get-tuple-element.52.perm.perm_ref, f32[16,32,512]{2,1,0:T(8,128)S(1)} %get-tuple-element.91.q_ref.image, f32[16,32,512]{2,1,0:T(8,128)S(1)} %get-tuple-element.101.p_ref), custom_call_target="tpu_custom_call" | custom-call | flops 2875000064 | tf_op jit(solution)/shard_map/pallas_call | solution.py:517
  90.2 3.1 %shard_map.143.refs_0_ = f32[8192,128]{1,0:T(8,128)S(1)} custom-call(s32[8192]{0:T(1024)S(1)} %copy-done.4, s32[16]{0:T(128)S(1)} %get-tuple-element.52.perm.perm_ref, f32[16,32,512]{2,1,0:T(8,128)S(1)} %get-tuple-element.91.q_ref.image, f32[16,32,512]{2,1,0:T(8,128)S(1)} %get-tuple-element.101.p_ref, ...), custom_call_target="tpu_custom_call", output_to_operand_aliasing={{}: (4, {})} | custom-call | flops 2875000064 | tf_op jit(solution)/shard_map/pallas_call | solution.py:517
  93.4 1.2 collective-permute-done.12
  94.6 1.6 %collective-permute-start.13 = (f32[64,96]{1,0:T(8,128)S(1)}, f32[64,96]{1,0:T(8,128)S(1)}, u32[]{:S(2)}, u32[]{:S(2)}) collective-permute-start(f32[64,96]{1,0:T(8,128)S(1)} %add.23), channel_id=1, source_target_pairs={{0,8},{1,9},{2,10},{3,11},{4,12},{5,13},{6,14},{7,15},{8,0},{9,1},... | collective-permute-start | bytes 73736 | tf_op jit(solution)/shard_map/ppermute | solution.py:612
  96.2 3.1 %shard_map.144.refs_0_ = f32[8192,128]{1,0:T(8,128)S(1)} custom-call(s32[8192]{0:T(1024)S(1)} %copy-done.4, s32[16]{0:T(128)S(1)} %get-tuple-element.52.perm.perm_ref, f32[16,32,512]{2,1,0:T(8,128)S(1)} %get-tuple-element.91.q_ref.image, f32[16,32,512]{2,1,0:T(8,128)S(1)} %get-tuple-element.101.p_ref, ...), custom_call_target="tpu_custom_call", output_to_operand_aliasing={{}: (4, {})} | custom-call | flops 2875000064 | tf_op jit(solution)/shard_map/pallas_call | solution.py:517
  99.4 2.3 %collective-permute-start.14 = (f32[64,96]{1,0:T(8,128)S(1)}, f32[64,96]{1,0:T(8,128)S(1)}, u32[]{:S(2)}, u32[]{:S(2)}) collective-permute-start(f32[64,96]{1,0:T(8,128)S(1)} %add.24), channel_id=1, source_target_pairs={{0,24},{1,25},{2,26},{3,27},{4,28},{5,29},{6,30},{7,31},{8,16},{9,... | collective-permute-start | bytes 73736 | tf_op jit(solution)/shard_map/ppermute | solution.py:612
  101.6 3.1 %shard_map.145.rows_ref = f32[8192,128]{1,0:T(8,128)S(1)} custom-call(s32[8192]{0:T(1024)S(1)} %copy-done.4, s32[16]{0:T(128)S(1)} %get-tuple-element.52.perm.perm_ref, f32[16,32,512]{2,1,0:T(8,128)S(1)} %get-tuple-element.91.q_ref.image, f32[16,32,512]{2,1,0:T(8,128)S(1)} %get-tuple-element.101.p_ref, ...), custom_call_target="tpu_custom_call", output_to_operand_aliasing={{}: (4, {})} | custom-call | flops 2875000064 | tf_op jit(solution)/shard_map/pallas_call | solution.py:517
  104.8 2.0 %collective-permute-start.15 = (f32[64,96]{1,0:T(8,128)S(1)}, f32[64,96]{1,0:T(8,128)S(1)}, u32[]{:S(2)}, u32[]{:S(2)}) collective-permute-start(f32[64,96]{1,0:T(8,128)S(1)} %add.25), channel_id=1, source_target_pairs={{0,32},{1,33},{2,34},{3,35},{4,36},{5,37},{6,38},{7,39},{8,40},{9,... | collective-permute-start | bytes 73736 | tf_op jit(solution)/shard_map/ppermute | solution.py:612
  107.4 1.4 %collective-permute-done.15 = f32[64,96]{1,0:T(8,128)S(1)} collective-permute-done((f32[64,96]{1,0:T(8,128)S(1)}, f32[64,96]{1,0:T(8,128)S(1)}, u32[]{:S(2)}, u32[]{:S(2)}) %collective-permute-start.15) | collective-permute-done | bytes 24608 | tf_op jit(solution)/shard_map/ppermute | solution.py:612
  108.8 4.1 %collective-permute-start.16 = (f32[64,96]{1,0:T(8,128)S(1)}, f32[64,96]{1,0:T(8,128)S(1)}, u32[]{:S(2)}, u32[]{:S(2)}) collective-permute-start(f32[64,96]{1,0:T(8,128)S(1)} %add.26), channel_id=1, source_target_pairs={{0,96},{1,97},{2,98},{3,99},{4,100},{5,101},{6,102},{7,103},{8,104... | collective-permute-start | bytes 73736 | tf_op jit(solution)/shard_map/ppermute | solution.py:612
  113.5 1.3 %collective-permute-done.16 = f32[64,96]{1,0:T(8,128)S(1)} collective-permute-done((f32[64,96]{1,0:T(8,128)S(1)}, f32[64,96]{1,0:T(8,128)S(1)}, u32[]{:S(2)}, u32[]{:S(2)}) %collective-permute-start.16) | collective-permute-done | bytes 24608 | tf_op jit(solution)/shard_map/ppermute | solution.py:612
  114.8 9.4 %shard_map.148 = (f32[32,8192]{1,0:T(8,128)}, f32[32,8192]{1,0:T(8,128)}) custom-call(f32[64,96]{1,0:T(8,128)S(1)} %add.27.gram, f32[32,8192]{1,0:T(8,128)S(1)} %copy-done, f32[64,4096]{1,0:T(8,128)S(1)} %shard_map.146.mapped0, f32[64,4096]{1,0:T(8,128)S(1)} %shard_map.147.mapped1), custom_call_target="tpu_custom_call" | custom-call | tf_op jit(solution)/shard_map/pallas_call | solution.py:601
  (55 shorter events, 8.2 us)
Async XLA Ops:
  0.6 0.7 copy-start.5
  1.4 0.7 copy-start.6
  2.0 0.7 copy-start.7
  28.3 8.5 %collective-permute-start = (bf16[1120,128]{1,0:T(8,128)(2,1)S(1)}, bf16[1120,128]{1,0:T(8,128)(2,1)S(1)}, u32[]{:S(2)}, u32[]{:S(2)}) collective-permute-start(bf16[1120,128]{1,0:T(8,128)(2,1)S(1)} %get-tuple-element.53), channel_id=1, source_target_pairs={{0,2},{1,3},{2,0},{3,1},{4,6},{5,7},{6,4},{7,5},{8,10},{9,11},{10,... | collective-permute-start | bytes 860168 | tf_op jit(solution)/shard_map/ppermute | solution.py:612
  36.9 6.3 %collective-permute-start.2 = (bf16[2,224,128]{2,1,0:T(8,128)(2,1)S(1)}, bf16[2,224,128]{2,1,0:T(8,128)(2,1)S(1)}, u32[]{:S(2)}, u32[]{:S(2)}) collective-permute-start(bf16[2,224,128]{2,1,0:T(8,128)(2,1)S(1)} %fusion), channel_id=1, source_target_pairs={{0,6},{1,7},{2,4},{3,5},{4,2},{5,3},{6,0},{7,1},{8,14},{9,15},{10,... | collective-permute-start | bytes 344072 | tf_op jit(solution)/shard_map/ppermute | solution.py:612
  40.0 11.8 %collective-permute-start.1 = (bf16[2,1120,128]{2,1,0:T(8,128)(2,1)S(1)}, bf16[2,1120,128]{2,1,0:T(8,128)(2,1)S(1)}, u32[]{:S(2)}, u32[]{:S(2)}) collective-permute-start(bf16[2,1120,128]{2,1,0:T(8,128)(2,1)S(1)} %pad_maximum_fusion.pair_a), channel_id=1, source_target_pairs={{0,1},{1,0},{2,3},{3,2},{4,5},{5,4},{6,7},{7,6},{8,9},{9,8},{10,11... | collective-permute-start | bytes 1720328 | tf_op jit(solution)/shard_map/ppermute | solution.py:612
  43.3 10.3 %copy-start.1 = (bf16[16,256,512]{2,1,0:T(8,128)(2,1)S(1)}, bf16[16,256,512]{2,1,0:T(8,128)(2,1)}, u32[]{:S(2)}) copy-start(bf16[16,256,512]{2,1,0:T(8,128)(2,1)} %leaf_v.3) | copy-start | bytes 12582916
  43.3 10.3 %copy-start.2 = (bf16[4,256,1024]{2,1,0:T(8,128)(2,1)S(1)}, bf16[4,256,1024]{2,1,0:T(8,128)(2,1)}, u32[]{:S(2)}) copy-start(bf16[4,256,1024]{2,1,0:T(8,128)(2,1)} %mid_v.3) | copy-start | bytes 6291460
  43.3 10.3 %copy-start.3 = (bf16[4,256,256]{2,1,0:T(8,128)(2,1)S(1)}, bf16[4,256,256]{2,1,0:T(8,128)(2,1)}, u32[]{:S(2)}) copy-start(bf16[4,256,256]{2,1,0:T(8,128)(2,1)} %top_v.3) | copy-start | bytes 1572868
  43.3 10.3 %copy-start.8 = (s32[4,4]{1,0:T(4,128)S(1)}, s32[4,4]{1,0:T(4,128)}, u32[]{:S(2)}) copy-start(s32[4,4]{1,0:T(4,128)} %far_mid.3) | copy-start | bytes 196
  43.3 10.3 %copy-start.9 = (s32[128,4]{0,1:T(4,128)S(1)}, s32[128,4]{0,1:T(4,128)}, u32[]{:S(2)}) copy-start(s32[128,4]{0,1:T(4,128)} %param.20) | copy-start | bytes 6148
  43.3 8.3 %collective-permute-start.3 = (bf16[4,224,128]{2,1,0:T(8,128)(2,1)S(1)}, bf16[4,224,128]{2,1,0:T(8,128)(2,1)S(1)}, u32[]{:S(2)}, u32[]{:S(2)}) collective-permute-start(bf16[4,224,128]{2,1,0:T(8,128)(2,1)S(1)} %pad_maximum_fusion.2), channel_id=1, source_target_pairs={{0,8},{1,9},{2,10},{3,11},{4,12},{5,13},{6,14},{7,15},{8,0},{9,1},... | collective-permute-start | bytes 688136 | tf_op jit(solution)/shard_map/ppermute | solution.py:612
  51.7 1.9 %collective-permute-start.4 = (bf16[8,224,128]{2,1,0:T(8,128)(2,1)S(1)}, bf16[8,224,128]{2,1,0:T(8,128)(2,1)S(1)}, u32[]{:S(2)}, u32[]{:S(2)}) collective-permute-start(bf16[8,224,128]{2,1,0:T(8,128)(2,1)S(1)} %pad_maximum_fusion.1.eight_a), channel_id=1, source_target_pairs={{0,1},{1,0},{2,3},{3,2},{4,5},{5,4},{6,7},{7,6},{8,9},{9,8},{10,11... | collective-permute-start | bytes 1376264 | tf_op jit(solution)/shard_map/ppermute | solution.py:612
  61.1 4.6 %collective-permute-start.5 = (bf16[320,128]{1,0:T(8,128)(2,1)S(1)}, bf16[320,128]{1,0:T(8,128)(2,1)S(1)}, u32[]{:S(2)}, u32[]{:S(2)}) collective-permute-start(bf16[320,128]{1,0:T(8,128)(2,1)S(1)} %get-tuple-element.80), channel_id=1, source_target_pairs={{0,2},{1,3},{2,0},{3,1},{4,6},{5,7},{6,4},{7,5},{8,10},{9,11},{10,... | collective-permute-start | bytes 245768 | tf_op jit(solution)/shard_map/ppermute | solution.py:612
  65.7 5.2 %collective-permute-start.7 = (bf16[2,64,128]{2,1,0:T(8,128)(2,1)S(1)}, bf16[2,64,128]{2,1,0:T(8,128)(2,1)S(1)}, u32[]{:S(2)}, u32[]{:S(2)}) collective-permute-start(bf16[2,64,128]{2,1,0:T(8,128)(2,1)S(1)} %fusion.1), channel_id=1, source_target_pairs={{0,6},{1,7},{2,4},{3,5},{4,2},{5,3},{6,0},{7,1},{8,14},{9,15},{10,... | collective-permute-start | bytes 98312 | tf_op jit(solution)/shard_map/ppermute | solution.py:612
  66.6 11.0 %collective-permute-start.6 = (bf16[2,320,128]{2,1,0:T(8,128)(2,1)S(1)}, bf16[2,320,128]{2,1,0:T(8,128)(2,1)S(1)}, u32[]{:S(2)}, u32[]{:S(2)}) collective-permute-start(bf16[2,320,128]{2,1,0:T(8,128)(2,1)S(1)} %pad_maximum_fusion.3.pair_a), channel_id=1, source_target_pairs={{0,1},{1,0},{2,3},{3,2},{4,5},{5,4},{6,7},{7,6},{8,9},{9,8},{10,11... | collective-permute-start | bytes 491528 | tf_op jit(solution)/shard_map/ppermute | solution.py:612
  70.9 4.3 %collective-permute-start.8 = (bf16[4,64,128]{2,1,0:T(8,128)(2,1)S(1)}, bf16[4,64,128]{2,1,0:T(8,128)(2,1)S(1)}, u32[]{:S(2)}, u32[]{:S(2)}) collective-permute-start(bf16[4,64,128]{2,1,0:T(8,128)(2,1)S(1)} %pad_maximum_fusion.5), channel_id=1, source_target_pairs={{0,8},{1,9},{2,10},{3,11},{4,12},{5,13},{6,14},{7,15},{8,0},{9,1},... | collective-permute-start | bytes 196616 | tf_op jit(solution)/shard_map/ppermute | solution.py:612
  75.3 2.3 %collective-permute-start.9 = (bf16[8,64,128]{2,1,0:T(8,128)(2,1)S(1)}, bf16[8,64,128]{2,1,0:T(8,128)(2,1)S(1)}, u32[]{:S(2)}, u32[]{:S(2)}) collective-permute-start(bf16[8,64,128]{2,1,0:T(8,128)(2,1)S(1)} %pad_maximum_fusion.4.eight_a), channel_id=1, source_target_pairs={{0,1},{1,0},{2,3},{3,2},{4,5},{5,4},{6,7},{7,6},{8,9},{9,8},{10,11... | collective-permute-start | bytes 393224 | tf_op jit(solution)/shard_map/ppermute | solution.py:612
  77.6 8.0 %copy-start.4 = (s32[8192]{0:T(1024)S(1)}, s32[8192]{0:T(1024)}, u32[]{:S(2)}) copy-start(s32[8192]{0:T(1024)} %order_ref.7) | copy-start | bytes 98308
  84.1 1.4 %collective-permute-start.10 = (f32[64,96]{1,0:T(8,128)S(1)}, f32[64,96]{1,0:T(8,128)S(1)}, u32[]{:S(2)}, u32[]{:S(2)}) collective-permute-start(f32[64,96]{1,0:T(8,128)S(1)} %get-tuple-element.100), channel_id=1, source_target_pairs={{0,1},{1,0},{2,3},{3,2},{4,5},{5,4},{6,7},{7,6},{8,9},{9,8},{10,11... | collective-permute-start | bytes 73736 | tf_op jit(solution)/shard_map/ppermute | solution.py:612
  85.6 3.9 %collective-permute-start.11 = (f32[64,96]{1,0:T(8,128)S(1)}, f32[64,96]{1,0:T(8,128)S(1)}, u32[]{:S(2)}, u32[]{:S(2)}) collective-permute-start(f32[64,96]{1,0:T(8,128)S(1)} %add.21), channel_id=1, source_target_pairs={{0,2},{1,3},{2,0},{3,1},{4,6},{5,7},{6,4},{7,5},{8,10},{9,11},{10,... | collective-permute-start | bytes 73736 | tf_op jit(solution)/shard_map/ppermute | solution.py:612
  89.5 5.1 %collective-permute-start.12 = (f32[64,96]{1,0:T(8,128)S(1)}, f32[64,96]{1,0:T(8,128)S(1)}, u32[]{:S(2)}, u32[]{:S(2)}) collective-permute-start(f32[64,96]{1,0:T(8,128)S(1)} %add.22), channel_id=1, source_target_pairs={{0,6},{1,7},{2,4},{3,5},{4,2},{5,3},{6,0},{7,1},{8,14},{9,15},{10,... | collective-permute-start | bytes 73736 | tf_op jit(solution)/shard_map/ppermute | solution.py:612
  94.6 4.7 %collective-permute-start.13 = (f32[64,96]{1,0:T(8,128)S(1)}, f32[64,96]{1,0:T(8,128)S(1)}, u32[]{:S(2)}, u32[]{:S(2)}) collective-permute-start(f32[64,96]{1,0:T(8,128)S(1)} %add.23), channel_id=1, source_target_pairs={{0,8},{1,9},{2,10},{3,11},{4,12},{5,13},{6,14},{7,15},{8,0},{9,1},... | collective-permute-start | bytes 73736 | tf_op jit(solution)/shard_map/ppermute | solution.py:612
  99.4 5.4 %collective-permute-start.14 = (f32[64,96]{1,0:T(8,128)S(1)}, f32[64,96]{1,0:T(8,128)S(1)}, u32[]{:S(2)}, u32[]{:S(2)}) collective-permute-start(f32[64,96]{1,0:T(8,128)S(1)} %add.24), channel_id=1, source_target_pairs={{0,24},{1,25},{2,26},{3,27},{4,28},{5,29},{6,30},{7,31},{8,16},{9,... | collective-permute-start | bytes 73736 | tf_op jit(solution)/shard_map/ppermute | solution.py:612
  104.8 4.0 %collective-permute-start.15 = (f32[64,96]{1,0:T(8,128)S(1)}, f32[64,96]{1,0:T(8,128)S(1)}, u32[]{:S(2)}, u32[]{:S(2)}) collective-permute-start(f32[64,96]{1,0:T(8,128)S(1)} %add.25), channel_id=1, source_target_pairs={{0,32},{1,33},{2,34},{3,35},{4,36},{5,37},{6,38},{7,39},{8,40},{9,... | collective-permute-start | bytes 73736 | tf_op jit(solution)/shard_map/ppermute | solution.py:612
  108.8 6.0 %copy-start = (f32[32,8192]{1,0:T(8,128)S(1)}, f32[32,8192]{1,0:T(8,128)}, u32[]{:S(2)}) copy-start(f32[32,8192]{1,0:T(8,128)} %rhs.1) | copy-start | bytes 3145732
  108.8 6.0 %collective-permute-start.16 = (f32[64,96]{1,0:T(8,128)S(1)}, f32[64,96]{1,0:T(8,128)S(1)}, u32[]{:S(2)}, u32[]{:S(2)}) collective-permute-start(f32[64,96]{1,0:T(8,128)S(1)} %add.26), channel_id=1, source_target_pairs={{0,96},{1,97},{2,98},{3,99},{4,100},{5,101},{6,102},{7,103},{8,104... | collective-permute-start | bytes 73736 | tf_op jit(solution)/shard_map/ppermute | solution.py:612

commit v2 on v1

--- a/solution.py
+++ b/solution.py
@@ -37,6 +37,7 @@
 S1_ROWS = MID * S_ROWS
 PAY2_ROWS = S1_ROWS + S_ROWS
 GROUPS = LEAVES // LIST
+SKEL_MID_AT = LEAVES * RANK
 PAIRS = [(p, q) for p in range(LIST) for q in range(p, LIST)]
 
 VM = pl.BlockSpec(memory_space=pltpu.VMEM)
@@ -138,9 +139,9 @@
 
 
 def setup_kernel(
-    leaf_skel, skel_mid, near, order_hbm, skel_top_hbm, points_hbm, rhs_hbm, leaf_hbm, mid_hbm, top_hbm,
+    leaf_skel_hbm, skel_mid_hbm, near_hbm, order_hbm, skel_top_hbm, points_hbm, rhs_hbm, leaf_hbm, mid_hbm, top_hbm,
     a_out, b_out, r_out, pay, perm,
-    order, skel_top, points, rhs, rows, tree, skel, leaf_v, mid_v, top_v, s0, sources, sems,
+    lists, near, order, skel_top, points, rhs, rows, tree, skel, leaf_v, mid_v, top_v, s0, sources, sems,
 ):
     device = this_device()
     eight = pl.multiple_of(device // 8 * 8, 8)
@@ -161,21 +162,14 @@
         pltpu.make_async_copy(mid_hbm, mid_v, sems.at[11]),
         pltpu.make_async_copy(top_hbm, top_v, sems.at[12]),
     ]
-    for copy in small + sum(chunks, []) + large:
+    small.append(pltpu.make_async_copy(near_hbm, near, sems.at[13]))
+    for i in range(LEAVES):
+        small.append(pltpu.make_async_copy(leaf_skel_hbm.at[i], lists.at[pl.ds(i * RANK, RANK)], sems.at[14 + i]))
+    for i in range(MID):
+        part = lists.at[pl.ds(SKEL_MID_AT + i * RANK, RANK)]
+        small.append(pltpu.make_async_copy(skel_mid_hbm.at[i], part, sems.at[14 + LEAVES + i]))
+    for copy in sum(chunks, []) + small:
         copy.start()
-
-    count = jnp.int32(0)
-    for leaf in range(LEAVES):
-        members = [near[m, leaf] & (LEAVES - 1) for m in range(LIST)]
-        first = jnp.minimum(jnp.minimum(members[0], members[1]), jnp.minimum(members[2], members[3]))
-        leads = first == leaf
-
-        @pl.when(leads)
-        def _(members=members, count=count):
-            for m in range(LIST):
-                perm[count * LIST + m] = members[m]
-
-        count = count + leads.astype(jnp.int32)
 
     def turn(step, _):
         at = pl.multiple_of(step * LEAF, LEAF)
@@ -194,25 +188,38 @@
         for copy in chunks[i]:
             copy.wait()
         lax.fori_loop(4 * i, 4 * i + 4, turn, 0)
+    for copy in large:
+        copy.start()
     for copy in small:
         copy.wait()
 
-    unroll = 16
-
-    for node in range(MID):
-        def pick_mid(step, _, node=node):
-            base = step * unroll
-            spots = [skel_mid[node, base + u] for u in range(unroll)]
-            leaves = [4 * node + (at >> 8) for at in spots]
-            inner = [leaf_skel[leaf, at & (RANK - 1)] for leaf, at in zip(leaves, spots)]
-            found = [order[leaf * LEAF + at] for leaf, at in zip(leaves, inner)]
-            for u in range(unroll):
-                skel[pl.ds(node * RANK + base + u, 1), :] = rows[pl.ds(found[u], 1), :]
-            for u in range(unroll):
-                sources[node * RANK + base + u] = found[u]
-            return 0
-
-        lax.fori_loop(0, RANK // unroll, pick_mid, 0)
+    count = jnp.int32(0)
+    for leaf in range(LEAVES):
+        members = [near[m, leaf] & (LEAVES - 1) for m in range(LIST)]
+        first = jnp.minimum(jnp.minimum(members[0], members[1]), jnp.minimum(members[2], members[3]))
+        leads = first == leaf
+
+        @pl.when(leads)
+        def _(members=members, count=count):
+            for m in range(LIST):
+                perm[count * LIST + m] = members[m]
+
+        count = count + leads.astype(jnp.int32)
+
+    unroll = 32
+
+    def pick_mid(step, _):
+        base = step * unroll
+        first = (base >> 8) * (4 * RANK)
+        spots = [first + lists[SKEL_MID_AT + base + u] for u in range(unroll)]
+        found = [order[((at >> 8) << 9) + lists[at]] for at in spots]
+        for u in range(unroll):
+            skel[pl.ds(base + u, 1), :] = rows[pl.ds(found[u], 1), :]
+        for u in range(unroll):
+            sources[base + u] = found[u]
+        return 0
+
+    lax.fori_loop(0, MID * RANK // unroll, pick_mid, 0)
 
     own = device & 7
 
@@ -228,6 +235,7 @@
     for node in range(MID + 1):
         pack_points(pay, MID_ROWS if node == MID else node * C_ROWS, skel[node * RANK : (node + 1) * RANK, :])
 
+
     for copy in large:
         copy.wait()
 
@@ -238,8 +246,7 @@
         def pick(step, _):
             at = step * 64
             for u in range(64):
-                source = order[base + at + u]
-                tree[pl.ds(at + u, 1), :] = rows[pl.ds(source, 1), :]
+                tree[pl.ds(at + u, 1), :] = rows[pl.ds(order[base + at + u], 1), :]
             return 0
 
         lax.fori_loop(0, LEAF // 64, pick, 0)
@@ -264,7 +271,9 @@
 
 
 def setup(leaf_skel, skel_mid, near, order, skel_top, points, rhs, interps):
-    order, skel_top, points, rhs, *interps = in_hbm(order, skel_top, points, rhs, *interps)
+    leaf_skel, skel_mid, near, order, skel_top, points, rhs, *interps = in_hbm(
+        leaf_skel, skel_mid, near, order, skel_top, points, rhs, *interps
+    )
     return pl.pallas_call(
         setup_kernel,
         out_shape=[
@@ -274,9 +283,11 @@
             jax.ShapeDtypeStruct((PAY_ROWS, LANES), bf16),
             jax.ShapeDtypeStruct((LEAVES,), jnp.int32),
         ],
-        in_specs=[SM] * 3 + [HBM] * 7,
+        in_specs=[HBM] * 10,
         out_specs=[VM] * 4 + [SM],
         scratch_shapes=[
+            pltpu.SMEM(((LEAVES + MID) * RANK,), jnp.int32),
+            pltpu.SMEM((LIST, LEAVES), jnp.int32),
             pltpu.SMEM((SPAN,), jnp.int32),
             pltpu.SMEM((8, RANK), jnp.int32),
             pltpu.VMEM((DIM, SPAN), bf16),
@@ -287,7 +298,7 @@
             *interp_scratch(),
             pltpu.VMEM((LEAVES, SIDES, RANK), bf16),
             pltpu.SMEM((MID * RANK,), jnp.int32),
-            pltpu.SemaphoreType.DMA((13,)),
+            pltpu.SemaphoreType.DMA((14 + LEAVES + MID,)),
         ],
         compiler_params=params(32),
         cost_estimate=lasting(20),
@@ -558,17 +569,19 @@
     return [values for _, values in systems]
 
 
-def finish_kernel(gram, rhs, mapped0, mapped1, x_out, r_out):
+def finish_kernel(gram, rhs, mapped0, mapped1, x_hbm, r_hbm, x_out, r_out, sems):
     n = SIDES
     rr, rq, rp = gram[0:n, 0:n], gram[0:n, n : 2 * n], gram[0:n, 2 * n : 3 * n]
     qr, qq, qp = gram[n : 2 * n, 0:n], gram[n : 2 * n, n : 2 * n], gram[n : 2 * n, 2 * n : 3 * n]
     eye = (lax.broadcasted_iota(jnp.int32, (n, n), 0) == lax.broadcasted_iota(jnp.int32, (n, n), 1)).astype(f32)
     alpha, rr_inverse = eliminate([(0.5 * (rq + qr), rr), (rr, eye)])
-    rq_alpha = dot(rq, alpha)
-    rho = rr - rq_alpha - dot(alpha, qr, (0, 0)) + dot(alpha, dot(qq, alpha), (0, 0))
+    by_alpha = dot(jnp.concatenate([rq, qq, rp, qp], axis=0), alpha)
+    rho = rr - by_alpha[:n] + dot(alpha, by_alpha[n : 2 * n] - qr, (0, 0))
     first = eye + dot(rr_inverse, rho)
-    half = dot(first, dot(rq, first) - dot(rp, alpha), (0, 0)) - dot(alpha, dot(qq, first) - dot(qp, alpha), (0, 0))
-    turned = dot(half, eye, (0, 0))
+    by_first = dot(jnp.concatenate([rq, qq], axis=0), first)
+    upper, lower = by_first[:n] - by_alpha[2 * n : 3 * n], by_first[n:] - by_alpha[3 * n :]
+    half = dot(first, upper, (0, 0)) - dot(alpha, lower, (0, 0))
+    turned = dot(upper, first, (0, 0)) - dot(lower, alpha, (0, 0))
     (beta,) = eliminate([(0.5 * (half + turned), rho)])
     c0 = alpha + dot(first, beta)
     c1 = -dot(alpha, beta)
@@ -585,6 +598,7 @@
     both = jnp.where(upper, high.astype(f32), low.astype(f32)).astype(bf16)
     both = jnp.concatenate([both, both], axis=1)
 
+    copies = []
     for i in range(LEAVES):
         span = slice(i * LEAF, (i + 1) * LEAF)
         part = (mapped0, mapped1)[i * LEAF // PART]
@@ -595,6 +609,13 @@
         result = result[: 2 * n] + result[2 * n :]
         x_out[:, span] = result[:n]
         r_out[:, span] = right + result[n:]
+        if i % 4 == 3:
+            done = slice((i - 3) * LEAF, (i + 1) * LEAF)
+            for which, (source, target) in enumerate(((x_out, x_hbm), (r_out, r_hbm))):
+                copies.append(pltpu.make_async_copy(source.at[:, done], target.at[:, done], sems.at[which, i // 4]))
+                copies[-1].start()
+    for copy in copies:
+        copy.wait()
 
 
 def finish(gram, rhs, mapped):
@@ -602,7 +623,8 @@
         finish_kernel,
         out_shape=[jax.ShapeDtypeStruct((SIDES, SPAN), f32)] * 2,
         in_specs=[VM] * 4,
-        out_specs=[VM] * 2,
+        out_specs=[HBM] * 2,
+        scratch_shapes=[pltpu.VMEM((SIDES, SPAN), f32)] * 2 + [pltpu.SemaphoreType.DMA((2, 4))],
         compiler_params=params(24),
     )(gram, rhs, *mapped)
 

time: 124 us -> 117 us (0.944)
  Pallas kernels: 83.6 us -> 77.7 us
  local copies, waits for them, and re-layouts: 2.12 us -> 0.04 us
    pallas_call x1, Pallas kernels: 25.6 us -> 20.3 us  [setup(): pl.pallas_call(setup_kernel, out_shape=[jax.ShapeDtypeStruct((LEAVES, LEA...]
    unnamed x20 -> x14, local copies, waits for them, and re-layouts: 2.12 us -> 0.04 us
  transfers between devices with their start and end apart: 17 -> 17, of which waited for: 11 -> 11; matrix products, arithmetic and copies ran while one was open for 0% -> 0% of each run, Pallas kernels for 28% -> 30%
where the time goes in v2:
time: 117 us; the launch traced here: 116 us
  Pallas kernels  77.7 us (66%)
  starting transfers between devices  21 us (18%)
  waiting for transfers between devices  16.4 us (14%)
    ppermute x17, starting transfers between devices, swapped(): lax.ppermute(value, AXES, [(source, source ^ mask) for source in range(co...  21 us
    pallas_call x1, Pallas kernels, setup(): pl.pallas_call(setup_kernel, out_shape=[jax.ShapeDtypeStruct((LEAVES, LEA...  20.3 us
    ppermute x17, waiting for transfers between devices, swapped(): lax.ppermute(value, AXES, [(source, source ^ mask) for source in range(co...  16.4 us
    pallas_call x4, Pallas kernels, near_first(): pl.pallas_call(kernel, out_shape=[jax.ShapeDtypeStruct((LIST, SIDES, LEAF...  12.9 us
    pallas_call x4, Pallas kernels, put_back(): pl.pallas_call(kernel, out_shape=jax.ShapeDtypeStruct((SPAN, LANES), f32)...  12.6 us
    pallas_call x1, Pallas kernels, finish(): pl.pallas_call(finish_kernel, out_shape=[jax.ShapeDtypeStruct((SIDES, SPA...  8.74 us
    pallas_call x4, Pallas kernels, near_second(): pl.pallas_call(kernel, out_shape=jax.ShapeDtypeStruct((LIST, SIDES, LEAF)...  7.83 us
    pallas_call x1, Pallas kernels, far_first(): pl.pallas_call(far_first_kernel, out_shape=[jax.ShapeDtypeStruct((LEAVES,...  7.55 us
  transfers between devices with their start and end apart: 17, of which 11 were waited for; matrix products, arithmetic and copies ran while one was open for 0% of the time, Pallas kernels for 30%

profile of v2, /device:TPU:0, one launch (start us, length us, event | category | flops | bytes accessed | tf_op | source)
XLA Modules:
  0.0 116.4 jit_solution(3702098930366904521)
XLA Ops:
  0.6 20.3 %shard_map.131 = (bf16[16,512,128]{2,1,0:T(8,128)(2,1)S(1)}, bf16[16,512,128]{2,1,0:T(8,128)(2,1)S(1)}, f32[16,32,512]{2,1,0:T(8,128)S(1)}, bf16[1120,128]{1,0:T(8,128)(2,1)S(1)}, s32[16]{0:T(128)S(1)}) custom-call(s32[16,256]{1,0:T(8,128)} %leaf_skel_hbm.1, s32[4,256]{1,0:T(4,128)} %skel_mid_hbm.1, s32[4,16]{1,0:T(4,128)} %bitcast.16, s32[8192]{0:T(1024)} %order_ref.7, ...), custom_call_target="tpu_custom_call" | custom-call | flops 23000000512 | tf_op jit(solution)/shard_map/pallas_call | solution.py:277
  21.0 1.7 %collective-permute-start = (bf16[1120,128]{1,0:T(8,128)(2,1)S(1)}, bf16[1120,128]{1,0:T(8,128)(2,1)S(1)}, u32[]{:S(2)}, u32[]{:S(2)}) collective-permute-start(bf16[1120,128]{1,0:T(8,128)(2,1)S(1)} %get-tuple-element.53), channel_id=1, source_target_pairs={{0,2},{1,3},{2,0},{3,1},{4,6},{5,7},{6,4},{7,5},{8,10},{9,11},{10,... | collective-permute-start | bytes 860168 | tf_op jit(solution)/shard_map/ppermute | solution.py:634
  22.6 3.2 %shard_map.133 = (f32[4,32,512]{2,1,0:T(8,128)S(1)}, bf16[10,512,512]{2,1,0:T(8,128)(2,1)S(1)}) custom-call(bf16[16,512,128]{2,1,0:T(8,128)(2,1)S(1)} %get-tuple-element.68.a_ref, bf16[16,512,128]{2,1,0:T(8,128)(2,1)S(1)} %get-tuple-element.69.b_ref, f32[16,32,512]{2,1,0:T(8,128)S(1)} %get-tuple-element.70.r_ref.right), custom_call_target="tpu_custom_call" | custom-call | flops 3795000064 | tf_op jit(solution)/shard_map/pallas_call | solution.py:323
  25.9 3.2 %shard_map.132 = (f32[4,32,512]{2,1,0:T(8,128)S(1)}, bf16[10,512,512]{2,1,0:T(8,128)(2,1)S(1)}) custom-call(bf16[16,512,128]{2,1,0:T(8,128)(2,1)S(1)} %get-tuple-element.68.a_ref, bf16[16,512,128]{2,1,0:T(8,128)(2,1)S(1)} %get-tuple-element.69.b_ref, f32[16,32,512]{2,1,0:T(8,128)S(1)} %get-tuple-element.70.r_ref.right), custom_call_target="tpu_custom_call" | custom-call | flops 3795000064 | tf_op jit(solution)/shard_map/pallas_call | solution.py:323
  29.6 3.1 %collective-permute-start.2 = (bf16[2,224,128]{2,1,0:T(8,128)(2,1)S(1)}, bf16[2,224,128]{2,1,0:T(8,128)(2,1)S(1)}, u32[]{:S(2)}, u32[]{:S(2)}) collective-permute-start(bf16[2,224,128]{2,1,0:T(8,128)(2,1)S(1)} %fusion), channel_id=1, source_target_pairs={{0,6},{1,7},{2,4},{3,5},{4,2},{5,3},{6,0},{7,1},{8,14},{9,15},{10,... | collective-permute-start | bytes 344072 | tf_op jit(solution)/shard_map/ppermute | solution.py:634
  32.6 3.2 %shard_map.134 = (f32[4,32,512]{2,1,0:T(8,128)S(1)}, bf16[10,512,512]{2,1,0:T(8,128)(2,1)S(1)}) custom-call(bf16[16,512,128]{2,1,0:T(8,128)(2,1)S(1)} %get-tuple-element.68.a_ref, bf16[16,512,128]{2,1,0:T(8,128)(2,1)S(1)} %get-tuple-element.69.b_ref, f32[16,32,512]{2,1,0:T(8,128)S(1)} %get-tuple-element.70.r_ref.right), custom_call_target="tpu_custom_call" | custom-call | flops 3795000064 | tf_op jit(solution)/shard_map/pallas_call | solution.py:323
  36.0 1.8 %collective-permute-start.3 = (bf16[4,224,128]{2,1,0:T(8,128)(2,1)S(1)}, bf16[4,224,128]{2,1,0:T(8,128)(2,1)S(1)}, u32[]{:S(2)}, u32[]{:S(2)}) collective-permute-start(bf16[4,224,128]{2,1,0:T(8,128)(2,1)S(1)} %pad_maximum_fusion.2), channel_id=1, source_target_pairs={{0,8},{1,9},{2,10},{3,11},{4,12},{5,13},{6,14},{7,15},{8,0},{9,1},... | collective-permute-start | bytes 688136 | tf_op jit(solution)/shard_map/ppermute | solution.py:634
  37.8 3.2 %shard_map.135 = (f32[4,32,512]{2,1,0:T(8,128)S(1)}, bf16[10,512,512]{2,1,0:T(8,128)(2,1)S(1)}) custom-call(bf16[16,512,128]{2,1,0:T(8,128)(2,1)S(1)} %get-tuple-element.68.a_ref, bf16[16,512,128]{2,1,0:T(8,128)(2,1)S(1)} %get-tuple-element.69.b_ref, f32[16,32,512]{2,1,0:T(8,128)S(1)} %get-tuple-element.70.r_ref.right), custom_call_target="tpu_custom_call" | custom-call | flops 3795000064 | tf_op jit(solution)/shard_map/pallas_call | solution.py:323
  41.1 3.2 %collective-permute-done.3 = bf16[4,224,128]{2,1,0:T(8,128)(2,1)S(1)} collective-permute-done((bf16[4,224,128]{2,1,0:T(8,128)(2,1)S(1)}, bf16[4,224,128]{2,1,0:T(8,128)(2,1)S(1)}, u32[]{:S(2)}, u32[]{:S(2)}) %collective-permute-start.3) | collective-permute-done | bytes 229408 | tf_op jit(solution)/shard_map/ppermute | solution.py:634
  44.4 1.8 %collective-permute-done.4.eight_b = bf16[8,224,128]{2,1,0:T(8,128)(2,1)S(1)} collective-permute-done((bf16[8,224,128]{2,1,0:T(8,128)(2,1)S(1)}, bf16[8,224,128]{2,1,0:T(8,128)(2,1)S(1)}, u32[]{:S(2)}, u32[]{:S(2)}) %collective-permute-start.4) | collective-permute-done | bytes 458784 | tf_op jit(solution)/shard_map/ppermute | solution.py:634
  46.2 7.6 %shard_map.136 = (f32[16,32,512]{2,1,0:T(8,128)S(1)}, bf16[320,128]{1,0:T(8,128)(2,1)S(1)}, bf16[16,256,256]{2,1,0:T(8,128)(2,1)S(1)}, bf16[4,256,256]{2,1,0:T(8,128)(2,1)S(1)}) custom-call(s32[4,4]{1,0:T(4,128)S(1)} %copy-done.5, s32[4,128]{1,0:T(4,128)S(1)} %bitcast.10, s32[16]{0:T(128)S(1)} %get-tuple-element.52.perm.perm_ref, ...), custom_call_target="tpu_custom_call" | custom-call | flops 9200000000 | tf_op jit(solution)/shard_map/pallas_call | solution.py:428
  54.1 2.0 %shard_map.137.near0 = f32[4,32,512]{2,1,0:T(8,128)S(1)} custom-call(bf16[10,512,512]{2,1,0:T(8,128)(2,1)S(1)} %get-tuple-element.81.tiles_ref, f32[16,32,512]{2,1,0:T(8,128)S(1)} %get-tuple-element.91.q_ref.image), custom_call_target="tpu_custom_call" | custom-call | flops 2990000128 | tf_op jit(solution)/shard_map/pallas_call | solution.py:341
  56.1 2.3 %collective-permute-done.5 = bf16[320,128]{1,0:T(8,128)(2,1)S(1)} collective-permute-done((bf16[320,128]{1,0:T(8,128)(2,1)S(1)}, bf16[320,128]{1,0:T(8,128)(2,1)S(1)}, u32[]{:S(2)}, u32[]{:S(2)}) %collective-permute-start.5) | collective-permute-done | bytes 81952 | tf_op jit(solution)/shard_map/ppermute | solution.py:634
  59.2 2.0 %shard_map.138.near1 = f32[4,32,512]{2,1,0:T(8,128)S(1)} custom-call(bf16[10,512,512]{2,1,0:T(8,128)(2,1)S(1)} %get-tuple-element.84.tiles_ref, f32[16,32,512]{2,1,0:T(8,128)S(1)} %get-tuple-element.91.q_ref.image), custom_call_target="tpu_custom_call" | custom-call | flops 2990000128 | tf_op jit(solution)/shard_map/pallas_call | solution.py:341
  61.2 2.4 %collective-permute-done.7 = bf16[2,64,128]{2,1,0:T(8,128)(2,1)S(1)} collective-permute-done((bf16[2,64,128]{2,1,0:T(8,128)(2,1)S(1)}, bf16[2,64,128]{2,1,0:T(8,128)(2,1)S(1)}, u32[]{:S(2)}, u32[]{:S(2)}) %collective-permute-start.7) | collective-permute-done | bytes 32800 | tf_op jit(solution)/shard_map/ppermute | solution.py:634
  63.6 1.7 %collective-permute-start.8 = (bf16[4,64,128]{2,1,0:T(8,128)(2,1)S(1)}, bf16[4,64,128]{2,1,0:T(8,128)(2,1)S(1)}, u32[]{:S(2)}, u32[]{:S(2)}) collective-permute-start(bf16[4,64,128]{2,1,0:T(8,128)(2,1)S(1)} %pad_maximum_fusion.5), channel_id=1, source_target_pairs={{0,8},{1,9},{2,10},{3,11},{4,12},{5,13},{6,14},{7,15},{8,0},{9,1},... | collective-permute-start | bytes 196616 | tf_op jit(solution)/shard_map/ppermute | solution.py:634
  65.3 2.0 %shard_map.139.near2 = f32[4,32,512]{2,1,0:T(8,128)S(1)} custom-call(bf16[10,512,512]{2,1,0:T(8,128)(2,1)S(1)} %get-tuple-element.87.tiles_ref, f32[16,32,512]{2,1,0:T(8,128)S(1)} %get-tuple-element.91.q_ref.image), custom_call_target="tpu_custom_call" | custom-call | flops 2990000128 | tf_op jit(solution)/shard_map/pallas_call | solution.py:341
  68.3 2.0 %shard_map.140.near3 = f32[4,32,512]{2,1,0:T(8,128)S(1)} custom-call(bf16[10,512,512]{2,1,0:T(8,128)(2,1)S(1)} %get-tuple-element.90.tiles_ref, f32[16,32,512]{2,1,0:T(8,128)S(1)} %get-tuple-element.91.q_ref.image), custom_call_target="tpu_custom_call" | custom-call | flops 2990000128 | tf_op jit(solution)/shard_map/pallas_call | solution.py:341
  70.3 6.5 %shard_map.141 = (f32[16,32,512]{2,1,0:T(8,128)S(1)}, f32[64,96]{1,0:T(8,128)S(1)}) custom-call(s32[4,4]{1,0:T(4,128)S(1)} %copy-done.5, s32[4,128]{1,0:T(4,128)S(1)} %bitcast.11, s32[16]{0:T(128)S(1)} %get-tuple-element.52.perm.perm_ref, bf16[2,320,128]{2,1,0:T(8,128)(2,1)S(1)} %pad_maximum_fusion.3.pair_a, ...), custom_call_target="tpu_custom_call" | custom-call | flops 9200000000 | tf_op jit(solution)/shard_map/pallas_call | solution.py:485
  77.4 0.9 collective-permute-done.10
  78.2 3.1 %shard_map.142.refs_0_ = f32[8192,128]{1,0:T(8,128)S(1)} custom-call(s32[8192]{0:T(1024)S(1)} %copy-done.4, s32[16]{0:T(128)S(1)} %get-tuple-element.52.perm.perm_ref, f32[16,32,512]{2,1,0:T(8,128)S(1)} %get-tuple-element.91.q_ref.image, f32[16,32,512]{2,1,0:T(8,128)S(1)} %get-tuple-element.101.p_ref), custom_call_target="tpu_custom_call" | custom-call | flops 2875000064 | tf_op jit(solution)/shard_map/pallas_call | solution.py:528
  82.9 3.1 %shard_map.143.refs_0_ = f32[8192,128]{1,0:T(8,128)S(1)} custom-call(s32[8192]{0:T(1024)S(1)} %copy-done.4, s32[16]{0:T(128)S(1)} %get-tuple-element.52.perm.perm_ref, f32[16,32,512]{2,1,0:T(8,128)S(1)} %get-tuple-element.91.q_ref.image, f32[16,32,512]{2,1,0:T(8,128)S(1)} %get-tuple-element.101.p_ref, ...), custom_call_target="tpu_custom_call", output_to_operand_aliasing={{}: (4, {})} | custom-call | flops 2875000064 | tf_op jit(solution)/shard_map/pallas_call | solution.py:528
  86.0 1.2 %collective-permute-done.12 = f32[64,96]{1,0:T(8,128)S(1)} collective-permute-done((f32[64,96]{1,0:T(8,128)S(1)}, f32[64,96]{1,0:T(8,128)S(1)}, u32[]{:S(2)}, u32[]{:S(2)}) %collective-permute-start.12) | collective-permute-done | bytes 24608 | tf_op jit(solution)/shard_map/ppermute | solution.py:634
  87.3 1.6 %collective-permute-start.13 = (f32[64,96]{1,0:T(8,128)S(1)}, f32[64,96]{1,0:T(8,128)S(1)}, u32[]{:S(2)}, u32[]{:S(2)}) collective-permute-start(f32[64,96]{1,0:T(8,128)S(1)} %add.23), channel_id=1, source_target_pairs={{0,8},{1,9},{2,10},{3,11},{4,12},{5,13},{6,14},{7,15},{8,0},{9,1},... | collective-permute-start | bytes 73736 | tf_op jit(solution)/shard_map/ppermute | solution.py:634
  88.9 3.1 %shard_map.144.refs_0_ = f32[8192,128]{1,0:T(8,128)S(1)} custom-call(s32[8192]{0:T(1024)S(1)} %copy-done.4, s32[16]{0:T(128)S(1)} %get-tuple-element.52.perm.perm_ref, f32[16,32,512]{2,1,0:T(8,128)S(1)} %get-tuple-element.91.q_ref.image, f32[16,32,512]{2,1,0:T(8,128)S(1)} %get-tuple-element.101.p_ref, ...), custom_call_target="tpu_custom_call", output_to_operand_aliasing={{}: (4, {})} | custom-call | flops 2875000064 | tf_op jit(solution)/shard_map/pallas_call | solution.py:528
  92.0 2.3 %collective-permute-start.14 = (f32[64,96]{1,0:T(8,128)S(1)}, f32[64,96]{1,0:T(8,128)S(1)}, u32[]{:S(2)}, u32[]{:S(2)}) collective-permute-start(f32[64,96]{1,0:T(8,128)S(1)} %add.24), channel_id=1, source_target_pairs={{0,24},{1,25},{2,26},{3,27},{4,28},{5,29},{6,30},{7,31},{8,16},{9,... | collective-permute-start | bytes 73736 | tf_op jit(solution)/shard_map/ppermute | solution.py:634
  94.3 3.1 %shard_map.145.rows_ref = f32[8192,128]{1,0:T(8,128)S(1)} custom-call(s32[8192]{0:T(1024)S(1)} %copy-done.4, s32[16]{0:T(128)S(1)} %get-tuple-element.52.perm.perm_ref, f32[16,32,512]{2,1,0:T(8,128)S(1)} %get-tuple-element.91.q_ref.image, f32[16,32,512]{2,1,0:T(8,128)S(1)} %get-tuple-element.101.p_ref, ...), custom_call_target="tpu_custom_call", output_to_operand_aliasing={{}: (4, {})} | custom-call | flops 2875000064 | tf_op jit(solution)/shard_map/pallas_call | solution.py:528
  97.5 2.0 %collective-permute-start.15 = (f32[64,96]{1,0:T(8,128)S(1)}, f32[64,96]{1,0:T(8,128)S(1)}, u32[]{:S(2)}, u32[]{:S(2)}) collective-permute-start(f32[64,96]{1,0:T(8,128)S(1)} %add.25), channel_id=1, source_target_pairs={{0,32},{1,33},{2,34},{3,35},{4,36},{5,37},{6,38},{7,39},{8,40},{9,... | collective-permute-start | bytes 73736 | tf_op jit(solution)/shard_map/ppermute | solution.py:634
  100.1 1.4 %collective-permute-done.15 = f32[64,96]{1,0:T(8,128)S(1)} collective-permute-done((f32[64,96]{1,0:T(8,128)S(1)}, f32[64,96]{1,0:T(8,128)S(1)}, u32[]{:S(2)}, u32[]{:S(2)}) %collective-permute-start.15) | collective-permute-done | bytes 24608 | tf_op jit(solution)/shard_map/ppermute | solution.py:634
  101.5 4.1 %collective-permute-start.16 = (f32[64,96]{1,0:T(8,128)S(1)}, f32[64,96]{1,0:T(8,128)S(1)}, u32[]{:S(2)}, u32[]{:S(2)}) collective-permute-start(f32[64,96]{1,0:T(8,128)S(1)} %add.26), channel_id=1, source_target_pairs={{0,96},{1,97},{2,98},{3,99},{4,100},{5,101},{6,102},{7,103},{8,104... | collective-permute-start | bytes 73736 | tf_op jit(solution)/shard_map/ppermute | solution.py:634
  106.2 1.3 %collective-permute-done.16 = f32[64,96]{1,0:T(8,128)S(1)} collective-permute-done((f32[64,96]{1,0:T(8,128)S(1)}, f32[64,96]{1,0:T(8,128)S(1)}, u32[]{:S(2)}, u32[]{:S(2)}) %collective-permute-start.16) | collective-permute-done | bytes 24608 | tf_op jit(solution)/shard_map/ppermute | solution.py:634
  107.5 8.7 %shard_map.148 = (f32[32,8192]{1,0:T(8,128)}, f32[32,8192]{1,0:T(8,128)}) custom-call(f32[64,96]{1,0:T(8,128)S(1)} %add.27.gram, f32[32,8192]{1,0:T(8,128)S(1)} %copy-done, f32[64,4096]{1,0:T(8,128)S(1)} %shard_map.146.mapped0, f32[64,4096]{1,0:T(8,128)S(1)} %shard_map.147.mapped1), custom_call_target="tpu_custom_call" | custom-call | tf_op jit(solution)/shard_map/pallas_call | solution.py:622
  (49 shorter events, 6.1 us)
Async XLA Ops:
  21.0 8.5 %collective-permute-start = (bf16[1120,128]{1,0:T(8,128)(2,1)S(1)}, bf16[1120,128]{1,0:T(8,128)(2,1)S(1)}, u32[]{:S(2)}, u32[]{:S(2)}) collective-permute-start(bf16[1120,128]{1,0:T(8,128)(2,1)S(1)} %get-tuple-element.53), channel_id=1, source_target_pairs={{0,2},{1,3},{2,0},{3,1},{4,6},{5,7},{6,4},{7,5},{8,10},{9,11},{10,... | collective-permute-start | bytes 860168 | tf_op jit(solution)/shard_map/ppermute | solution.py:634
  29.6 6.3 %collective-permute-start.2 = (bf16[2,224,128]{2,1,0:T(8,128)(2,1)S(1)}, bf16[2,224,128]{2,1,0:T(8,128)(2,1)S(1)}, u32[]{:S(2)}, u32[]{:S(2)}) collective-permute-start(bf16[2,224,128]{2,1,0:T(8,128)(2,1)S(1)} %fusion), channel_id=1, source_target_pairs={{0,6},{1,7},{2,4},{3,5},{4,2},{5,3},{6,0},{7,1},{8,14},{9,15},{10,... | collective-permute-start | bytes 344072 | tf_op jit(solution)/shard_map/ppermute | solution.py:634
  32.6 11.8 %collective-permute-start.1 = (bf16[2,1120,128]{2,1,0:T(8,128)(2,1)S(1)}, bf16[2,1120,128]{2,1,0:T(8,128)(2,1)S(1)}, u32[]{:S(2)}, u32[]{:S(2)}) collective-permute-start(bf16[2,1120,128]{2,1,0:T(8,128)(2,1)S(1)} %pad_maximum_fusion.pair_a), channel_id=1, source_target_pairs={{0,1},{1,0},{2,3},{3,2},{4,5},{5,4},{6,7},{7,6},{8,9},{9,8},{10,11... | collective-permute-start | bytes 1720328 | tf_op jit(solution)/shard_map/ppermute | solution.py:634
  35.9 10.3 %copy-start.1 = (bf16[16,256,512]{2,1,0:T(8,128)(2,1)S(1)}, bf16[16,256,512]{2,1,0:T(8,128)(2,1)}, u32[]{:S(2)}) copy-start(bf16[16,256,512]{2,1,0:T(8,128)(2,1)} %leaf_v.3) | copy-start | bytes 12582916
  35.9 10.3 %copy-start.2 = (bf16[4,256,1024]{2,1,0:T(8,128)(2,1)S(1)}, bf16[4,256,1024]{2,1,0:T(8,128)(2,1)}, u32[]{:S(2)}) copy-start(bf16[4,256,1024]{2,1,0:T(8,128)(2,1)} %mid_v.3) | copy-start | bytes 6291460
  35.9 10.3 %copy-start.3 = (bf16[4,256,256]{2,1,0:T(8,128)(2,1)S(1)}, bf16[4,256,256]{2,1,0:T(8,128)(2,1)}, u32[]{:S(2)}) copy-start(bf16[4,256,256]{2,1,0:T(8,128)(2,1)} %top_v.3) | copy-start | bytes 1572868
  36.0 10.3 %copy-start.5 = (s32[4,4]{1,0:T(4,128)S(1)}, s32[4,4]{1,0:T(4,128)}, u32[]{:S(2)}) copy-start(s32[4,4]{1,0:T(4,128)} %far_mid.3) | copy-start | bytes 196
  36.0 10.3 %copy-start.6 = (s32[128,4]{0,1:T(4,128)S(1)}, s32[128,4]{0,1:T(4,128)}, u32[]{:S(2)}) copy-start(s32[128,4]{0,1:T(4,128)} %param.20) | copy-start | bytes 6148
  36.0 8.3 %collective-permute-start.3 = (bf16[4,224,128]{2,1,0:T(8,128)(2,1)S(1)}, bf16[4,224,128]{2,1,0:T(8,128)(2,1)S(1)}, u32[]{:S(2)}, u32[]{:S(2)}) collective-permute-start(bf16[4,224,128]{2,1,0:T(8,128)(2,1)S(1)} %pad_maximum_fusion.2), channel_id=1, source_target_pairs={{0,8},{1,9},{2,10},{3,11},{4,12},{5,13},{6,14},{7,15},{8,0},{9,1},... | collective-permute-start | bytes 688136 | tf_op jit(solution)/shard_map/ppermute | solution.py:634
  44.3 1.9 %collective-permute-start.4 = (bf16[8,224,128]{2,1,0:T(8,128)(2,1)S(1)}, bf16[8,224,128]{2,1,0:T(8,128)(2,1)S(1)}, u32[]{:S(2)}, u32[]{:S(2)}) collective-permute-start(bf16[8,224,128]{2,1,0:T(8,128)(2,1)S(1)} %pad_maximum_fusion.1.eight_a), channel_id=1, source_target_pairs={{0,1},{1,0},{2,3},{3,2},{4,5},{5,4},{6,7},{7,6},{8,9},{9,8},{10,11... | collective-permute-start | bytes 1376264 | tf_op jit(solution)/shard_map/ppermute | solution.py:634
  53.8 4.6 %collective-permute-start.5 = (bf16[320,128]{1,0:T(8,128)(2,1)S(1)}, bf16[320,128]{1,0:T(8,128)(2,1)S(1)}, u32[]{:S(2)}, u32[]{:S(2)}) collective-permute-start(bf16[320,128]{1,0:T(8,128)(2,1)S(1)} %get-tuple-element.80), channel_id=1, source_target_pairs={{0,2},{1,3},{2,0},{3,1},{4,6},{5,7},{6,4},{7,5},{8,10},{9,11},{10,... | collective-permute-start | bytes 245768 | tf_op jit(solution)/shard_map/ppermute | solution.py:634
  58.4 5.2 %collective-permute-start.7 = (bf16[2,64,128]{2,1,0:T(8,128)(2,1)S(1)}, bf16[2,64,128]{2,1,0:T(8,128)(2,1)S(1)}, u32[]{:S(2)}, u32[]{:S(2)}) collective-permute-start(bf16[2,64,128]{2,1,0:T(8,128)(2,1)S(1)} %fusion.1), channel_id=1, source_target_pairs={{0,6},{1,7},{2,4},{3,5},{4,2},{5,3},{6,0},{7,1},{8,14},{9,15},{10,... | collective-permute-start | bytes 98312 | tf_op jit(solution)/shard_map/ppermute | solution.py:634
  59.2 11.0 %collective-permute-start.6 = (bf16[2,320,128]{2,1,0:T(8,128)(2,1)S(1)}, bf16[2,320,128]{2,1,0:T(8,128)(2,1)S(1)}, u32[]{:S(2)}, u32[]{:S(2)}) collective-permute-start(bf16[2,320,128]{2,1,0:T(8,128)(2,1)S(1)} %pad_maximum_fusion.3.pair_a), channel_id=1, source_target_pairs={{0,1},{1,0},{2,3},{3,2},{4,5},{5,4},{6,7},{7,6},{8,9},{9,8},{10,11... | collective-permute-start | bytes 491528 | tf_op jit(solution)/shard_map/ppermute | solution.py:634
  63.6 4.3 %collective-permute-start.8 = (bf16[4,64,128]{2,1,0:T(8,128)(2,1)S(1)}, bf16[4,64,128]{2,1,0:T(8,128)(2,1)S(1)}, u32[]{:S(2)}, u32[]{:S(2)}) collective-permute-start(bf16[4,64,128]{2,1,0:T(8,128)(2,1)S(1)} %pad_maximum_fusion.5), channel_id=1, source_target_pairs={{0,8},{1,9},{2,10},{3,11},{4,12},{5,13},{6,14},{7,15},{8,0},{9,1},... | collective-permute-start | bytes 196616 | tf_op jit(solution)/shard_map/ppermute | solution.py:634
  68.0 2.3 %collective-permute-start.9 = (bf16[8,64,128]{2,1,0:T(8,128)(2,1)S(1)}, bf16[8,64,128]{2,1,0:T(8,128)(2,1)S(1)}, u32[]{:S(2)}, u32[]{:S(2)}) collective-permute-start(bf16[8,64,128]{2,1,0:T(8,128)(2,1)S(1)} %pad_maximum_fusion.4.eight_a), channel_id=1, source_target_pairs={{0,1},{1,0},{2,3},{3,2},{4,5},{5,4},{6,7},{7,6},{8,9},{9,8},{10,11... | collective-permute-start | bytes 393224 | tf_op jit(solution)/shard_map/ppermute | solution.py:634
  70.3 8.0 %copy-start.4 = (s32[8192]{0:T(1024)S(1)}, s32[8192]{0:T(1024)}, u32[]{:S(2)}) copy-start(s32[8192]{0:T(1024)} %order_ref.7) | copy-start | bytes 98308
  76.8 1.4 %collective-permute-start.10 = (f32[64,96]{1,0:T(8,128)S(1)}, f32[64,96]{1,0:T(8,128)S(1)}, u32[]{:S(2)}, u32[]{:S(2)}) collective-permute-start(f32[64,96]{1,0:T(8,128)S(1)} %get-tuple-element.100), channel_id=1, source_target_pairs={{0,1},{1,0},{2,3},{3,2},{4,5},{5,4},{6,7},{7,6},{8,9},{9,8},{10,11... | collective-permute-start | bytes 73736 | tf_op jit(solution)/shard_map/ppermute | solution.py:634
  78.2 3.9 %collective-permute-start.11 = (f32[64,96]{1,0:T(8,128)S(1)}, f32[64,96]{1,0:T(8,128)S(1)}, u32[]{:S(2)}, u32[]{:S(2)}) collective-permute-start(f32[64,96]{1,0:T(8,128)S(1)} %add.21), channel_id=1, source_target_pairs={{0,2},{1,3},{2,0},{3,1},{4,6},{5,7},{6,4},{7,5},{8,10},{9,11},{10,... | collective-permute-start | bytes 73736 | tf_op jit(solution)/shard_map/ppermute | solution.py:634
  82.1 5.1 %collective-permute-start.12 = (f32[64,96]{1,0:T(8,128)S(1)}, f32[64,96]{1,0:T(8,128)S(1)}, u32[]{:S(2)}, u32[]{:S(2)}) collective-permute-start(f32[64,96]{1,0:T(8,128)S(1)} %add.22), channel_id=1, source_target_pairs={{0,6},{1,7},{2,4},{3,5},{4,2},{5,3},{6,0},{7,1},{8,14},{9,15},{10,... | collective-permute-start | bytes 73736 | tf_op jit(solution)/shard_map/ppermute | solution.py:634
  87.3 4.7 %collective-permute-start.13 = (f32[64,96]{1,0:T(8,128)S(1)}, f32[64,96]{1,0:T(8,128)S(1)}, u32[]{:S(2)}, u32[]{:S(2)}) collective-permute-start(f32[64,96]{1,0:T(8,128)S(1)} %add.23), channel_id=1, source_target_pairs={{0,8},{1,9},{2,10},{3,11},{4,12},{5,13},{6,14},{7,15},{8,0},{9,1},... | collective-permute-start | bytes 73736 | tf_op jit(solution)/shard_map/ppermute | solution.py:634
  92.0 5.4 %collective-permute-start.14 = (f32[64,96]{1,0:T(8,128)S(1)}, f32[64,96]{1,0:T(8,128)S(1)}, u32[]{:S(2)}, u32[]{:S(2)}) collective-permute-start(f32[64,96]{1,0:T(8,128)S(1)} %add.24), channel_id=1, source_target_pairs={{0,24},{1,25},{2,26},{3,27},{4,28},{5,29},{6,30},{7,31},{8,16},{9,... | collective-permute-start | bytes 73736 | tf_op jit(solution)/shard_map/ppermute | solution.py:634
  97.5 4.0 %collective-permute-start.15 = (f32[64,96]{1,0:T(8,128)S(1)}, f32[64,96]{1,0:T(8,128)S(1)}, u32[]{:S(2)}, u32[]{:S(2)}) collective-permute-start(f32[64,96]{1,0:T(8,128)S(1)} %add.25), channel_id=1, source_target_pairs={{0,32},{1,33},{2,34},{3,35},{4,36},{5,37},{6,38},{7,39},{8,40},{9,... | collective-permute-start | bytes 73736 | tf_op jit(solution)/shard_map/ppermute | solution.py:634
  101.5 6.0 %copy-start = (f32[32,8192]{1,0:T(8,128)S(1)}, f32[32,8192]{1,0:T(8,128)}, u32[]{:S(2)}) copy-start(f32[32,8192]{1,0:T(8,128)} %rhs.1) | copy-start | bytes 3145732
  101.5 6.0 %collective-permute-start.16 = (f32[64,96]{1,0:T(8,128)S(1)}, f32[64,96]{1,0:T(8,128)S(1)}, u32[]{:S(2)}, u32[]{:S(2)}) collective-permute-start(f32[64,96]{1,0:T(8,128)S(1)} %add.26), channel_id=1, source_target_pairs={{0,96},{1,97},{2,98},{3,99},{4,100},{5,101},{6,102},{7,103},{8,104... | collective-permute-start | bytes 73736 | tf_op jit(solution)/shard_map/ppermute | solution.py:634

commit v3 on v2

--- a/solution.py
+++ b/solution.py
@@ -376,27 +376,89 @@
     return lax.axis_index("outer") * lax.axis_size("inner") + lax.axis_index("inner")
 
 
-def pool_copies(pair_a, pair_b, eight_a, eight_b, four, sixteen, sems):
-    return [
-        pltpu.make_async_copy(pair_a, four.at[0:2], sems.at[0]),
-        pltpu.make_async_copy(pair_b, four.at[2:4], sems.at[1]),
-        pltpu.make_async_copy(eight_a, sixteen.at[0:8], sems.at[2]),
-        pltpu.make_async_copy(eight_b, sixteen.at[8:16], sems.at[3]),
-    ]
+def mid_weights(pairs, entry, device, first):
+    slot = mid_slot(entry, device)
+    at = pl.multiple_of(first + (entry & 3) * S_ROWS, S_ROWS)
+    return slot, joined(pairs, slot, at)
+
+
+def mid_first(far_mid, pair_a, pair_b):
+    def kernel(lists, near_pair, far_pair, sums, tiles, four):
+        four[0:2] = near_pair[...]
+        four[2:4] = far_pair[...]
+        device = this_device()
+        for node in range(MID):
+            target = far_target(*unpack_points(four, 0, node * C_ROWS))
+            total = jnp.zeros((SIDES, RANK), f32)
+            for m in range(LIST):
+                entry = lists[node, m]
+                slot, weights = mid_weights(four, entry, device, S1_AT)
+                source = unpack_points(four, slot, pl.multiple_of((entry & 3) * C_ROWS, C_ROWS))
+                block = far_tile(target, source)
+                tiles[node * LIST + m] = block
+                total = total + nt(weights, block)
+            sums[node] = total
+
+    return pl.pallas_call(
+        kernel,
+        out_shape=[
+            jax.ShapeDtypeStruct((MID, SIDES, RANK), f32),
+            jax.ShapeDtypeStruct((MID * LIST, RANK, RANK), bf16),
+        ],
+        in_specs=[SM] + [VM] * 2, out_specs=[VM] * 2,
+        scratch_shapes=[pltpu.VMEM((4, PAY_ROWS, LANES), bf16)],
+        compiler_params=params(12), cost_estimate=lasting(3),
+    )(far_mid, pair_a, pair_b)
+
+
+def mid_second(far_mid, pair_a, pair_b, tiles):
+    def kernel(lists, near_pair, far_pair, tiles_ref, sums, four):
+        four[0:2] = near_pair[...]
+        four[2:4] = far_pair[...]
+        device = this_device()
+        for node in range(MID):
+            total = jnp.zeros((SIDES, RANK), f32)
+            for m in range(LIST):
+                _, weights = mid_weights(four, lists[node, m], device, 0)
+                total = total + nt(weights, tiles_ref[node * LIST + m])
+            sums[node] = total
+
+    return pl.pallas_call(
+        kernel, out_shape=jax.ShapeDtypeStruct((MID, SIDES, RANK), f32),
+        in_specs=[SM] + [VM] * 3, out_specs=VM,
+        scratch_shapes=[pltpu.VMEM((4, PAY2_ROWS, LANES), bf16)],
+        compiler_params=params(12), cost_estimate=lasting(1),
+    )(far_mid, pair_a, pair_b, tiles)
+
+
+def products(lefts, rights):
+    wide = len(rights) * SIDES
+    total = jnp.zeros((2 * len(lefts) * SIDES, 2 * wide), f32)
+    for place in range(LEAVES):
+        parts = [[split(ref[place]) for ref in refs] for refs in (lefts, rights)]
+        left, right = [jnp.concatenate([part[i] for i in range(2) for part in side], axis=0) for side in parts]
+        total = total + nt(left, right)
+    return total[: len(lefts) * SIDES] + total[len(lefts) * SIDES :]
+
+
+def early_products(right, image):
+    def kernel(r_ref, q_ref, out):
+        out[...] = products((r_ref, q_ref), (r_ref, q_ref))
+
+    return pl.pallas_call(
+        kernel, out_shape=jax.ShapeDtypeStruct((2 * SIDES, LANES), f32), in_specs=[VM] * 2, out_specs=VM,
+        compiler_params=params(12), cost_estimate=lasting(1),
+    )(right, image)
 
 
 def far_first_kernel(
-    far_mid, far_top, perm, pair_a, pair_b, eight_a, eight_b, leaf_v, mid_v, top_v, right, near0, near1, near2, near3,
-    q_out, pay, mid_tiles, top_tiles,
-    four, sixteen, s0, sems,
+    far_top, perm, eight_a, eight_b, leaf_v, mid_v, top_v, mid_far, right, near0, near1, near2, near3,
+    q_out, pay, top_tiles,
+    sixteen, s0,
 ):
-    pools = pool_copies(pair_a, pair_b, eight_a, eight_b, four, sixteen, sems)
-    for copy in pools:
-        copy.start()
-    for copy in pools:
-        copy.wait()
+    sixteen[0:8] = eight_a[...]
+    sixteen[8:16] = eight_b[...]
     device = this_device()
-
     target = far_target(*unpack_points(sixteen, 0, 0))
     top_far = jnp.zeros((SIDES, RANK), f32)
     for m in range(LIST):
@@ -404,18 +466,6 @@
         block = far_tile(target, unpack_points(sixteen, slot, 0))
         top_tiles[m] = block
         top_far = top_far + nt(joined(sixteen, slot, C_ROWS), block)
-    mid_far = []
-    for node in range(MID):
-        target = far_target(*unpack_points(four, 0, node * C_ROWS))
-        total = jnp.zeros((SIDES, RANK), f32)
-        for m in range(LIST):
-            entry = far_mid[node, m]
-            slot = mid_slot(entry, device)
-            local = entry & 3
-            block = far_tile(target, unpack_points(four, slot, pl.multiple_of(local * C_ROWS, C_ROWS)))
-            mid_tiles[node * LIST + m] = block
-            total = total + nt(joined(four, slot, pl.multiple_of(S1_AT + local * S_ROWS, S_ROWS)), block)
-        mid_far.append(total)
     descend(mid_far, top_far, perm, mid_v, top_v, leaf_v, s0, right, (near0, near1, near2, near3), q_out)
     for place in range(LEAVES):
         leaf = perm[place]
@@ -424,102 +474,81 @@
     climb(s0, mid_v, top_v, pay, 0, S1_ROWS)
 
 
-def far_first(far_mid, far_top, perm, pools, interps, right, near):
+def far_first(far_top, perm, eights, interps, mid_far, right, near):
     return pl.pallas_call(
         far_first_kernel,
         out_shape=[
             jax.ShapeDtypeStruct((LEAVES, SIDES, LEAF), f32),
             jax.ShapeDtypeStruct((PAY2_ROWS, LANES), bf16),
-            jax.ShapeDtypeStruct((MID * LIST, RANK, RANK), bf16),
             jax.ShapeDtypeStruct((LIST, RANK, RANK), bf16),
         ],
-        in_specs=[SM] * 3 + [pl.BlockSpec(memory_space=pl.ANY)] * 4 + [VM] * 8,
-        out_specs=[VM] * 4,
+        in_specs=[SM] * 2 + [VM] * 11,
+        out_specs=[VM] * 3,
         scratch_shapes=[
-            pltpu.VMEM((4, PAY_ROWS, LANES), bf16),
             pltpu.VMEM((16, TOP_ROWS, LANES), bf16),
             pltpu.VMEM((LEAVES, SIDES, RANK), bf16),
-            pltpu.SemaphoreType.DMA((4,)),
         ],
         compiler_params=params(14),
         cost_estimate=lasting(8),
-    )(far_mid, far_top, perm, *pools, *interps, right, *near)
+    )(far_top, perm, *eights, *interps, mid_far, right, *near)
 
 
 def far_second_kernel(
-    far_mid, far_top, perm, pair_a, pair_b, eight_a, eight_b, leaf_v, mid_v, top_v, mid_tiles, top_tiles,
+    far_top, perm, eight_a, eight_b, leaf_v, mid_v, top_v, mid_far, top_tiles, early,
     right, image, near0, near1, near2, near3,
     p_out, gram,
-    four, sixteen, u0, sems,
+    sixteen, u0,
 ):
-    pools = pool_copies(pair_a, pair_b, eight_a, eight_b, four, sixteen, sems)
-    for copy in pools:
-        copy.start()
-    for copy in pools:
-        copy.wait()
+    sixteen[0:8] = eight_a[...]
+    sixteen[8:16] = eight_b[...]
     device = this_device()
     top_far = jnp.zeros((SIDES, RANK), f32)
     for m in range(LIST):
         top_far = top_far + nt(joined(sixteen, top_slot(far_top[m, device], device), 0), top_tiles[m])
-    mid_far = []
-    for node in range(MID):
-        total = jnp.zeros((SIDES, RANK), f32)
-        for m in range(LIST):
-            entry = far_mid[node, m]
-            weights = joined(four, mid_slot(entry, device), pl.multiple_of((entry & 3) * S_ROWS, S_ROWS))
-            total = total + nt(weights, mid_tiles[node * LIST + m])
-        mid_far.append(total)
     descend(mid_far, top_far, perm, mid_v, top_v, leaf_v, u0, image, (near0, near1, near2, near3), p_out)
-    total = jnp.zeros((4 * SIDES, 6 * SIDES), f32)
-    for place in range(LEAVES):
-        parts = [split(ref[place]) for ref in (right, image, p_out)]
-        left = jnp.concatenate([part[i] for i in range(2) for part in parts[:2]], axis=0)
-        total = total + nt(left, jnp.concatenate([part[i] for i in range(2) for part in parts], axis=0))
-    total = total[: 2 * SIDES] + total[2 * SIDES :]
-    turned = total.T
-    total = (turned[: 3 * SIDES] + turned[3 * SIDES :]).T
-    gram[...] = total
-
-
-def far_second(far_mid, far_top, perm, pools, interps, mid_tiles, top_tiles, right, image, near):
+    late = products((right, image), (p_out,))
+    late = jnp.concatenate([late, jnp.zeros((2 * SIDES, LANES - 2 * SIDES), f32)], axis=1)
+    late = pltpu.roll(late + pltpu.roll(late, LANES - SIDES, 1), 2 * SIDES, 1)
+    both = early[...] + pltpu.roll(early[...], 2 * SIDES, 1)
+    gram[...] = jnp.where(lax.broadcasted_iota(jnp.int32, both.shape, 1) < 2 * SIDES, both, late)
+
+
+def far_second(far_top, perm, eights, interps, mid_far, top_tiles, early, right, image, near):
     return pl.pallas_call(
         far_second_kernel,
         out_shape=[
             jax.ShapeDtypeStruct((LEAVES, SIDES, LEAF), f32),
-            jax.ShapeDtypeStruct((2 * SIDES, 3 * SIDES), f32),
+            jax.ShapeDtypeStruct((2 * SIDES, LANES), f32),
         ],
-        in_specs=[SM] * 3 + [pl.BlockSpec(memory_space=pl.ANY)] * 4 + [VM] * 11,
+        in_specs=[SM] * 2 + [VM] * 14,
         out_specs=[VM] * 2,
         scratch_shapes=[
-            pltpu.VMEM((4, PAY2_ROWS, LANES), bf16),
             pltpu.VMEM((16, S_ROWS, LANES), bf16),
             pltpu.VMEM((LEAVES, SIDES, RANK), bf16),
-            pltpu.SemaphoreType.DMA((4,)),
         ],
         compiler_params=params(14),
         cost_estimate=lasting(8),
-    )(far_mid, far_top, perm, *pools, *interps, mid_tiles, top_tiles, right, image, *near)
+    )(far_top, perm, *eights, *interps, mid_far, top_tiles, early, right, image, *near)
 
 
 PARTS = 2
 PART = SPAN // PARTS
 
 
-def put_back(group, order, perm, image, second, rows):
+def put_back(places, order, perm, image, second, rows):
     def kernel(order_ref, perm_ref, q_ref, p_ref, *refs):
         out, tree = refs[-2:]
-        for member in range(LIST):
-            place = LIST * group + member
+        for i, place in enumerate(places):
             stacked = jnp.concatenate([q_ref[place], p_ref[place], jnp.zeros((2 * SIDES, LEAF), f32)], axis=0)
-            tree[member * LEAF : (member + 1) * LEAF, :] = stacked.T
-
-        for member in range(LIST):
-            base = perm_ref[LIST * group + member] * LEAF
-
-            def put(step, _, member=member, base=base):
+            tree[i * LEAF : (i + 1) * LEAF, :] = stacked.T
+
+        for i, place in enumerate(places):
+            base = perm_ref[place] * LEAF
+
+            def put(step, _, i=i, base=base):
                 at = step * 64
                 for u in range(64):
-                    out[pl.ds(order_ref[base + at + u], 1), :] = tree[pl.ds(member * LEAF + at + u, 1), :]
+                    out[pl.ds(order_ref[base + at + u], 1), :] = tree[pl.ds(i * LEAF + at + u, 1), :]
                 return 0
 
             lax.fori_loop(0, LEAF // 64, put, 0)
@@ -528,7 +557,7 @@
     return pl.pallas_call(
         kernel, out_shape=jax.ShapeDtypeStruct((SPAN, LANES), f32),
         in_specs=[SM] * 2 + [VM] * (2 + len(earlier)), out_specs=VM,
-        scratch_shapes=[pltpu.VMEM((LIST * LEAF, LANES), f32)],
+        scratch_shapes=[pltpu.VMEM((len(places) * LEAF, LANES), f32)],
         input_output_aliases={4: 0} if earlier else {},
         compiler_params=params(12), cost_estimate=lasting(2.5),
     )(order, perm, image, second, *earlier)
@@ -634,21 +663,24 @@
     return lax.ppermute(value, AXES, [(source, source ^ mask) for source in range(count)])
 
 
-def gather_pools(payload, top_at, inputs, steps):
+def gather_pools(payload, top_at, inputs, steps, beside_mid):
     done = []
 
-    def beside(step, values):
+    def beside(values, work):
         nonlocal inputs
-        arrived, results, inputs = lax.optimization_barrier((values, steps[step](inputs), inputs))
+        arrived, results, inputs = lax.optimization_barrier((values, work(inputs), inputs))
         done.append(results)
         return arrived
 
-    pair = jnp.stack([payload, beside(0, swapped(payload, 2))])
+    pair = jnp.stack([payload, beside(swapped(payload, 2), steps[0])])
     two = pair[:, top_at:]
-    four = jnp.concatenate([two, beside(1, swapped(two, 6))])
-    eight = jnp.concatenate([four, beside(2, swapped(four, 8))])
-    other_pair, other_eight = beside(3, (swapped(pair, 1), swapped(eight, 1)))
-    return (pair, other_pair, eight, other_eight), [result for results in done for result in results]
+    other_two, other_pair = beside((swapped(two, 6), swapped(pair, 1)), steps[1])
+    four = jnp.concatenate([two, other_two])
+    other_four = beside(swapped(four, 8), lambda inputs: [beside_mid(pair, other_pair), *steps[2](inputs)])
+    mid = done[2].pop(0)
+    eight = jnp.concatenate([four, other_four])
+    other_eight = beside(swapped(eight, 1), steps[3])
+    return (eight, other_eight), mid, [result for results in done for result in results]
 
 
 def shards(
@@ -659,25 +691,41 @@
     a_rows, b_rows, right, payload, perm = setup(
         leaf_skel, skel_mid, near_lists.T, tree_order, skel_top, points, rhs, interps
     )
+
     def first(*groups):
         return lambda inputs: [near_first(group, *inputs) for group in groups]
 
-    pools, found = gather_pools(payload, MID_ROWS, (a_rows, b_rows, right), [first(0, 1), first(2), first(3), first()])
+    eights, (mid_far, mid_tiles), found = gather_pools(
+        payload, MID_ROWS, (a_rows, b_rows, right), [first(0, 1), first(2), first(3), first()],
+        lambda *pairs: mid_first(far_mid, *pairs),
+    )
     near, tiles = zip(*found)
-    lists = (far_mid, far_top.T)
-    image, payload, mid_tiles, top_tiles = far_first(*lists, perm, pools, interps, right, near)
+    image, payload, top_tiles = far_first(far_top.T, perm, eights, interps, mid_far, right, near)
+
     def again(*groups):
         return lambda inputs: [near_second(group, tiles[group], *inputs) for group in groups]
 
-    pools, near = gather_pools(payload, S1_ROWS, (image,), [again(0), again(1), again(2), again(3)])
-    second, gram = far_second(*lists, perm, pools, interps, mid_tiles, top_tiles, right, image, near)
-    rows = None
-    for group in range(GROUPS):
-        rows = put_back(group, tree_order, perm, image, second, rows)
-    mapped = [to_columns(part, rows) for part in range(PARTS)]
-    for mask in (1, 2, 6, 8, 24, 32, 96):
-        gram = gram + swapped(gram, mask)
-    return tuple(finish(gram, rhs, mapped))
+    early = []
+
+    def again_and_products(inputs):
+        early.append(early_products(right, *inputs))
+        return again(1)(inputs)
+
+    eights, mid_far, near = gather_pools(
+        payload, S1_ROWS, (image,), [again(0), again_and_products, again(2), again(3)],
+        lambda *pairs: mid_second(far_mid, *pairs, mid_tiles),
+    )
+    second, gram = far_second(
+        far_top.T, perm, eights, interps, mid_far, top_tiles, early[0], right, image, near
+    )
+    rows, place = None, 0
+    for mask, count in ((1, 2), (2, 3), (6, 3), (8, 3), (24, 3), (32, 2)):
+        places = range(place, place + count)
+        rows = put_back(places, tree_order, perm, image, second, rows)
+        sent, rows = lax.optimization_barrier((swapped(gram, mask), rows))
+        gram, place = gram + sent, place + count
+    gram = gram + swapped(gram, 96)
+    return tuple(finish(gram, rhs, [to_columns(part, rows) for part in range(PARTS)]))
 
 
 def solution(mesh):

time: 117 us -> 114 us (0.974)
  waiting for transfers between devices: 16.4 us -> 7.06 us
  starting transfers between devices: 21 us -> 25 us
  Pallas kernels: 77.7 us -> 80 us
    ppermute x17, waiting for transfers between devices: 16.4 us -> 7.06 us  [swapped(): lax.ppermute(value, AXES, [(source, source ^ mask) for source in range(co...]
    pallas_call x0 -> x3, Pallas kernels: none -> 4.33 us  [the longest x1 2.27 us: mid_first(): pl.pallas_call(kernel, out_shape=[jax.ShapeDtypeStruct((MID, SIDES, RANK)...]
    ppermute x17, starting transfers between devices: 21 us -> 25 us  [swapped(): lax.ppermute(value, AXES, [(source, source ^ mask) for source in range(co...]
    pallas_call x1, Pallas kernels: 6.5 us -> 4.06 us  [far_second(): pl.pallas_call(far_second_kernel, out_shape=[jax.ShapeDtypeStruct((LEAVES...]
    pallas_call x4 -> x6, Pallas kernels: 12.6 us -> 14.9 us  [put_back(): pl.pallas_call(kernel, out_shape=jax.ShapeDtypeStruct((SPAN, LANES), f32)...]
    pallas_call x1, Pallas kernels: 7.55 us -> 5.7 us  [far_first(): pl.pallas_call(far_first_kernel, out_shape=[jax.ShapeDtypeStruct((LEAVES,...]
  transfers between devices with their start and end apart: 17 -> 17, of which waited for: 11 -> 8; matrix products, arithmetic and copies ran while one was open for 0% -> 0% of each run, Pallas kernels for 30% -> 36%
where the time goes in v3:
time: 114 us; the launch traced here: 113 us
  Pallas kernels  80 us (70%)
  starting transfers between devices  25 us (22%)
  waiting for transfers between devices  7.06 us (6%)
  between operations  1.16 us (1%)
    ppermute x17, starting transfers between devices, swapped(): lax.ppermute(value, AXES, [(source, source ^ mask) for source in range(co...  25 us
    pallas_call x1, Pallas kernels, setup(): pl.pallas_call(setup_kernel, out_shape=[jax.ShapeDtypeStruct((LEAVES, LEA...  20.3 us
    pallas_call x6, Pallas kernels, put_back(): pl.pallas_call(kernel, out_shape=jax.ShapeDtypeStruct((SPAN, LANES), f32)...  14.9 us
    pallas_call x4, Pallas kernels, near_first(): pl.pallas_call(kernel, out_shape=[jax.ShapeDtypeStruct((LIST, SIDES, LEAF...  12.9 us
    pallas_call x1, Pallas kernels, finish(): pl.pallas_call(finish_kernel, out_shape=[jax.ShapeDtypeStruct((SIDES, SPA...  8.74 us
    pallas_call x4, Pallas kernels, near_second(): pl.pallas_call(kernel, out_shape=jax.ShapeDtypeStruct((LIST, SIDES, LEAF)...  7.83 us
    ppermute x17, waiting for transfers between devices, swapped(): lax.ppermute(value, AXES, [(source, source ^ mask) for source in range(co...  7.06 us
    pallas_call x1, Pallas kernels, far_first(): pl.pallas_call(far_first_kernel, out_shape=[jax.ShapeDtypeStruct((LEAVES,...  5.7 us
  transfers between devices with their start and end apart: 17, of which 8 were waited for; matrix products, arithmetic and copies ran while one was open for 0% of the time, Pallas kernels for 36%

profile of v3, /device:TPU:0, one launch (start us, length us, event | category | flops | bytes accessed | tf_op | source)
XLA Modules:
  0.0 113.4 jit_solution(7528169362880969267)
XLA Ops:
  0.6 20.3 %shard_map.131 = (bf16[16,512,128]{2,1,0:T(8,128)(2,1)S(1)}, bf16[16,512,128]{2,1,0:T(8,128)(2,1)S(1)}, f32[16,32,512]{2,1,0:T(8,128)S(1)}, bf16[1120,128]{1,0:T(8,128)(2,1)S(1)}, s32[16]{0:T(128)S(1)}) custom-call(s32[16,256]{1,0:T(8,128)} %leaf_skel_hbm.1, s32[4,256]{1,0:T(4,128)} %skel_mid_hbm.1, s32[4,16]{1,0:T(4,128)} %bitcast.16, s32[8192]{0:T(1024)} %order_ref.11, ...), custom_call_target="tpu_custom_call" | custom-call | flops 23000000512 | tf_op jit(solution)/shard_map/pallas_call | solution.py:277
  21.0 1.7 %collective-permute-start = (bf16[1120,128]{1,0:T(8,128)(2,1)S(1)}, bf16[1120,128]{1,0:T(8,128)(2,1)S(1)}, u32[]{:S(2)}, u32[]{:S(2)}) collective-permute-start(bf16[1120,128]{1,0:T(8,128)(2,1)S(1)} %get-tuple-element.68), channel_id=1, source_target_pairs={{0,2},{1,3},{2,0},{3,1},{4,6},{5,7},{6,4},{7,5},{8,10},{9,11},{10,... | collective-permute-start | bytes 860168 | tf_op jit(solution)/shard_map/ppermute | solution.py:663
  22.6 3.2 %shard_map.133 = (f32[4,32,512]{2,1,0:T(8,128)S(1)}, bf16[10,512,512]{2,1,0:T(8,128)(2,1)S(1)}) custom-call(bf16[16,512,128]{2,1,0:T(8,128)(2,1)S(1)} %get-tuple-element.86.a_ref, bf16[16,512,128]{2,1,0:T(8,128)(2,1)S(1)} %get-tuple-element.87.b_ref, f32[16,32,512]{2,1,0:T(8,128)S(1)} %get-tuple-element.88.r_ref.right), custom_call_target="tpu_custom_call" | custom-call | flops 3795000064 | tf_op jit(solution)/shard_map/pallas_call | solution.py:323
  25.9 3.2 %shard_map.132 = (f32[4,32,512]{2,1,0:T(8,128)S(1)}, bf16[10,512,512]{2,1,0:T(8,128)(2,1)S(1)}) custom-call(bf16[16,512,128]{2,1,0:T(8,128)(2,1)S(1)} %get-tuple-element.86.a_ref, bf16[16,512,128]{2,1,0:T(8,128)(2,1)S(1)} %get-tuple-element.87.b_ref, f32[16,32,512]{2,1,0:T(8,128)S(1)} %get-tuple-element.88.r_ref.right), custom_call_target="tpu_custom_call" | custom-call | flops 3795000064 | tf_op jit(solution)/shard_map/pallas_call | solution.py:323
  29.6 3.1 %collective-permute-start.1 = (bf16[2,224,128]{2,1,0:T(8,128)(2,1)S(1)}, bf16[2,224,128]{2,1,0:T(8,128)(2,1)S(1)}, u32[]{:S(2)}, u32[]{:S(2)}) collective-permute-start(bf16[2,224,128]{2,1,0:T(8,128)(2,1)S(1)} %fusion), channel_id=1, source_target_pairs={{0,6},{1,7},{2,4},{3,5},{4,2},{5,3},{6,0},{7,1},{8,14},{9,15},{10,... | collective-permute-start | bytes 344072 | tf_op jit(solution)/shard_map/ppermute | solution.py:663
  32.7 3.2 %shard_map.134 = (f32[4,32,512]{2,1,0:T(8,128)S(1)}, bf16[10,512,512]{2,1,0:T(8,128)(2,1)S(1)}) custom-call(bf16[16,512,128]{2,1,0:T(8,128)(2,1)S(1)} %get-tuple-element.86.a_ref, bf16[16,512,128]{2,1,0:T(8,128)(2,1)S(1)} %get-tuple-element.87.b_ref, f32[16,32,512]{2,1,0:T(8,128)S(1)} %get-tuple-element.88.r_ref.right), custom_call_target="tpu_custom_call" | custom-call | flops 3795000064 | tf_op jit(solution)/shard_map/pallas_call | solution.py:323
  36.6 2.0 %collective-permute-start.3 = (bf16[4,224,128]{2,1,0:T(8,128)(2,1)S(1)}, bf16[4,224,128]{2,1,0:T(8,128)(2,1)S(1)}, u32[]{:S(2)}, u32[]{:S(2)}) collective-permute-start(bf16[4,224,128]{2,1,0:T(8,128)(2,1)S(1)} %pad_maximum_fusion.2), channel_id=1, source_target_pairs={{0,8},{1,9},{2,10},{3,11},{4,12},{5,13},{6,14},{7,15},{8,0},{9,1},... | collective-permute-start | bytes 688136 | tf_op jit(solution)/shard_map/ppermute | solution.py:663
  38.6 3.2 %shard_map.136 = (f32[4,32,512]{2,1,0:T(8,128)S(1)}, bf16[10,512,512]{2,1,0:T(8,128)(2,1)S(1)}) custom-call(bf16[16,512,128]{2,1,0:T(8,128)(2,1)S(1)} %get-tuple-element.86.a_ref, bf16[16,512,128]{2,1,0:T(8,128)(2,1)S(1)} %get-tuple-element.87.b_ref, f32[16,32,512]{2,1,0:T(8,128)S(1)} %get-tuple-element.88.r_ref.right), custom_call_target="tpu_custom_call" | custom-call | flops 3795000064 | tf_op jit(solution)/shard_map/pallas_call | solution.py:323
  41.9 2.3 %shard_map.135 = (f32[4,32,256]{2,1,0:T(8,128)S(1)}, bf16[16,256,256]{2,1,0:T(8,128)(2,1)S(1)}) custom-call(s32[4,4]{1,0:T(4,128)S(1)} %copy-done.5, bf16[2,1120,128]{2,1,0:T(8,128)(2,1)S(1)} %pad_maximum_fusion.near_pair, bf16[2,1120,128]{2,1,0:T(8,128)(2,1)S(1)} %collective-permute-done.2.far_pair), custom_call_target="tpu_custom_call" | custom-call | flops 3449999872 | tf_op jit(solution)/shard_map/pallas_call | solution.py:402
  44.3 1.8 %collective-permute-done.4.eight_b = bf16[8,224,128]{2,1,0:T(8,128)(2,1)S(1)} collective-permute-done((bf16[8,224,128]{2,1,0:T(8,128)(2,1)S(1)}, bf16[8,224,128]{2,1,0:T(8,128)(2,1)S(1)}, u32[]{:S(2)}, u32[]{:S(2)}) %collective-permute-start.4) | collective-permute-done | bytes 458784 | tf_op jit(solution)/shard_map/ppermute | solution.py:663
  46.2 5.7 %shard_map.137 = (f32[16,32,512]{2,1,0:T(8,128)S(1)}, bf16[320,128]{1,0:T(8,128)(2,1)S(1)}, bf16[4,256,256]{2,1,0:T(8,128)(2,1)S(1)}) custom-call(s32[4,128]{1,0:T(4,128)S(1)} %bitcast.10, s32[16]{0:T(128)S(1)} %get-tuple-element.67.perm.perm_ref, bf16[8,224,128]{2,1,0:T(8,128)(2,1)S(1)} %pad_maximum_fusion.1.eight_a, ...), custom_call_target="tpu_custom_call" | custom-call | flops 9200000000 | tf_op jit(solution)/shard_map/pallas_call | solution.py:478
  52.3 2.0 %shard_map.138.near0 = f32[4,32,512]{2,1,0:T(8,128)S(1)} custom-call(bf16[10,512,512]{2,1,0:T(8,128)(2,1)S(1)} %get-tuple-element.98.tiles_ref, f32[16,32,512]{2,1,0:T(8,128)S(1)} %get-tuple-element.110.q_ref.image), custom_call_target="tpu_custom_call" | custom-call | flops 2990000128 | tf_op jit(solution)/shard_map/pallas_call | solution.py:341
  54.2 2.2 %collective-permute-done.5 = bf16[320,128]{1,0:T(8,128)(2,1)S(1)} collective-permute-done((bf16[320,128]{1,0:T(8,128)(2,1)S(1)}, bf16[320,128]{1,0:T(8,128)(2,1)S(1)}, u32[]{:S(2)}, u32[]{:S(2)}) %collective-permute-start.5) | collective-permute-done | bytes 81952 | tf_op jit(solution)/shard_map/ppermute | solution.py:663
  56.4 2.9 %collective-permute-start.6 = (bf16[2,64,128]{2,1,0:T(8,128)(2,1)S(1)}, bf16[2,64,128]{2,1,0:T(8,128)(2,1)S(1)}, u32[]{:S(2)}, u32[]{:S(2)}) collective-permute-start(bf16[2,64,128]{2,1,0:T(8,128)(2,1)S(1)} %fusion.1), channel_id=1, source_target_pairs={{0,6},{1,7},{2,4},{3,5},{4,2},{5,3},{6,0},{7,1},{8,14},{9,15},{10,... | collective-permute-start | bytes 98312 | tf_op jit(solution)/shard_map/ppermute | solution.py:663
  59.3 2.0 %shard_map.139.near1 = f32[4,32,512]{2,1,0:T(8,128)S(1)} custom-call(bf16[10,512,512]{2,1,0:T(8,128)(2,1)S(1)} %get-tuple-element.101.tiles_ref, f32[16,32,512]{2,1,0:T(8,128)S(1)} %get-tuple-element.110.q_ref.image), custom_call_target="tpu_custom_call" | custom-call | flops 2990000128 | tf_op jit(solution)/shard_map/pallas_call | solution.py:341
  62.1 1.9 %collective-permute-start.8 = (bf16[4,64,128]{2,1,0:T(8,128)(2,1)S(1)}, bf16[4,64,128]{2,1,0:T(8,128)(2,1)S(1)}, u32[]{:S(2)}, u32[]{:S(2)}) collective-permute-start(bf16[4,64,128]{2,1,0:T(8,128)(2,1)S(1)} %pad_maximum_fusion.5), channel_id=1, source_target_pairs={{0,8},{1,9},{2,10},{3,11},{4,12},{5,13},{6,14},{7,15},{8,0},{9,1},... | collective-permute-start | bytes 196616 | tf_op jit(solution)/shard_map/ppermute | solution.py:663
  64.0 2.0 %shard_map.141.near2 = f32[4,32,512]{2,1,0:T(8,128)S(1)} custom-call(bf16[10,512,512]{2,1,0:T(8,128)(2,1)S(1)} %get-tuple-element.106.tiles_ref, f32[16,32,512]{2,1,0:T(8,128)S(1)} %get-tuple-element.110.q_ref.image), custom_call_target="tpu_custom_call" | custom-call | flops 2990000128 | tf_op jit(solution)/shard_map/pallas_call | solution.py:341
  65.9 1.3 %shard_map.140.mid_far = f32[4,32,256]{2,1,0:T(8,128)S(1)} custom-call(s32[4,4]{1,0:T(4,128)S(1)} %copy-done.5, bf16[2,320,128]{2,1,0:T(8,128)(2,1)S(1)} %pad_maximum_fusion.3.near_pair, bf16[2,320,128]{2,1,0:T(8,128)(2,1)S(1)} %collective-permute-done.7.far_pair, bf16[16,256,256]{2,1,0:T(8,128)(2,1)S(1)} %get-tuple-element.105.tiles_ref), custom_call_target="tpu_custom_call" | custom-call | flops 1150000000 | tf_op jit(solution)/shard_map/pallas_call | solution.py:426
  67.6 2.0 %shard_map.142.near3 = f32[4,32,512]{2,1,0:T(8,128)S(1)} custom-call(bf16[10,512,512]{2,1,0:T(8,128)(2,1)S(1)} %get-tuple-element.109.tiles_ref, f32[16,32,512]{2,1,0:T(8,128)S(1)} %get-tuple-element.110.q_ref.image), custom_call_target="tpu_custom_call" | custom-call | flops 2990000128 | tf_op jit(solution)/shard_map/pallas_call | solution.py:341
  69.6 4.1 %shard_map.144 = (f32[16,32,512]{2,1,0:T(8,128)S(1)}, f32[64,128]{1,0:T(8,128)S(1)}) custom-call(s32[4,128]{1,0:T(4,128)S(1)} %bitcast.11, s32[16]{0:T(128)S(1)} %get-tuple-element.67.perm.perm_ref, bf16[8,64,128]{2,1,0:T(8,128)(2,1)S(1)} %pad_maximum_fusion.4.eight_a, bf16[8,64,128]{2,1,0:T(8,128)(2,1)S(1)} %collective-permute-done.9.eight_b, ...), custom_call_target="tpu_custom_call" | custom-call | flops 9200000000 | tf_op jit(solution)/shard_map/pallas_call | solution.py:517
  74.0 2.1 %shard_map.145.refs_0_ = f32[8192,128]{1,0:T(8,128)S(1)} custom-call(s32[8192]{0:T(1024)S(1)} %copy-done.4, s32[16]{0:T(128)S(1)} %get-tuple-element.67.perm.perm_ref, f32[16,32,512]{2,1,0:T(8,128)S(1)} %get-tuple-element.110.q_ref.image, f32[16,32,512]{2,1,0:T(8,128)S(1)} %get-tuple-element.119.p_ref), custom_call_target="tpu_custom_call" | custom-call | flops 2875000064 | tf_op jit(solution)/shard_map/pallas_call | solution.py:557
  76.2 2.6 %shard_map.146.refs_0_ = f32[8192,128]{1,0:T(8,128)S(1)} custom-call(s32[8192]{0:T(1024)S(1)} %copy-done.4, s32[16]{0:T(128)S(1)} %get-tuple-element.67.perm.perm_ref, f32[16,32,512]{2,1,0:T(8,128)S(1)} %get-tuple-element.110.q_ref.image, f32[16,32,512]{2,1,0:T(8,128)S(1)} %get-tuple-element.119.p_ref, ...), custom_call_target="tpu_custom_call", output_to_operand_aliasing={{}: (4, {})} | custom-call | flops 2875000064 | tf_op jit(solution)/shard_map/pallas_call | solution.py:557
  78.9 1.2 %collective-permute-done.11 = f32[64,128]{1,0:T(8,128)S(1)} collective-permute-done((f32[64,128]{1,0:T(8,128)S(1)}, f32[64,128]{1,0:T(8,128)S(1)}, u32[]{:S(2)}, u32[]{:S(2)}) %collective-permute-start.11) | collective-permute-done | bytes 32800 | tf_op jit(solution)/shard_map/ppermute | solution.py:663
  80.2 2.4 %collective-permute-start.12 = (f32[64,128]{1,0:T(8,128)S(1)}, f32[64,128]{1,0:T(8,128)S(1)}, u32[]{:S(2)}, u32[]{:S(2)}) collective-permute-start(f32[64,128]{1,0:T(8,128)S(1)} %add.22), channel_id=1, source_target_pairs={{0,6},{1,7},{2,4},{3,5},{4,2},{5,3},{6,0},{7,1},{8,14},{9,15},{10,... | collective-permute-start | bytes 98312 | tf_op jit(solution)/shard_map/ppermute | solution.py:663
  82.5 2.6 %shard_map.147.refs_0_ = f32[8192,128]{1,0:T(8,128)S(1)} custom-call(s32[8192]{0:T(1024)S(1)} %copy-done.4, s32[16]{0:T(128)S(1)} %get-tuple-element.67.perm.perm_ref, f32[16,32,512]{2,1,0:T(8,128)S(1)} %get-tuple-element.110.q_ref.image, f32[16,32,512]{2,1,0:T(8,128)S(1)} %get-tuple-element.119.p_ref, ...), custom_call_target="tpu_custom_call", output_to_operand_aliasing={{}: (4, {})} | custom-call | flops 2875000064 | tf_op jit(solution)/shard_map/pallas_call | solution.py:557
  86.5 2.6 %shard_map.148.refs_0_ = f32[8192,128]{1,0:T(8,128)S(1)} custom-call(s32[8192]{0:T(1024)S(1)} %copy-done.4, s32[16]{0:T(128)S(1)} %get-tuple-element.67.perm.perm_ref, f32[16,32,512]{2,1,0:T(8,128)S(1)} %get-tuple-element.110.q_ref.image, f32[16,32,512]{2,1,0:T(8,128)S(1)} %get-tuple-element.119.p_ref, ...), custom_call_target="tpu_custom_call", output_to_operand_aliasing={{}: (4, {})} | custom-call | flops 2875000064 | tf_op jit(solution)/shard_map/pallas_call | solution.py:557
  89.2 2.6 %collective-permute-start.14 = (f32[64,128]{1,0:T(8,128)S(1)}, f32[64,128]{1,0:T(8,128)S(1)}, u32[]{:S(2)}, u32[]{:S(2)}) collective-permute-start(f32[64,128]{1,0:T(8,128)S(1)} %add.24), channel_id=1, source_target_pairs={{0,24},{1,25},{2,26},{3,27},{4,28},{5,29},{6,30},{7,31},{8,16},{9,... | collective-permute-start | bytes 98312 | tf_op jit(solution)/shard_map/ppermute | solution.py:663
  91.9 2.6 %shard_map.149.refs_0_ = f32[8192,128]{1,0:T(8,128)S(1)} custom-call(s32[8192]{0:T(1024)S(1)} %copy-done.4, s32[16]{0:T(128)S(1)} %get-tuple-element.67.perm.perm_ref, f32[16,32,512]{2,1,0:T(8,128)S(1)} %get-tuple-element.110.q_ref.image, f32[16,32,512]{2,1,0:T(8,128)S(1)} %get-tuple-element.119.p_ref, ...), custom_call_target="tpu_custom_call", output_to_operand_aliasing={{}: (4, {})} | custom-call | flops 2875000064 | tf_op jit(solution)/shard_map/pallas_call | solution.py:557
  94.5 2.0 %collective-permute-start.15 = (f32[64,128]{1,0:T(8,128)S(1)}, f32[64,128]{1,0:T(8,128)S(1)}, u32[]{:S(2)}, u32[]{:S(2)}) collective-permute-start(f32[64,128]{1,0:T(8,128)S(1)} %add.25), channel_id=1, source_target_pairs={{0,32},{1,33},{2,34},{3,35},{4,36},{5,37},{6,38},{7,39},{8,40},{9,... | collective-permute-start | bytes 98312 | tf_op jit(solution)/shard_map/ppermute | solution.py:663
  96.5 2.1 %shard_map.150.rows_ref = f32[8192,128]{1,0:T(8,128)S(1)} custom-call(s32[8192]{0:T(1024)S(1)} %copy-done.4, s32[16]{0:T(128)S(1)} %get-tuple-element.67.perm.perm_ref, f32[16,32,512]{2,1,0:T(8,128)S(1)} %get-tuple-element.110.q_ref.image, f32[16,32,512]{2,1,0:T(8,128)S(1)} %get-tuple-element.119.p_ref, ...), custom_call_target="tpu_custom_call", output_to_operand_aliasing={{}: (4, {})} | custom-call | flops 2875000064 | tf_op jit(solution)/shard_map/pallas_call | solution.py:557
  98.7 3.9 %collective-permute-start.16 = (f32[64,128]{1,0:T(8,128)S(1)}, f32[64,128]{1,0:T(8,128)S(1)}, u32[]{:S(2)}, u32[]{:S(2)}) collective-permute-start(f32[64,128]{1,0:T(8,128)S(1)} %add.26), channel_id=1, source_target_pairs={{0,96},{1,97},{2,98},{3,99},{4,100},{5,101},{6,102},{7,103},{8,104... | collective-permute-start | bytes 98312 | tf_op jit(solution)/shard_map/ppermute | solution.py:663
  104.5 8.7 %shard_map.153 = (f32[32,8192]{1,0:T(8,128)}, f32[32,8192]{1,0:T(8,128)}) custom-call(f32[64,128]{1,0:T(8,128)S(1)} %add.27.gram, f32[32,8192]{1,0:T(8,128)S(1)} %copy-done, f32[64,4096]{1,0:T(8,128)S(1)} %shard_map.151.mapped0, f32[64,4096]{1,0:T(8,128)S(1)} %shard_map.152.mapped1), custom_call_target="tpu_custom_call" | custom-call | tf_op jit(solution)/shard_map/pallas_call | solution.py:651
  (54 shorter events, 6.6 us)
Async XLA Ops:
  21.0 8.5 %collective-permute-start = (bf16[1120,128]{1,0:T(8,128)(2,1)S(1)}, bf16[1120,128]{1,0:T(8,128)(2,1)S(1)}, u32[]{:S(2)}, u32[]{:S(2)}) collective-permute-start(bf16[1120,128]{1,0:T(8,128)(2,1)S(1)} %get-tuple-element.68), channel_id=1, source_target_pairs={{0,2},{1,3},{2,0},{3,1},{4,6},{5,7},{6,4},{7,5},{8,10},{9,11},{10,... | collective-permute-start | bytes 860168 | tf_op jit(solution)/shard_map/ppermute | solution.py:663
  29.5 7.0 %collective-permute-start.2 = (bf16[2,1120,128]{2,1,0:T(8,128)(2,1)S(1)}, bf16[2,1120,128]{2,1,0:T(8,128)(2,1)S(1)}, u32[]{:S(2)}, u32[]{:S(2)}) collective-permute-start(bf16[2,1120,128]{2,1,0:T(8,128)(2,1)S(1)} %pad_maximum_fusion.near_pair), channel_id=1, source_target_pairs={{0,1},{1,0},{2,3},{3,2},{4,5},{5,4},{6,7},{7,6},{8,9},{9,8},{10,11... | collective-permute-start | bytes 1720328 | tf_op jit(solution)/shard_map/ppermute | solution.py:663
  29.6 6.9 %collective-permute-start.1 = (bf16[2,224,128]{2,1,0:T(8,128)(2,1)S(1)}, bf16[2,224,128]{2,1,0:T(8,128)(2,1)S(1)}, u32[]{:S(2)}, u32[]{:S(2)}) collective-permute-start(bf16[2,224,128]{2,1,0:T(8,128)(2,1)S(1)} %fusion), channel_id=1, source_target_pairs={{0,6},{1,7},{2,4},{3,5},{4,2},{5,3},{6,0},{7,1},{8,14},{9,15},{10,... | collective-permute-start | bytes 344072 | tf_op jit(solution)/shard_map/ppermute | solution.py:663
  36.6 5.3 %copy-start.5 = (s32[4,4]{1,0:T(4,128)S(1)}, s32[4,4]{1,0:T(4,128)}, u32[]{:S(2)}) copy-start(s32[4,4]{1,0:T(4,128)} %lists.3) | copy-start | bytes 196
  36.6 7.6 %collective-permute-start.3 = (bf16[4,224,128]{2,1,0:T(8,128)(2,1)S(1)}, bf16[4,224,128]{2,1,0:T(8,128)(2,1)S(1)}, u32[]{:S(2)}, u32[]{:S(2)}) collective-permute-start(bf16[4,224,128]{2,1,0:T(8,128)(2,1)S(1)} %pad_maximum_fusion.2), channel_id=1, source_target_pairs={{0,8},{1,9},{2,10},{3,11},{4,12},{5,13},{6,14},{7,15},{8,0},{9,1},... | collective-permute-start | bytes 688136 | tf_op jit(solution)/shard_map/ppermute | solution.py:663
  41.9 4.3 %copy-start.1 = (bf16[16,256,512]{2,1,0:T(8,128)(2,1)S(1)}, bf16[16,256,512]{2,1,0:T(8,128)(2,1)}, u32[]{:S(2)}) copy-start(bf16[16,256,512]{2,1,0:T(8,128)(2,1)} %leaf_v.3) | copy-start | bytes 12582916
  41.9 4.3 %copy-start.2 = (bf16[4,256,1024]{2,1,0:T(8,128)(2,1)S(1)}, bf16[4,256,1024]{2,1,0:T(8,128)(2,1)}, u32[]{:S(2)}) copy-start(bf16[4,256,1024]{2,1,0:T(8,128)(2,1)} %mid_v.3) | copy-start | bytes 6291460
  41.9 4.3 %copy-start.3 = (bf16[4,256,256]{2,1,0:T(8,128)(2,1)S(1)}, bf16[4,256,256]{2,1,0:T(8,128)(2,1)}, u32[]{:S(2)}) copy-start(bf16[4,256,256]{2,1,0:T(8,128)(2,1)} %top_v.3) | copy-start | bytes 1572868
  41.9 4.3 %copy-start.6 = (s32[128,4]{0,1:T(4,128)S(1)}, s32[128,4]{0,1:T(4,128)}, u32[]{:S(2)}) copy-start(s32[128,4]{0,1:T(4,128)} %param.20) | copy-start | bytes 6148
  44.2 1.9 %collective-permute-start.4 = (bf16[8,224,128]{2,1,0:T(8,128)(2,1)S(1)}, bf16[8,224,128]{2,1,0:T(8,128)(2,1)S(1)}, u32[]{:S(2)}, u32[]{:S(2)}) collective-permute-start(bf16[8,224,128]{2,1,0:T(8,128)(2,1)S(1)} %pad_maximum_fusion.1.eight_a), channel_id=1, source_target_pairs={{0,1},{1,0},{2,3},{3,2},{4,5},{5,4},{6,7},{7,6},{8,9},{9,8},{10,11... | collective-permute-start | bytes 1376264 | tf_op jit(solution)/shard_map/ppermute | solution.py:663
  51.9 4.5 %collective-permute-start.5 = (bf16[320,128]{1,0:T(8,128)(2,1)S(1)}, bf16[320,128]{1,0:T(8,128)(2,1)S(1)}, u32[]{:S(2)}, u32[]{:S(2)}) collective-permute-start(bf16[320,128]{1,0:T(8,128)(2,1)S(1)} %get-tuple-element.97), channel_id=1, source_target_pairs={{0,2},{1,3},{2,0},{3,1},{4,6},{5,7},{6,4},{7,5},{8,10},{9,11},{10,... | collective-permute-start | bytes 245768 | tf_op jit(solution)/shard_map/ppermute | solution.py:663
  56.4 5.6 %collective-permute-start.6 = (bf16[2,64,128]{2,1,0:T(8,128)(2,1)S(1)}, bf16[2,64,128]{2,1,0:T(8,128)(2,1)S(1)}, u32[]{:S(2)}, u32[]{:S(2)}) collective-permute-start(bf16[2,64,128]{2,1,0:T(8,128)(2,1)S(1)} %fusion.1), channel_id=1, source_target_pairs={{0,6},{1,7},{2,4},{3,5},{4,2},{5,3},{6,0},{7,1},{8,14},{9,15},{10,... | collective-permute-start | bytes 98312 | tf_op jit(solution)/shard_map/ppermute | solution.py:663
  59.3 2.7 %collective-permute-start.7 = (bf16[2,320,128]{2,1,0:T(8,128)(2,1)S(1)}, bf16[2,320,128]{2,1,0:T(8,128)(2,1)S(1)}, u32[]{:S(2)}, u32[]{:S(2)}) collective-permute-start(bf16[2,320,128]{2,1,0:T(8,128)(2,1)S(1)} %pad_maximum_fusion.3.near_pair), channel_id=1, source_target_pairs={{0,1},{1,0},{2,3},{3,2},{4,5},{5,4},{6,7},{7,6},{8,9},{9,8},{10,11... | collective-permute-start | bytes 491528 | tf_op jit(solution)/shard_map/ppermute | solution.py:663
  62.1 5.1 %collective-permute-start.8 = (bf16[4,64,128]{2,1,0:T(8,128)(2,1)S(1)}, bf16[4,64,128]{2,1,0:T(8,128)(2,1)S(1)}, u32[]{:S(2)}, u32[]{:S(2)}) collective-permute-start(bf16[4,64,128]{2,1,0:T(8,128)(2,1)S(1)} %pad_maximum_fusion.5), channel_id=1, source_target_pairs={{0,8},{1,9},{2,10},{3,11},{4,12},{5,13},{6,14},{7,15},{8,0},{9,1},... | collective-permute-start | bytes 196616 | tf_op jit(solution)/shard_map/ppermute | solution.py:663
  67.3 2.3 %collective-permute-start.9 = (bf16[8,64,128]{2,1,0:T(8,128)(2,1)S(1)}, bf16[8,64,128]{2,1,0:T(8,128)(2,1)S(1)}, u32[]{:S(2)}, u32[]{:S(2)}) collective-permute-start(bf16[8,64,128]{2,1,0:T(8,128)(2,1)S(1)} %pad_maximum_fusion.4.eight_a), channel_id=1, source_target_pairs={{0,1},{1,0},{2,3},{3,2},{4,5},{5,4},{6,7},{7,6},{8,9},{9,8},{10,11... | collective-permute-start | bytes 393224 | tf_op jit(solution)/shard_map/ppermute | solution.py:663
  69.5 4.4 %copy-start.4 = (s32[8192]{0:T(1024)S(1)}, s32[8192]{0:T(1024)}, u32[]{:S(2)}) copy-start(s32[8192]{0:T(1024)} %order_ref.11) | copy-start | bytes 98308
  73.6 2.5 %collective-permute-start.10 = (f32[64,128]{1,0:T(8,128)S(1)}, f32[64,128]{1,0:T(8,128)S(1)}, u32[]{:S(2)}, u32[]{:S(2)}) collective-permute-start(f32[64,128]{1,0:T(8,128)S(1)} %get-tuple-element.118), channel_id=1, source_target_pairs={{0,1},{1,0},{2,3},{3,2},{4,5},{5,4},{6,7},{7,6},{8,9},{9,8},{10,11... | collective-permute-start | bytes 98312 | tf_op jit(solution)/shard_map/ppermute | solution.py:663
  76.1 4.0 %collective-permute-start.11 = (f32[64,128]{1,0:T(8,128)S(1)}, f32[64,128]{1,0:T(8,128)S(1)}, u32[]{:S(2)}, u32[]{:S(2)}) collective-permute-start(f32[64,128]{1,0:T(8,128)S(1)} %add.21), channel_id=1, source_target_pairs={{0,2},{1,3},{2,0},{3,1},{4,6},{5,7},{6,4},{7,5},{8,10},{9,11},{10,... | collective-permute-start | bytes 98312 | tf_op jit(solution)/shard_map/ppermute | solution.py:663
  80.2 5.1 %collective-permute-start.12 = (f32[64,128]{1,0:T(8,128)S(1)}, f32[64,128]{1,0:T(8,128)S(1)}, u32[]{:S(2)}, u32[]{:S(2)}) collective-permute-start(f32[64,128]{1,0:T(8,128)S(1)} %add.22), channel_id=1, source_target_pairs={{0,6},{1,7},{2,4},{3,5},{4,2},{5,3},{6,0},{7,1},{8,14},{9,15},{10,... | collective-permute-start | bytes 98312 | tf_op jit(solution)/shard_map/ppermute | solution.py:663
  85.3 3.9 %collective-permute-start.13 = (f32[64,128]{1,0:T(8,128)S(1)}, f32[64,128]{1,0:T(8,128)S(1)}, u32[]{:S(2)}, u32[]{:S(2)}) collective-permute-start(f32[64,128]{1,0:T(8,128)S(1)} %add.23), channel_id=1, source_target_pairs={{0,8},{1,9},{2,10},{3,11},{4,12},{5,13},{6,14},{7,15},{8,0},{9,1},... | collective-permute-start | bytes 98312 | tf_op jit(solution)/shard_map/ppermute | solution.py:663
  89.2 5.3 %collective-permute-start.14 = (f32[64,128]{1,0:T(8,128)S(1)}, f32[64,128]{1,0:T(8,128)S(1)}, u32[]{:S(2)}, u32[]{:S(2)}) collective-permute-start(f32[64,128]{1,0:T(8,128)S(1)} %add.24), channel_id=1, source_target_pairs={{0,24},{1,25},{2,26},{3,27},{4,28},{5,29},{6,30},{7,31},{8,16},{9,... | collective-permute-start | bytes 98312 | tf_op jit(solution)/shard_map/ppermute | solution.py:663
  94.5 4.1 %collective-permute-start.15 = (f32[64,128]{1,0:T(8,128)S(1)}, f32[64,128]{1,0:T(8,128)S(1)}, u32[]{:S(2)}, u32[]{:S(2)}) collective-permute-start(f32[64,128]{1,0:T(8,128)S(1)} %add.25), channel_id=1, source_target_pairs={{0,32},{1,33},{2,34},{3,35},{4,36},{5,37},{6,38},{7,39},{8,40},{9,... | collective-permute-start | bytes 98312 | tf_op jit(solution)/shard_map/ppermute | solution.py:663
  98.7 5.8 %collective-permute-start.16 = (f32[64,128]{1,0:T(8,128)S(1)}, f32[64,128]{1,0:T(8,128)S(1)}, u32[]{:S(2)}, u32[]{:S(2)}) collective-permute-start(f32[64,128]{1,0:T(8,128)S(1)} %add.26), channel_id=1, source_target_pairs={{0,96},{1,97},{2,98},{3,99},{4,100},{5,101},{6,102},{7,103},{8,104... | collective-permute-start | bytes 98312 | tf_op jit(solution)/shard_map/ppermute | solution.py:663
  103.2 1.3 %copy-start = (f32[32,8192]{1,0:T(8,128)S(1)}, f32[32,8192]{1,0:T(8,128)}, u32[]{:S(2)}) copy-start(f32[32,8192]{1,0:T(8,128)} %rhs.1) | copy-start | bytes 3145732

commit v4 on v3

--- a/solution.py
+++ b/solution.py
@@ -709,10 +709,10 @@
 
     def again_and_products(inputs):
         early.append(early_products(right, *inputs))
-        return again(1)(inputs)
+        return again(2)(inputs)
 
     eights, mid_far, near = gather_pools(
-        payload, S1_ROWS, (image,), [again(0), again_and_products, again(2), again(3)],
+        payload, S1_ROWS, (image,), [again(0, 1), again_and_products, again(3), again()],
         lambda *pairs: mid_second(far_mid, *pairs, mid_tiles),
     )
     second, gram = far_second(

time: 114 us -> 112 us (0.982)
  waiting for transfers between devices: 7.06 us -> 5.61 us
    ppermute x17, waiting for transfers between devices: 7.06 us -> 5.61 us  [swapped(): lax.ppermute(value, AXES, [(source, source ^ mask) for source in range(co...]
  transfers between devices with their start and end apart: 17 -> 17, of which waited for: 8 -> 10; matrix products, arithmetic and copies ran while one was open for 0% -> 0% of each run, Pallas kernels for 36% -> 37%
where the time goes in v4:
time: 112 us
  Pallas kernels  79.9 us (71%)
  starting transfers between devices  25.2 us (22%)
  waiting for transfers between devices  5.61 us (5%)
  between operations  1.12 us (1%)
    ppermute x17, starting transfers between devices, swapped(): lax.ppermute(value, AXES, [(source, source ^ mask) for source in range(co...  25.2 us
    pallas_call x1, Pallas kernels, setup(): pl.pallas_call(setup_kernel, out_shape=[jax.ShapeDtypeStruct((LEAVES, LEA...  20.3 us
    pallas_call x6, Pallas kernels, put_back(): pl.pallas_call(kernel, out_shape=jax.ShapeDtypeStruct((SPAN, LANES), f32)...  14.9 us
    pallas_call x4, Pallas kernels, near_first(): pl.pallas_call(kernel, out_shape=[jax.ShapeDtypeStruct((LIST, SIDES, LEAF...  12.9 us
    pallas_call x1, Pallas kernels, finish(): pl.pallas_call(finish_kernel, out_shape=[jax.ShapeDtypeStruct((SIDES, SPA...  8.72 us
    pallas_call x4, Pallas kernels, near_second(): pl.pallas_call(kernel, out_shape=jax.ShapeDtypeStruct((LIST, SIDES, LEAF)...  7.85 us
    pallas_call x1, Pallas kernels, far_first(): pl.pallas_call(far_first_kernel, out_shape=[jax.ShapeDtypeStruct((LEAVES,...  5.7 us
    ppermute x17, waiting for transfers between devices, swapped(): lax.ppermute(value, AXES, [(source, source ^ mask) for source in range(co...  5.61 us
  transfers between devices with their start and end apart: 17, of which 10 were waited for; matrix products, arithmetic and copies ran while one was open for 0% of the time, Pallas kernels for 37%

profile of v4, /device:TPU:0, one launch (start us, length us, event | category | flops | bytes accessed | tf_op | source)
XLA Modules:
  0.0 112.2 jit_solution(9381769116305565466)
XLA Ops:
  0.6 20.3 %shard_map.131 = (bf16[16,512,128]{2,1,0:T(8,128)(2,1)S(1)}, bf16[16,512,128]{2,1,0:T(8,128)(2,1)S(1)}, f32[16,32,512]{2,1,0:T(8,128)S(1)}, bf16[1120,128]{1,0:T(8,128)(2,1)S(1)}, s32[16]{0:T(128)S(1)}) custom-call(s32[16,256]{1,0:T(8,128)} %leaf_skel_hbm.1, s32[4,256]{1,0:T(4,128)} %skel_mid_hbm.1, s32[4,16]{1,0:T(4,128)} %bitcast.16, s32[8192]{0:T(1024)} %order_ref.11, ...), custom_call_target="tpu_custom_call" | custom-call | flops 23000000512 | tf_op jit(solution)/shard_map/pallas_call | solution.py:277
  21.0 1.7 %collective-permute-start = (bf16[1120,128]{1,0:T(8,128)(2,1)S(1)}, bf16[1120,128]{1,0:T(8,128)(2,1)S(1)}, u32[]{:S(2)}, u32[]{:S(2)}) collective-permute-start(bf16[1120,128]{1,0:T(8,128)(2,1)S(1)} %get-tuple-element.66), channel_id=1, source_target_pairs={{0,2},{1,3},{2,0},{3,1},{4,6},{5,7},{6,4},{7,5},{8,10},{9,11},{10,... | collective-permute-start | bytes 860168 | tf_op jit(solution)/shard_map/ppermute | solution.py:663
  22.6 3.2 %shard_map.133 = (f32[4,32,512]{2,1,0:T(8,128)S(1)}, bf16[10,512,512]{2,1,0:T(8,128)(2,1)S(1)}) custom-call(bf16[16,512,128]{2,1,0:T(8,128)(2,1)S(1)} %get-tuple-element.84.a_ref, bf16[16,512,128]{2,1,0:T(8,128)(2,1)S(1)} %get-tuple-element.85.b_ref, f32[16,32,512]{2,1,0:T(8,128)S(1)} %get-tuple-element.86.r_ref.right), custom_call_target="tpu_custom_call" | custom-call | flops 3795000064 | tf_op jit(solution)/shard_map/pallas_call | solution.py:323
  25.9 3.2 %shard_map.132 = (f32[4,32,512]{2,1,0:T(8,128)S(1)}, bf16[10,512,512]{2,1,0:T(8,128)(2,1)S(1)}) custom-call(bf16[16,512,128]{2,1,0:T(8,128)(2,1)S(1)} %get-tuple-element.84.a_ref, bf16[16,512,128]{2,1,0:T(8,128)(2,1)S(1)} %get-tuple-element.85.b_ref, f32[16,32,512]{2,1,0:T(8,128)S(1)} %get-tuple-element.86.r_ref.right), custom_call_target="tpu_custom_call" | custom-call | flops 3795000064 | tf_op jit(solution)/shard_map/pallas_call | solution.py:323
  29.6 3.1 %collective-permute-start.1 = (bf16[2,224,128]{2,1,0:T(8,128)(2,1)S(1)}, bf16[2,224,128]{2,1,0:T(8,128)(2,1)S(1)}, u32[]{:S(2)}, u32[]{:S(2)}) collective-permute-start(bf16[2,224,128]{2,1,0:T(8,128)(2,1)S(1)} %fusion), channel_id=1, source_target_pairs={{0,6},{1,7},{2,4},{3,5},{4,2},{5,3},{6,0},{7,1},{8,14},{9,15},{10,... | collective-permute-start | bytes 344072 | tf_op jit(solution)/shard_map/ppermute | solution.py:663
  32.7 3.2 %shard_map.134 = (f32[4,32,512]{2,1,0:T(8,128)S(1)}, bf16[10,512,512]{2,1,0:T(8,128)(2,1)S(1)}) custom-call(bf16[16,512,128]{2,1,0:T(8,128)(2,1)S(1)} %get-tuple-element.84.a_ref, bf16[16,512,128]{2,1,0:T(8,128)(2,1)S(1)} %get-tuple-element.85.b_ref, f32[16,32,512]{2,1,0:T(8,128)S(1)} %get-tuple-element.86.r_ref.right), custom_call_target="tpu_custom_call" | custom-call | flops 3795000064 | tf_op jit(solution)/shard_map/pallas_call | solution.py:323
  36.6 2.0 %collective-permute-start.3 = (bf16[4,224,128]{2,1,0:T(8,128)(2,1)S(1)}, bf16[4,224,128]{2,1,0:T(8,128)(2,1)S(1)}, u32[]{:S(2)}, u32[]{:S(2)}) collective-permute-start(bf16[4,224,128]{2,1,0:T(8,128)(2,1)S(1)} %pad_maximum_fusion.2), channel_id=1, source_target_pairs={{0,8},{1,9},{2,10},{3,11},{4,12},{5,13},{6,14},{7,15},{8,0},{9,1},... | collective-permute-start | bytes 688136 | tf_op jit(solution)/shard_map/ppermute | solution.py:663
  38.6 3.2 %shard_map.136 = (f32[4,32,512]{2,1,0:T(8,128)S(1)}, bf16[10,512,512]{2,1,0:T(8,128)(2,1)S(1)}) custom-call(bf16[16,512,128]{2,1,0:T(8,128)(2,1)S(1)} %get-tuple-element.84.a_ref, bf16[16,512,128]{2,1,0:T(8,128)(2,1)S(1)} %get-tuple-element.85.b_ref, f32[16,32,512]{2,1,0:T(8,128)S(1)} %get-tuple-element.86.r_ref.right), custom_call_target="tpu_custom_call" | custom-call | flops 3795000064 | tf_op jit(solution)/shard_map/pallas_call | solution.py:323
  41.9 2.3 %shard_map.135 = (f32[4,32,256]{2,1,0:T(8,128)S(1)}, bf16[16,256,256]{2,1,0:T(8,128)(2,1)S(1)}) custom-call(s32[4,4]{1,0:T(4,128)S(1)} %copy-done.5, bf16[2,1120,128]{2,1,0:T(8,128)(2,1)S(1)} %pad_maximum_fusion.near_pair, bf16[2,1120,128]{2,1,0:T(8,128)(2,1)S(1)} %collective-permute-done.2.far_pair), custom_call_target="tpu_custom_call" | custom-call | flops 3449999872 | tf_op jit(solution)/shard_map/pallas_call | solution.py:402
  44.3 1.8 %collective-permute-done.4.eight_b = bf16[8,224,128]{2,1,0:T(8,128)(2,1)S(1)} collective-permute-done((bf16[8,224,128]{2,1,0:T(8,128)(2,1)S(1)}, bf16[8,224,128]{2,1,0:T(8,128)(2,1)S(1)}, u32[]{:S(2)}, u32[]{:S(2)}) %collective-permute-start.4) | collective-permute-done | bytes 458784 | tf_op jit(solution)/shard_map/ppermute | solution.py:663
  46.2 5.7 %shard_map.137 = (f32[16,32,512]{2,1,0:T(8,128)S(1)}, bf16[320,128]{1,0:T(8,128)(2,1)S(1)}, bf16[4,256,256]{2,1,0:T(8,128)(2,1)S(1)}) custom-call(s32[4,128]{1,0:T(4,128)S(1)} %bitcast.10, s32[16]{0:T(128)S(1)} %get-tuple-element.65.perm.perm_ref, bf16[8,224,128]{2,1,0:T(8,128)(2,1)S(1)} %pad_maximum_fusion.1.eight_a, ...), custom_call_target="tpu_custom_call" | custom-call | flops 9200000000 | tf_op jit(solution)/shard_map/pallas_call | solution.py:478
  52.3 2.0 %shard_map.139.near1 = f32[4,32,512]{2,1,0:T(8,128)S(1)} custom-call(bf16[10,512,512]{2,1,0:T(8,128)(2,1)S(1)} %get-tuple-element.98.tiles_ref, f32[16,32,512]{2,1,0:T(8,128)S(1)} %get-tuple-element.106.q_ref.image), custom_call_target="tpu_custom_call" | custom-call | flops 2990000128 | tf_op jit(solution)/shard_map/pallas_call | solution.py:341
  54.2 2.0 %shard_map.138.near0 = f32[4,32,512]{2,1,0:T(8,128)S(1)} custom-call(bf16[10,512,512]{2,1,0:T(8,128)(2,1)S(1)} %get-tuple-element.96.tiles_ref, f32[16,32,512]{2,1,0:T(8,128)S(1)} %get-tuple-element.106.q_ref.image), custom_call_target="tpu_custom_call" | custom-call | flops 2990000128 | tf_op jit(solution)/shard_map/pallas_call | solution.py:341
  56.4 2.9 %collective-permute-start.6 = (bf16[2,64,128]{2,1,0:T(8,128)(2,1)S(1)}, bf16[2,64,128]{2,1,0:T(8,128)(2,1)S(1)}, u32[]{:S(2)}, u32[]{:S(2)}) collective-permute-start(bf16[2,64,128]{2,1,0:T(8,128)(2,1)S(1)} %fusion.1), channel_id=1, source_target_pairs={{0,6},{1,7},{2,4},{3,5},{4,2},{5,3},{6,0},{7,1},{8,14},{9,15},{10,... | collective-permute-start | bytes 98312 | tf_op jit(solution)/shard_map/ppermute | solution.py:663
  59.3 2.0 %shard_map.140.near2 = f32[4,32,512]{2,1,0:T(8,128)S(1)} custom-call(bf16[10,512,512]{2,1,0:T(8,128)(2,1)S(1)} %get-tuple-element.100.tiles_ref, f32[16,32,512]{2,1,0:T(8,128)S(1)} %get-tuple-element.106.q_ref.image), custom_call_target="tpu_custom_call" | custom-call | flops 2990000128 | tf_op jit(solution)/shard_map/pallas_call | solution.py:341
  61.7 1.9 %collective-permute-start.8 = (bf16[4,64,128]{2,1,0:T(8,128)(2,1)S(1)}, bf16[4,64,128]{2,1,0:T(8,128)(2,1)S(1)}, u32[]{:S(2)}, u32[]{:S(2)}) collective-permute-start(bf16[4,64,128]{2,1,0:T(8,128)(2,1)S(1)} %pad_maximum_fusion.5), channel_id=1, source_target_pairs={{0,8},{1,9},{2,10},{3,11},{4,12},{5,13},{6,14},{7,15},{8,0},{9,1},... | collective-permute-start | bytes 196616 | tf_op jit(solution)/shard_map/ppermute | solution.py:663
  63.6 2.0 %shard_map.142.near3 = f32[4,32,512]{2,1,0:T(8,128)S(1)} custom-call(bf16[10,512,512]{2,1,0:T(8,128)(2,1)S(1)} %get-tuple-element.105.tiles_ref, f32[16,32,512]{2,1,0:T(8,128)S(1)} %get-tuple-element.106.q_ref.image), custom_call_target="tpu_custom_call" | custom-call | flops 2990000128 | tf_op jit(solution)/shard_map/pallas_call | solution.py:341
  65.5 1.3 %shard_map.141.mid_far = f32[4,32,256]{2,1,0:T(8,128)S(1)} custom-call(s32[4,4]{1,0:T(4,128)S(1)} %copy-done.5, bf16[2,320,128]{2,1,0:T(8,128)(2,1)S(1)} %pad_maximum_fusion.3.near_pair, bf16[2,320,128]{2,1,0:T(8,128)(2,1)S(1)} %collective-permute-done.7.far_pair, bf16[16,256,256]{2,1,0:T(8,128)(2,1)S(1)} %get-tuple-element.104.tiles_ref), custom_call_target="tpu_custom_call" | custom-call | flops 1150000000 | tf_op jit(solution)/shard_map/pallas_call | solution.py:426
  67.0 0.7 shard_map.143.early
  68.3 4.0 %shard_map.144 = (f32[16,32,512]{2,1,0:T(8,128)S(1)}, f32[64,128]{1,0:T(8,128)S(1)}) custom-call(s32[4,128]{1,0:T(4,128)S(1)} %bitcast.11, s32[16]{0:T(128)S(1)} %get-tuple-element.65.perm.perm_ref, bf16[8,64,128]{2,1,0:T(8,128)(2,1)S(1)} %pad_maximum_fusion.4.eight_a, bf16[8,64,128]{2,1,0:T(8,128)(2,1)S(1)} %collective-permute-done.9.eight_b, ...), custom_call_target="tpu_custom_call" | custom-call | flops 9200000000 | tf_op jit(solution)/shard_map/pallas_call | solution.py:517
  72.6 2.1 %shard_map.145.refs_0_ = f32[8192,128]{1,0:T(8,128)S(1)} custom-call(s32[8192]{0:T(1024)S(1)} %copy-done.4, s32[16]{0:T(128)S(1)} %get-tuple-element.65.perm.perm_ref, f32[16,32,512]{2,1,0:T(8,128)S(1)} %get-tuple-element.106.q_ref.image, f32[16,32,512]{2,1,0:T(8,128)S(1)} %get-tuple-element.115.p_ref), custom_call_target="tpu_custom_call" | custom-call | flops 2875000064 | tf_op jit(solution)/shard_map/pallas_call | solution.py:557
  75.5 2.6 %shard_map.146.refs_0_ = f32[8192,128]{1,0:T(8,128)S(1)} custom-call(s32[8192]{0:T(1024)S(1)} %copy-done.4, s32[16]{0:T(128)S(1)} %get-tuple-element.65.perm.perm_ref, f32[16,32,512]{2,1,0:T(8,128)S(1)} %get-tuple-element.106.q_ref.image, f32[16,32,512]{2,1,0:T(8,128)S(1)} %get-tuple-element.115.p_ref, ...), custom_call_target="tpu_custom_call", output_to_operand_aliasing={{}: (4, {})} | custom-call | flops 2875000064 | tf_op jit(solution)/shard_map/pallas_call | solution.py:557
  78.8 2.8 %collective-permute-start.12 = (f32[64,128]{1,0:T(8,128)S(1)}, f32[64,128]{1,0:T(8,128)S(1)}, u32[]{:S(2)}, u32[]{:S(2)}) collective-permute-start(f32[64,128]{1,0:T(8,128)S(1)} %add.22), channel_id=1, source_target_pairs={{0,6},{1,7},{2,4},{3,5},{4,2},{5,3},{6,0},{7,1},{8,14},{9,15},{10,... | collective-permute-start | bytes 98312 | tf_op jit(solution)/shard_map/ppermute | solution.py:663
  81.5 2.6 %shard_map.147.refs_0_ = f32[8192,128]{1,0:T(8,128)S(1)} custom-call(s32[8192]{0:T(1024)S(1)} %copy-done.4, s32[16]{0:T(128)S(1)} %get-tuple-element.65.perm.perm_ref, f32[16,32,512]{2,1,0:T(8,128)S(1)} %get-tuple-element.106.q_ref.image, f32[16,32,512]{2,1,0:T(8,128)S(1)} %get-tuple-element.115.p_ref, ...), custom_call_target="tpu_custom_call", output_to_operand_aliasing={{}: (4, {})} | custom-call | flops 2875000064 | tf_op jit(solution)/shard_map/pallas_call | solution.py:557
  84.2 1.1 collective-permute-start.13
  85.3 2.6 %shard_map.148.refs_0_ = f32[8192,128]{1,0:T(8,128)S(1)} custom-call(s32[8192]{0:T(1024)S(1)} %copy-done.4, s32[16]{0:T(128)S(1)} %get-tuple-element.65.perm.perm_ref, f32[16,32,512]{2,1,0:T(8,128)S(1)} %get-tuple-element.106.q_ref.image, f32[16,32,512]{2,1,0:T(8,128)S(1)} %get-tuple-element.115.p_ref, ...), custom_call_target="tpu_custom_call", output_to_operand_aliasing={{}: (4, {})} | custom-call | flops 2875000064 | tf_op jit(solution)/shard_map/pallas_call | solution.py:557
  88.2 2.4 %collective-permute-start.14 = (f32[64,128]{1,0:T(8,128)S(1)}, f32[64,128]{1,0:T(8,128)S(1)}, u32[]{:S(2)}, u32[]{:S(2)}) collective-permute-start(f32[64,128]{1,0:T(8,128)S(1)} %add.24), channel_id=1, source_target_pairs={{0,24},{1,25},{2,26},{3,27},{4,28},{5,29},{6,30},{7,31},{8,16},{9,... | collective-permute-start | bytes 98312 | tf_op jit(solution)/shard_map/ppermute | solution.py:663
  90.6 2.6 %shard_map.149.refs_0_ = f32[8192,128]{1,0:T(8,128)S(1)} custom-call(s32[8192]{0:T(1024)S(1)} %copy-done.4, s32[16]{0:T(128)S(1)} %get-tuple-element.65.perm.perm_ref, f32[16,32,512]{2,1,0:T(8,128)S(1)} %get-tuple-element.106.q_ref.image, f32[16,32,512]{2,1,0:T(8,128)S(1)} %get-tuple-element.115.p_ref, ...), custom_call_target="tpu_custom_call", output_to_operand_aliasing={{}: (4, {})} | custom-call | flops 2875000064 | tf_op jit(solution)/shard_map/pallas_call | solution.py:557
  93.3 2.0 %collective-permute-start.15 = (f32[64,128]{1,0:T(8,128)S(1)}, f32[64,128]{1,0:T(8,128)S(1)}, u32[]{:S(2)}, u32[]{:S(2)}) collective-permute-start(f32[64,128]{1,0:T(8,128)S(1)} %add.25), channel_id=1, source_target_pairs={{0,32},{1,33},{2,34},{3,35},{4,36},{5,37},{6,38},{7,39},{8,40},{9,... | collective-permute-start | bytes 98312 | tf_op jit(solution)/shard_map/ppermute | solution.py:663
  95.3 2.1 %shard_map.150.rows_ref = f32[8192,128]{1,0:T(8,128)S(1)} custom-call(s32[8192]{0:T(1024)S(1)} %copy-done.4, s32[16]{0:T(128)S(1)} %get-tuple-element.65.perm.perm_ref, f32[16,32,512]{2,1,0:T(8,128)S(1)} %get-tuple-element.106.q_ref.image, f32[16,32,512]{2,1,0:T(8,128)S(1)} %get-tuple-element.115.p_ref, ...), custom_call_target="tpu_custom_call", output_to_operand_aliasing={{}: (4, {})} | custom-call | flops 2875000064 | tf_op jit(solution)/shard_map/pallas_call | solution.py:557
  97.5 3.9 %collective-permute-start.16 = (f32[64,128]{1,0:T(8,128)S(1)}, f32[64,128]{1,0:T(8,128)S(1)}, u32[]{:S(2)}, u32[]{:S(2)}) collective-permute-start(f32[64,128]{1,0:T(8,128)S(1)} %add.26), channel_id=1, source_target_pairs={{0,96},{1,97},{2,98},{3,99},{4,100},{5,101},{6,102},{7,103},{8,104... | collective-permute-start | bytes 98312 | tf_op jit(solution)/shard_map/ppermute | solution.py:663
  103.3 8.7 %shard_map.153 = (f32[32,8192]{1,0:T(8,128)}, f32[32,8192]{1,0:T(8,128)}) custom-call(f32[64,128]{1,0:T(8,128)S(1)} %add.27.gram, f32[32,8192]{1,0:T(8,128)S(1)} %copy-done, f32[64,4096]{1,0:T(8,128)S(1)} %shard_map.151.mapped0, f32[64,4096]{1,0:T(8,128)S(1)} %shard_map.152.mapped1), custom_call_target="tpu_custom_call" | custom-call | tf_op jit(solution)/shard_map/pallas_call | solution.py:651
  (54 shorter events, 6.8 us)
Async XLA Ops:
  21.0 8.5 %collective-permute-start = (bf16[1120,128]{1,0:T(8,128)(2,1)S(1)}, bf16[1120,128]{1,0:T(8,128)(2,1)S(1)}, u32[]{:S(2)}, u32[]{:S(2)}) collective-permute-start(bf16[1120,128]{1,0:T(8,128)(2,1)S(1)} %get-tuple-element.66), channel_id=1, source_target_pairs={{0,2},{1,3},{2,0},{3,1},{4,6},{5,7},{6,4},{7,5},{8,10},{9,11},{10,... | collective-permute-start | bytes 860168 | tf_op jit(solution)/shard_map/ppermute | solution.py:663
  29.5 7.0 %collective-permute-start.2 = (bf16[2,1120,128]{2,1,0:T(8,128)(2,1)S(1)}, bf16[2,1120,128]{2,1,0:T(8,128)(2,1)S(1)}, u32[]{:S(2)}, u32[]{:S(2)}) collective-permute-start(bf16[2,1120,128]{2,1,0:T(8,128)(2,1)S(1)} %pad_maximum_fusion.near_pair), channel_id=1, source_target_pairs={{0,1},{1,0},{2,3},{3,2},{4,5},{5,4},{6,7},{7,6},{8,9},{9,8},{10,11... | collective-permute-start | bytes 1720328 | tf_op jit(solution)/shard_map/ppermute | solution.py:663
  29.6 6.9 %collective-permute-start.1 = (bf16[2,224,128]{2,1,0:T(8,128)(2,1)S(1)}, bf16[2,224,128]{2,1,0:T(8,128)(2,1)S(1)}, u32[]{:S(2)}, u32[]{:S(2)}) collective-permute-start(bf16[2,224,128]{2,1,0:T(8,128)(2,1)S(1)} %fusion), channel_id=1, source_target_pairs={{0,6},{1,7},{2,4},{3,5},{4,2},{5,3},{6,0},{7,1},{8,14},{9,15},{10,... | collective-permute-start | bytes 344072 | tf_op jit(solution)/shard_map/ppermute | solution.py:663
  36.6 5.3 %copy-start.5 = (s32[4,4]{1,0:T(4,128)S(1)}, s32[4,4]{1,0:T(4,128)}, u32[]{:S(2)}) copy-start(s32[4,4]{1,0:T(4,128)} %lists.3) | copy-start | bytes 196
  36.6 7.6 %collective-permute-start.3 = (bf16[4,224,128]{2,1,0:T(8,128)(2,1)S(1)}, bf16[4,224,128]{2,1,0:T(8,128)(2,1)S(1)}, u32[]{:S(2)}, u32[]{:S(2)}) collective-permute-start(bf16[4,224,128]{2,1,0:T(8,128)(2,1)S(1)} %pad_maximum_fusion.2), channel_id=1, source_target_pairs={{0,8},{1,9},{2,10},{3,11},{4,12},{5,13},{6,14},{7,15},{8,0},{9,1},... | collective-permute-start | bytes 688136 | tf_op jit(solution)/shard_map/ppermute | solution.py:663
  41.9 4.3 %copy-start.1 = (bf16[16,256,512]{2,1,0:T(8,128)(2,1)S(1)}, bf16[16,256,512]{2,1,0:T(8,128)(2,1)}, u32[]{:S(2)}) copy-start(bf16[16,256,512]{2,1,0:T(8,128)(2,1)} %leaf_v.3) | copy-start | bytes 12582916
  41.9 4.3 %copy-start.2 = (bf16[4,256,1024]{2,1,0:T(8,128)(2,1)S(1)}, bf16[4,256,1024]{2,1,0:T(8,128)(2,1)}, u32[]{:S(2)}) copy-start(bf16[4,256,1024]{2,1,0:T(8,128)(2,1)} %mid_v.3) | copy-start | bytes 6291460
  41.9 4.3 %copy-start.3 = (bf16[4,256,256]{2,1,0:T(8,128)(2,1)S(1)}, bf16[4,256,256]{2,1,0:T(8,128)(2,1)}, u32[]{:S(2)}) copy-start(bf16[4,256,256]{2,1,0:T(8,128)(2,1)} %top_v.3) | copy-start | bytes 1572868
  41.9 4.3 %copy-start.6 = (s32[128,4]{0,1:T(4,128)S(1)}, s32[128,4]{0,1:T(4,128)}, u32[]{:S(2)}) copy-start(s32[128,4]{0,1:T(4,128)} %param.20) | copy-start | bytes 6148
  44.2 1.9 %collective-permute-start.4 = (bf16[8,224,128]{2,1,0:T(8,128)(2,1)S(1)}, bf16[8,224,128]{2,1,0:T(8,128)(2,1)S(1)}, u32[]{:S(2)}, u32[]{:S(2)}) collective-permute-start(bf16[8,224,128]{2,1,0:T(8,128)(2,1)S(1)} %pad_maximum_fusion.1.eight_a), channel_id=1, source_target_pairs={{0,1},{1,0},{2,3},{3,2},{4,5},{5,4},{6,7},{7,6},{8,9},{9,8},{10,11... | collective-permute-start | bytes 1376264 | tf_op jit(solution)/shard_map/ppermute | solution.py:663
  51.9 4.5 %collective-permute-start.5 = (bf16[320,128]{1,0:T(8,128)(2,1)S(1)}, bf16[320,128]{1,0:T(8,128)(2,1)S(1)}, u32[]{:S(2)}, u32[]{:S(2)}) collective-permute-start(bf16[320,128]{1,0:T(8,128)(2,1)S(1)} %get-tuple-element.95), channel_id=1, source_target_pairs={{0,2},{1,3},{2,0},{3,1},{4,6},{5,7},{6,4},{7,5},{8,10},{9,11},{10,... | collective-permute-start | bytes 245768 | tf_op jit(solution)/shard_map/ppermute | solution.py:663
  56.4 5.2 %collective-permute-start.6 = (bf16[2,64,128]{2,1,0:T(8,128)(2,1)S(1)}, bf16[2,64,128]{2,1,0:T(8,128)(2,1)S(1)}, u32[]{:S(2)}, u32[]{:S(2)}) collective-permute-start(bf16[2,64,128]{2,1,0:T(8,128)(2,1)S(1)} %fusion.1), channel_id=1, source_target_pairs={{0,6},{1,7},{2,4},{3,5},{4,2},{5,3},{6,0},{7,1},{8,14},{9,15},{10,... | collective-permute-start | bytes 98312 | tf_op jit(solution)/shard_map/ppermute | solution.py:663
  59.3 2.3 %collective-permute-start.7 = (bf16[2,320,128]{2,1,0:T(8,128)(2,1)S(1)}, bf16[2,320,128]{2,1,0:T(8,128)(2,1)S(1)}, u32[]{:S(2)}, u32[]{:S(2)}) collective-permute-start(bf16[2,320,128]{2,1,0:T(8,128)(2,1)S(1)} %pad_maximum_fusion.3.near_pair), channel_id=1, source_target_pairs={{0,1},{1,0},{2,3},{3,2},{4,5},{5,4},{6,7},{7,6},{8,9},{9,8},{10,11... | collective-permute-start | bytes 491528 | tf_op jit(solution)/shard_map/ppermute | solution.py:663
  61.7 5.2 %collective-permute-start.8 = (bf16[4,64,128]{2,1,0:T(8,128)(2,1)S(1)}, bf16[4,64,128]{2,1,0:T(8,128)(2,1)S(1)}, u32[]{:S(2)}, u32[]{:S(2)}) collective-permute-start(bf16[4,64,128]{2,1,0:T(8,128)(2,1)S(1)} %pad_maximum_fusion.5), channel_id=1, source_target_pairs={{0,8},{1,9},{2,10},{3,11},{4,12},{5,13},{6,14},{7,15},{8,0},{9,1},... | collective-permute-start | bytes 196616 | tf_op jit(solution)/shard_map/ppermute | solution.py:663
  66.9 1.4 %collective-permute-start.9 = (bf16[8,64,128]{2,1,0:T(8,128)(2,1)S(1)}, bf16[8,64,128]{2,1,0:T(8,128)(2,1)S(1)}, u32[]{:S(2)}, u32[]{:S(2)}) collective-permute-start(bf16[8,64,128]{2,1,0:T(8,128)(2,1)S(1)} %pad_maximum_fusion.4.eight_a), channel_id=1, source_target_pairs={{0,1},{1,0},{2,3},{3,2},{4,5},{5,4},{6,7},{7,6},{8,9},{9,8},{10,11... | collective-permute-start | bytes 393224 | tf_op jit(solution)/shard_map/ppermute | solution.py:663
  68.3 4.3 %copy-start.4 = (s32[8192]{0:T(1024)S(1)}, s32[8192]{0:T(1024)}, u32[]{:S(2)}) copy-start(s32[8192]{0:T(1024)} %order_ref.11) | copy-start | bytes 98308
  72.4 2.4 %collective-permute-start.10 = (f32[64,128]{1,0:T(8,128)S(1)}, f32[64,128]{1,0:T(8,128)S(1)}, u32[]{:S(2)}, u32[]{:S(2)}) collective-permute-start(f32[64,128]{1,0:T(8,128)S(1)} %get-tuple-element.114), channel_id=1, source_target_pairs={{0,1},{1,0},{2,3},{3,2},{4,5},{5,4},{6,7},{7,6},{8,9},{9,8},{10,11... | collective-permute-start | bytes 98312 | tf_op jit(solution)/shard_map/ppermute | solution.py:663
  74.8 4.0 %collective-permute-start.11 = (f32[64,128]{1,0:T(8,128)S(1)}, f32[64,128]{1,0:T(8,128)S(1)}, u32[]{:S(2)}, u32[]{:S(2)}) collective-permute-start(f32[64,128]{1,0:T(8,128)S(1)} %add.21), channel_id=1, source_target_pairs={{0,2},{1,3},{2,0},{3,1},{4,6},{5,7},{6,4},{7,5},{8,10},{9,11},{10,... | collective-permute-start | bytes 98312 | tf_op jit(solution)/shard_map/ppermute | solution.py:663
  78.8 5.4 %collective-permute-start.12 = (f32[64,128]{1,0:T(8,128)S(1)}, f32[64,128]{1,0:T(8,128)S(1)}, u32[]{:S(2)}, u32[]{:S(2)}) collective-permute-start(f32[64,128]{1,0:T(8,128)S(1)} %add.22), channel_id=1, source_target_pairs={{0,6},{1,7},{2,4},{3,5},{4,2},{5,3},{6,0},{7,1},{8,14},{9,15},{10,... | collective-permute-start | bytes 98312 | tf_op jit(solution)/shard_map/ppermute | solution.py:663
  84.2 4.0 %collective-permute-start.13 = (f32[64,128]{1,0:T(8,128)S(1)}, f32[64,128]{1,0:T(8,128)S(1)}, u32[]{:S(2)}, u32[]{:S(2)}) collective-permute-start(f32[64,128]{1,0:T(8,128)S(1)} %add.23), channel_id=1, source_target_pairs={{0,8},{1,9},{2,10},{3,11},{4,12},{5,13},{6,14},{7,15},{8,0},{9,1},... | collective-permute-start | bytes 98312 | tf_op jit(solution)/shard_map/ppermute | solution.py:663
  88.2 5.1 %collective-permute-start.14 = (f32[64,128]{1,0:T(8,128)S(1)}, f32[64,128]{1,0:T(8,128)S(1)}, u32[]{:S(2)}, u32[]{:S(2)}) collective-permute-start(f32[64,128]{1,0:T(8,128)S(1)} %add.24), channel_id=1, source_target_pairs={{0,24},{1,25},{2,26},{3,27},{4,28},{5,29},{6,30},{7,31},{8,16},{9,... | collective-permute-start | bytes 98312 | tf_op jit(solution)/shard_map/ppermute | solution.py:663
  93.3 4.1 %collective-permute-start.15 = (f32[64,128]{1,0:T(8,128)S(1)}, f32[64,128]{1,0:T(8,128)S(1)}, u32[]{:S(2)}, u32[]{:S(2)}) collective-permute-start(f32[64,128]{1,0:T(8,128)S(1)} %add.25), channel_id=1, source_target_pairs={{0,32},{1,33},{2,34},{3,35},{4,36},{5,37},{6,38},{7,39},{8,40},{9,... | collective-permute-start | bytes 98312 | tf_op jit(solution)/shard_map/ppermute | solution.py:663
  97.5 5.8 %collective-permute-start.16 = (f32[64,128]{1,0:T(8,128)S(1)}, f32[64,128]{1,0:T(8,128)S(1)}, u32[]{:S(2)}, u32[]{:S(2)}) collective-permute-start(f32[64,128]{1,0:T(8,128)S(1)} %add.26), channel_id=1, source_target_pairs={{0,96},{1,97},{2,98},{3,99},{4,100},{5,101},{6,102},{7,103},{8,104... | collective-permute-start | bytes 98312 | tf_op jit(solution)/shard_map/ppermute | solution.py:663
  101.9 1.3 %copy-start = (f32[32,8192]{1,0:T(8,128)S(1)}, f32[32,8192]{1,0:T(8,128)}, u32[]{:S(2)}) copy-start(f32[32,8192]{1,0:T(8,128)} %rhs.1) | copy-start | bytes 3145732
